TPU v7x, 32 devices: a whole 2x2x4 slice. The times are simulated.
32 devices in a mesh: scen: 2 (over x), row: 16 (over z, y, core).
Axes of the slice: x: 2, y: 2, z: 4, core: 2. Of those that a mesh axis runs over, the one named last changes fastest.
Arguments:
- basin_state: float32 [6, 256, 2048], P('scen', 'row'), parts along dimension 0, may hold values from -1.5 to 1.5
- basin_depth: float32 [256, 4096], P('row', 'scen'), parts along dimension 1, may hold values from 0.7 to 1.5
- coast_depth: float32 [16, 512, 256], P('row', 'scen'), parts along dimension 1, may hold values from 0.1 to 2
- coast_flow: float32 [16, 4, 256, 256], P('row', 'scen'), parts along dimension 1, may hold values from -0.4 to 0.4
- coast_link: int32 [16, 6], P('row', 'scen'), parts along dimension 1, may hold values from 0 to 2031, as said below
Outputs:
- basin_out: float32 [6, 256, 2048], P('scen', 'row'), parts along dimension 0
- coast_out: float32 [16, 6, 256, 256], P('row', 'scen'), parts along dimension 1
There are 2 independent parts, one for each index of `scen`. A program takes and returns all parts, laid end to end along the dimension named above; each array names one. Nothing has to cross between parts.
Inputs may be any that keep to these rules, and one draw needn't show every extreme that they name: `coast_link`: column 0 is a basin row below 256, column 1 a column at most 2031, column 2 is 0 or 1; block 0 links to the last row and last start column, block 1 to row 0 and column 0.
All inputs are finite; a program needn't handle non-finite values.
Results may differ from a plain program's by a relative error of at most 0.0003.
Values sent between devices are 32-bit elements; how exact they have to be, the bound alone decides.
No kernel may reach another device: no remote copies, remote signals or barrier semaphores. Data moves between devices by JAX's collectives and lax.ppermute only.
A program may use at most 64 MiB of HBM per device.

v0:
```python
import jax
import jax.numpy as jnp
from jax import lax
from jax.sharding import PartitionSpec as P

BSTEPS = 8
CSTEPS = 10


basin_courant = 0.5
coast_courant = 0.1
depth_floor = 0.2
ghost_level = 2.0


def padded_2(cells, sides, width):
    for axis, dim in sides:
        count = lax.axis_size(axis)
        ends = count - 1
        head = lax.slice_in_dim(cells, 0, width, axis=dim)
        tail = lax.slice_in_dim(cells, cells.shape[dim] - width, cells.shape[dim], axis=dim)
        cells = jnp.concatenate(
            [
                lax.ppermute(tail, axis, [(i, (i + 1) % count) for i in range(ends)]),
                cells,
                lax.ppermute(head, axis, [((i + 1) % count, i) for i in range(ends)]),
            ],
            axis=dim,
        )
    return cells


def basin_step(state, depth, inside):
    eta, east, north = (state[0], state[1], state[2])
    zcol = jnp.zeros((eta.shape[0], 1), jnp.float32)
    zrow = jnp.zeros((1, eta.shape[1]), jnp.float32)
    east_west = jnp.concatenate([zcol, east[:, :-1]], axis=1)
    north_south = jnp.concatenate([zrow, north[:-1]], axis=0)
    eta_new = (eta - basin_courant * (east - east_west + (north - north_south))) * inside
    eta_east = jnp.concatenate([eta_new[:, 1:], zcol], axis=1)
    eta_north = jnp.concatenate([eta_new[1:], zrow], axis=0)
    east_new = (east - basin_courant * depth * (eta_east - eta_new)) * inside
    north_new = (north - basin_courant * depth * (eta_north - eta_new)) * inside
    return jnp.stack([eta_new, east_new, north_new])


def interp_table(strip_len, cells):
    rows = jnp.arange(strip_len, dtype=jnp.int32)[:, None]
    cols = jnp.arange(cells, dtype=jnp.int32)[None, :]
    base = cols // 16
    weight = ((cols % 16).astype(jnp.float32) + 0.5) / 16.0
    return jnp.where(rows == base, 1.0 - weight, 0.0) + jnp.where(rows == base + 1, weight, 0.0)


def make_ghost(strip, cells):
    table = interp_table(strip.shape[1], cells)
    values = jnp.dot(
        strip, table, precision=lax.Precision.HIGHEST, preferred_element_type=jnp.float32
    )
    return jnp.stack([ghost_level + values[0], jnp.zeros((cells,), jnp.float32), values[1]])


def phys_flux(state, normal):
    depth = state[0]
    along = state[normal]
    across = state[3 - normal]
    speed_u = along / jnp.maximum(depth, depth_floor)
    press = along * speed_u + 0.5 * depth * depth
    cross = across * speed_u
    if normal == 1:
        flux = jnp.stack([along, press, cross])
    else:
        flux = jnp.stack([along, cross, press])
    return (flux, jnp.abs(speed_u) + jnp.sqrt(jnp.maximum(depth, 0.0)))


def rusanov(left, right, normal):
    flux_l, speed_l = phys_flux(left, normal)
    flux_r, speed_r = phys_flux(right, normal)
    speed = jnp.maximum(speed_l, speed_r)
    return 0.5 * (flux_l + flux_r) - 0.5 * speed * (right - left)


def coast_step(block, ghost):
    rows = jnp.concatenate([ghost[:, None, :], block, block[:, -1:, :]], axis=1)
    padded = jnp.concatenate([rows[:, :, :1], rows, rows[:, :, -1:]], axis=2)
    flux_x = rusanov(padded[:, 1:-1, :-1], padded[:, 1:-1, 1:], 1)
    flux_y = rusanov(padded[:, :-1, 1:-1], padded[:, 1:, 1:-1], 2)
    return block - coast_courant * (
        flux_x[:, :, 1:] - flux_x[:, :, :-1] + (flux_y[:, 1:, :] - flux_y[:, :-1, :])
    )


def coast_run(block, ghost, steps):
    return lax.fori_loop(0, steps, lambda step, value: coast_step(value, ghost), block)


def row_mask(first_row, extent, total_rows):
    global_rows = first_row + jnp.arange(extent, dtype=jnp.int32)
    return ((global_rows >= 0) & (global_rows < total_rows)).astype(jnp.float32)[:, None]


def extract_strip(surface_pair, link, first_row, strip_len):
    local_row = link[0] - first_row
    owned = (local_row >= 0) & (local_row < surface_pair.shape[1])
    safe_row = jnp.clip(local_row, 0, surface_pair.shape[1] - 1)
    safe_col = jnp.clip(link[1], 0, surface_pair.shape[2] - strip_len)
    strip = lax.dynamic_slice(surface_pair, (jnp.int32(0), safe_row, safe_col), (2, 1, strip_len))[
        :, 0, :
    ]
    return jnp.where(owned, strip, 0.0)


def local(basin_state, basin_depth, coast_depth, coast_flow, coast_link):
    strip_rows = basin_state.shape[1]
    width_cells = basin_state.shape[2]
    devices = lax.axis_size("row")
    position = lax.axis_index("row")
    first_row = position * strip_rows
    total_rows = strip_rows * devices
    block_cells = coast_depth.shape[1]
    strip_len = block_cells // 16 + 1
    surface_pair = jnp.stack([basin_state[0], basin_state[2]])
    all_links = lax.all_gather(coast_link, "row", axis=0, tiled=True)
    pieces = jax.vmap(lambda link: extract_strip(surface_pair, link, first_row, strip_len))(
        all_links
    )
    strips = lax.psum_scatter(pieces, "row", scatter_dimension=0, tiled=True)
    blocks = jnp.concatenate([coast_depth[:, None], coast_flow], axis=1)
    ghosts = jax.vmap(lambda strip: make_ghost(strip, block_cells))(strips)
    wet_flags = coast_link[:, 2]
    stepped = jax.vmap(lambda block, ghost: coast_run(block, ghost, CSTEPS))(blocks, ghosts)
    coast_out = jnp.where((wet_flags > 0)[:, None, None, None], stepped, blocks)
    state = basin_state
    zero_rows = jnp.zeros((1, width_cells), jnp.float32)
    depth_wide = jnp.concatenate([zero_rows, basin_depth, zero_rows], axis=0)
    inside_wide = row_mask(first_row - 1, strip_rows + 2, total_rows)
    for step in range(BSTEPS):
        widened = padded_2(state, (("row", 1),), 1)
        state = basin_step(widened, depth_wide, inside_wide)[:, 1:-1]
    return (state, coast_out)


def solution(mesh):
    in_specs = (
        P("scen", "row", None),
        P("row", "scen"),
        P("row", "scen", None),
        P("row", "scen", None, None),
        P("row", "scen"),
    )
    out_specs = (P("scen", "row", None), P("row", "scen", None, None))
    return jax.shard_map(local, mesh=mesh, in_specs=in_specs, out_specs=out_specs, check_vma=False)
```

profile of v0, /device:TPU:0, one launch (start us, length us, event | category | flops | bytes accessed | tf_op | source)
XLA Modules:
  0.0 189.2 jit_solution(678344031429108496)
XLA Ops:
  0.6 1.1 fusion.71
  1.7 2.4 %collective-permute-start = (f32[3,1,2048]{2,1,0:T(1,128)S(1)}, f32[3,1,2048]{2,1,0:T(1,128)S(1)}, u32[]{:S(2)}, u32[]{:S(2)}) collective-permute-start(f32[3,1,2048]{2,1,0:T(1,128)S(1)} %get-tuple-element.84), channel_id=1, source_target_pairs={{0,1},{1,2},{2,3},{3,4},{4,5},{5,6},{6,7},{7,8},{8,9},{9,10},{10,1... | collective-permute-start | bytes 73736 | tf_op jit(solution)/shard_map/ppermute | solution.py:24
  4.1 1.3 collective-permute-start.1
  5.4 1.0 fusion.70
  6.4 25.1 %all-gather = s32[16,1,3]{2,1,0:T(1,128)S(1)} all-gather(s32[1,1,3]{2,1,0:T(1,128)} %bitcast.266), channel_id=1, replica_groups=mesh['scen'=2,'row'=16] {'row'}, dimensions={0}, use_global_device_ids=true | all-gather | bytes 204 | tf_op jit(solution)/shard_map/all_gather | solution.py:124
  31.6 1.2 slice.480
  32.9 10.7 %copy.13 = f32[2,16,2048]{0,1,2:T(8,128)} copy(f32[2,16,2048]{2,1,0:T(8,128)S(1)} %pad_maximum_fusion.22) | data formatting | bytes 524288 | tf_op jit(solution)/shard_map/stack | solution.py:123
  43.6 1.5 gather_fusion
  45.5 57.8 %all-reduce.32 = f32[16,2,17]{2,1,0:T(2,128)S(1)} all-reduce(f32[16,2,17]{2,1,0:T(2,128)S(1)} %copy.14), channel_id=2, replica_groups=mesh['scen'=2,'row'=16] {'row'}, use_global_device_ids=true, to_apply=%region_0.1.clone | all-reduce | flops 544 | bytes 4352
  103.2 0.6 dynamic-slice
  103.8 0.8 convolution_bitcast_fusion
  104.8 31.1 %while.10 = (s32[]{:T(128)}, f32[1,3,256,256]{3,2,1,0:T(8,128)S(1)}, f32[1,3,256]{2,0,1:T(1,128)S(1)}, s32[]{:T(128)}) while((s32[]{:T(128)}, f32[1,3,256,256]{3,2,1,0:T(8,128)S(1)}, f32[1,3,256]{2,0,1:T(1,128)S(1)}, s32[]{:T(128)}) %tuple.68), condition=%wide.region_2.3_spmd, body=%wide.region_1.2_spmd.sunk | while | flops 10599462 | bytes 23722228 | solution.py:95
  105.6 0.7 multiply_bitcast_fusion.21
  108.7 0.7 multiply_bitcast_fusion.21
  109.3 0.5 fusion.80
  111.8 0.7 multiply_bitcast_fusion.21
  114.9 0.7 multiply_bitcast_fusion.21
  118.0 0.7 multiply_bitcast_fusion.21
  118.7 0.5 fusion.80
  121.1 0.7 multiply_bitcast_fusion.21
  124.2 0.7 multiply_bitcast_fusion.21
  127.3 0.7 multiply_bitcast_fusion.21
  130.4 0.7 multiply_bitcast_fusion.21
  133.6 0.7 multiply_bitcast_fusion.21
  136.6 1.0 broadcast_select_fusion
  138.1 0.6 copy-done
  138.8 1.3 collective-permute-start.2
  140.1 1.3 collective-permute-start.3
  141.5 1.7 collective-permute-done.3
  143.8 2.1 %collective-permute-start.4 = (f32[3,1,2048]{2,1,0:T(1,128)S(1)}, f32[3,1,2048]{2,1,0:T(1,128)S(1)}, u32[]{:S(2)}, u32[]{:S(2)}) collective-permute-start(f32[3,1,2048]{2,1,0:T(1,128)S(1)} %get-tuple-element.78), channel_id=1, source_target_pairs={{0,1},{1,2},{2,3},{3,4},{4,5},{5,6},{6,7},{7,8},{8,9},{9,10},{10,1... | collective-permute-start | bytes 73736 | tf_op jit(solution)/shard_map/ppermute | solution.py:24
  145.9 1.3 collective-permute-start.5
  147.3 1.7 collective-permute-done.5
  149.6 4.0 %collective-permute-start.6 = (f32[3,1,2048]{2,1,0:T(1,128)S(1)}, f32[3,1,2048]{2,1,0:T(1,128)S(1)}, u32[]{:S(2)}, u32[]{:S(2)}) collective-permute-start(f32[3,1,2048]{2,1,0:T(1,128)S(1)} %get-tuple-element.76), channel_id=1, source_target_pairs={{0,1},{1,2},{2,3},{3,4},{4,5},{5,6},{6,7},{7,8},{8,9},{9,10},{10,1... | collective-permute-start | bytes 73736 | tf_op jit(solution)/shard_map/ppermute | solution.py:24
  153.6 1.3 collective-permute-start.7
  155.0 1.7 collective-permute-done.7
  157.2 4.0 %collective-permute-start.8 = (f32[3,1,2048]{2,1,0:T(1,128)S(1)}, f32[3,1,2048]{2,1,0:T(1,128)S(1)}, u32[]{:S(2)}, u32[]{:S(2)}) collective-permute-start(f32[3,1,2048]{2,1,0:T(1,128)S(1)} %get-tuple-element.74), channel_id=1, source_target_pairs={{0,1},{1,2},{2,3},{3,4},{4,5},{5,6},{6,7},{7,8},{8,9},{9,10},{10,1... | collective-permute-start | bytes 73736 | tf_op jit(solution)/shard_map/ppermute | solution.py:24
  161.2 1.3 collective-permute-start.9
  162.6 1.7 collective-permute-done.9
  164.9 4.0 %collective-permute-start.10 = (f32[3,1,2048]{2,1,0:T(1,128)S(1)}, f32[3,1,2048]{2,1,0:T(1,128)S(1)}, u32[]{:S(2)}, u32[]{:S(2)}) collective-permute-start(f32[3,1,2048]{2,1,0:T(1,128)S(1)} %get-tuple-element.72), channel_id=1, source_target_pairs={{0,1},{1,2},{2,3},{3,4},{4,5},{5,6},{6,7},{7,8},{8,9},{9,10},{10,1... | collective-permute-start | bytes 73736 | tf_op jit(solution)/shard_map/ppermute | solution.py:24
  168.9 1.3 collective-permute-start.11
  170.3 1.7 collective-permute-done.11
  172.6 4.0 %collective-permute-start.12 = (f32[3,1,2048]{2,1,0:T(1,128)S(1)}, f32[3,1,2048]{2,1,0:T(1,128)S(1)}, u32[]{:S(2)}, u32[]{:S(2)}) collective-permute-start(f32[3,1,2048]{2,1,0:T(1,128)S(1)} %get-tuple-element.70), channel_id=1, source_target_pairs={{0,1},{1,2},{2,3},{3,4},{4,5},{5,6},{6,7},{7,8},{8,9},{9,10},{10,1... | collective-permute-start | bytes 73736 | tf_op jit(solution)/shard_map/ppermute | solution.py:24
  176.5 1.3 collective-permute-start.13
  178.0 1.7 collective-permute-done.13
  180.2 4.5 %collective-permute-start.14 = (f32[3,1,2048]{2,1,0:T(1,128)S(1)}, f32[3,1,2048]{2,1,0:T(1,128)S(1)}, u32[]{:S(2)}, u32[]{:S(2)}) collective-permute-start(f32[3,1,2048]{2,1,0:T(1,128)S(1)} %get-tuple-element.68), channel_id=1, source_target_pairs={{0,1},{1,2},{2,3},{3,4},{4,5},{5,6},{6,7},{7,8},{8,9},{9,10},{10,1... | collective-permute-start | bytes 73736 | tf_op jit(solution)/shard_map/ppermute | solution.py:24
  184.7 1.3 collective-permute-start.15
  186.1 1.7 collective-permute-done.15
  188.4 0.8 pad_maximum_fusion.20
  (198 shorter events, 28.4 us)
Async XLA Ops:
  1.7 135.9 %collective-permute-start = (f32[3,1,2048]{2,1,0:T(1,128)S(1)}, f32[3,1,2048]{2,1,0:T(1,128)S(1)}, u32[]{:S(2)}, u32[]{:S(2)}) collective-permute-start(f32[3,1,2048]{2,1,0:T(1,128)S(1)} %get-tuple-element.84), channel_id=1, source_target_pairs={{0,1},{1,2},{2,3},{3,4},{4,5},{5,6},{6,7},{7,8},{8,9},{9,10},{10,1... | collective-permute-start | bytes 73736 | tf_op jit(solution)/shard_map/ppermute | solution.py:24
  4.1 133.6 %collective-permute-start.1 = (f32[3,1,2048]{2,1,0:T(1,128)S(1)}, f32[3,1,2048]{2,1,0:T(1,128)S(1)}, u32[]{:S(2)}, u32[]{:S(2)}) collective-permute-start(f32[3,1,2048]{2,1,0:T(1,128)S(1)} %get-tuple-element.85), channel_id=1, source_target_pairs={{1,0},{2,1},{3,2},{4,3},{5,4},{6,5},{7,6},{8,7},{9,8},{10,9},{11,1... | collective-permute-start | bytes 73736 | tf_op jit(solution)/shard_map/ppermute | solution.py:26
  32.8 70.4 %copy-start.4 = (u32[32]{0:T(128)S(1)}, u32[32]{0:T(128)}, u32[]{:S(2)}) copy-start(u32[32]{0:T(128)} %constant.178) | copy-start | bytes 388
  32.8 71.9 %copy-start.2 = (f32[1,2,256,256]{3,2,1,0:T(8,128)S(1)}, f32[1,2,256,256]{3,2,1,0:T(8,128)}, u32[]{:S(2)}) copy-start(f32[1,2,256,256]{3,2,1,0:T(8,128)} %param.10) | copy-start | bytes 1572868
  32.9 71.9 %copy-start.3 = (f32[1,256,256]{2,1,0:T(8,128)S(1)}, f32[1,256,256]{2,1,0:T(8,128)}, u32[]{:S(2)}) copy-start(f32[1,256,256]{2,1,0:T(8,128)} %param.9) | copy-start | bytes 786436
  135.9 1.7 copy-start.1
  137.8 0.9 copy-start
  138.8 2.7 %collective-permute-start.2 = (f32[3,1,2048]{2,1,0:T(1,128)S(1)}, f32[3,1,2048]{2,1,0:T(1,128)S(1)}, u32[]{:S(2)}, u32[]{:S(2)}) collective-permute-start(f32[3,1,2048]{2,1,0:T(1,128)S(1)} %get-tuple-element.80), channel_id=1, source_target_pairs={{0,1},{1,2},{2,3},{3,4},{4,5},{5,6},{6,7},{7,8},{8,9},{9,10},{10,1... | collective-permute-start | bytes 73736 | tf_op jit(solution)/shard_map/ppermute | solution.py:24
  140.1 3.1 %collective-permute-start.3 = (f32[3,1,2048]{2,1,0:T(1,128)S(1)}, f32[3,1,2048]{2,1,0:T(1,128)S(1)}, u32[]{:S(2)}, u32[]{:S(2)}) collective-permute-start(f32[3,1,2048]{2,1,0:T(1,128)S(1)} %get-tuple-element.81), channel_id=1, source_target_pairs={{1,0},{2,1},{3,2},{4,3},{5,4},{6,5},{7,6},{8,7},{9,8},{10,9},{11,1... | collective-permute-start | bytes 73736 | tf_op jit(solution)/shard_map/ppermute | solution.py:26
  143.8 3.5 %collective-permute-start.4 = (f32[3,1,2048]{2,1,0:T(1,128)S(1)}, f32[3,1,2048]{2,1,0:T(1,128)S(1)}, u32[]{:S(2)}, u32[]{:S(2)}) collective-permute-start(f32[3,1,2048]{2,1,0:T(1,128)S(1)} %get-tuple-element.78), channel_id=1, source_target_pairs={{0,1},{1,2},{2,3},{3,4},{4,5},{5,6},{6,7},{7,8},{8,9},{9,10},{10,1... | collective-permute-start | bytes 73736 | tf_op jit(solution)/shard_map/ppermute | solution.py:24
  145.9 3.1 %collective-permute-start.5 = (f32[3,1,2048]{2,1,0:T(1,128)S(1)}, f32[3,1,2048]{2,1,0:T(1,128)S(1)}, u32[]{:S(2)}, u32[]{:S(2)}) collective-permute-start(f32[3,1,2048]{2,1,0:T(1,128)S(1)} %get-tuple-element.79), channel_id=1, source_target_pairs={{1,0},{2,1},{3,2},{4,3},{5,4},{6,5},{7,6},{8,7},{9,8},{10,9},{11,1... | collective-permute-start | bytes 73736 | tf_op jit(solution)/shard_map/ppermute | solution.py:26
  149.6 5.4 %collective-permute-start.6 = (f32[3,1,2048]{2,1,0:T(1,128)S(1)}, f32[3,1,2048]{2,1,0:T(1,128)S(1)}, u32[]{:S(2)}, u32[]{:S(2)}) collective-permute-start(f32[3,1,2048]{2,1,0:T(1,128)S(1)} %get-tuple-element.76), channel_id=1, source_target_pairs={{0,1},{1,2},{2,3},{3,4},{4,5},{5,6},{6,7},{7,8},{8,9},{9,10},{10,1... | collective-permute-start | bytes 73736 | tf_op jit(solution)/shard_map/ppermute | solution.py:24
  153.6 3.1 %collective-permute-start.7 = (f32[3,1,2048]{2,1,0:T(1,128)S(1)}, f32[3,1,2048]{2,1,0:T(1,128)S(1)}, u32[]{:S(2)}, u32[]{:S(2)}) collective-permute-start(f32[3,1,2048]{2,1,0:T(1,128)S(1)} %get-tuple-element.77), channel_id=1, source_target_pairs={{1,0},{2,1},{3,2},{4,3},{5,4},{6,5},{7,6},{8,7},{9,8},{10,9},{11,1... | collective-permute-start | bytes 73736 | tf_op jit(solution)/shard_map/ppermute | solution.py:26
  157.2 5.4 %collective-permute-start.8 = (f32[3,1,2048]{2,1,0:T(1,128)S(1)}, f32[3,1,2048]{2,1,0:T(1,128)S(1)}, u32[]{:S(2)}, u32[]{:S(2)}) collective-permute-start(f32[3,1,2048]{2,1,0:T(1,128)S(1)} %get-tuple-element.74), channel_id=1, source_target_pairs={{0,1},{1,2},{2,3},{3,4},{4,5},{5,6},{6,7},{7,8},{8,9},{9,10},{10,1... | collective-permute-start | bytes 73736 | tf_op jit(solution)/shard_map/ppermute | solution.py:24
  161.2 3.1 %collective-permute-start.9 = (f32[3,1,2048]{2,1,0:T(1,128)S(1)}, f32[3,1,2048]{2,1,0:T(1,128)S(1)}, u32[]{:S(2)}, u32[]{:S(2)}) collective-permute-start(f32[3,1,2048]{2,1,0:T(1,128)S(1)} %get-tuple-element.75), channel_id=1, source_target_pairs={{1,0},{2,1},{3,2},{4,3},{5,4},{6,5},{7,6},{8,7},{9,8},{10,9},{11,1... | collective-permute-start | bytes 73736 | tf_op jit(solution)/shard_map/ppermute | solution.py:26
  164.9 5.4 %collective-permute-start.10 = (f32[3,1,2048]{2,1,0:T(1,128)S(1)}, f32[3,1,2048]{2,1,0:T(1,128)S(1)}, u32[]{:S(2)}, u32[]{:S(2)}) collective-permute-start(f32[3,1,2048]{2,1,0:T(1,128)S(1)} %get-tuple-element.72), channel_id=1, source_target_pairs={{0,1},{1,2},{2,3},{3,4},{4,5},{5,6},{6,7},{7,8},{8,9},{9,10},{10,1... | collective-permute-start | bytes 73736 | tf_op jit(solution)/shard_map/ppermute | solution.py:24
  168.9 3.1 %collective-permute-start.11 = (f32[3,1,2048]{2,1,0:T(1,128)S(1)}, f32[3,1,2048]{2,1,0:T(1,128)S(1)}, u32[]{:S(2)}, u32[]{:S(2)}) collective-permute-start(f32[3,1,2048]{2,1,0:T(1,128)S(1)} %get-tuple-element.73), channel_id=1, source_target_pairs={{1,0},{2,1},{3,2},{4,3},{5,4},{6,5},{7,6},{8,7},{9,8},{10,9},{11,1... | collective-permute-start | bytes 73736 | tf_op jit(solution)/shard_map/ppermute | solution.py:26
  172.6 5.4 %collective-permute-start.12 = (f32[3,1,2048]{2,1,0:T(1,128)S(1)}, f32[3,1,2048]{2,1,0:T(1,128)S(1)}, u32[]{:S(2)}, u32[]{:S(2)}) collective-permute-start(f32[3,1,2048]{2,1,0:T(1,128)S(1)} %get-tuple-element.70), channel_id=1, source_target_pairs={{0,1},{1,2},{2,3},{3,4},{4,5},{5,6},{6,7},{7,8},{8,9},{9,10},{10,1... | collective-permute-start | bytes 73736 | tf_op jit(solution)/shard_map/ppermute | solution.py:24
  176.5 3.1 %collective-permute-start.13 = (f32[3,1,2048]{2,1,0:T(1,128)S(1)}, f32[3,1,2048]{2,1,0:T(1,128)S(1)}, u32[]{:S(2)}, u32[]{:S(2)}) collective-permute-start(f32[3,1,2048]{2,1,0:T(1,128)S(1)} %get-tuple-element.71), channel_id=1, source_target_pairs={{1,0},{2,1},{3,2},{4,3},{5,4},{6,5},{7,6},{8,7},{9,8},{10,9},{11,1... | collective-permute-start | bytes 73736 | tf_op jit(solution)/shard_map/ppermute | solution.py:26
  180.2 5.9 %collective-permute-start.14 = (f32[3,1,2048]{2,1,0:T(1,128)S(1)}, f32[3,1,2048]{2,1,0:T(1,128)S(1)}, u32[]{:S(2)}, u32[]{:S(2)}) collective-permute-start(f32[3,1,2048]{2,1,0:T(1,128)S(1)} %get-tuple-element.68), channel_id=1, source_target_pairs={{0,1},{1,2},{2,3},{3,4},{4,5},{5,6},{6,7},{7,8},{8,9},{9,10},{10,1... | collective-permute-start | bytes 73736 | tf_op jit(solution)/shard_map/ppermute | solution.py:24
  184.7 3.1 %collective-permute-start.15 = (f32[3,1,2048]{2,1,0:T(1,128)S(1)}, f32[3,1,2048]{2,1,0:T(1,128)S(1)}, u32[]{:S(2)}, u32[]{:S(2)}) collective-permute-start(f32[3,1,2048]{2,1,0:T(1,128)S(1)} %get-tuple-element.69), channel_id=1, source_target_pairs={{1,0},{2,1},{3,2},{4,3},{5,4},{6,5},{7,6},{8,7},{9,8},{10,9},{11,1... | collective-permute-start | bytes 73736 | tf_op jit(solution)/shard_map/ppermute | solution.py:26
where the time goes:
time: 193 us; the launch traced here: 189 us
  blocking collectives  82.9 us (43%)
  starting transfers between devices  36.5 us (19%)
  other arithmetic  34.1 us (18%)
  local copies, waits for them, and re-layouts  20.3 us (11%)
  waiting for transfers between devices  11.8 us (6%)
  between operations  2.19 us (1%)
    unnamed x1, blocking collectives  57.8 us
    ppermute x8, starting transfers between devices, padded_2(): lax.ppermute(tail, axis, [(i, (i + 1) % count) for i in range(ends)])  26.1 us
    all_gather x1, blocking collectives, local(): all_links = lax.all_gather(coast_link, 'row', axis=0, tiled=True)  25.1 us
    ppermute x8, waiting for transfers between devices, padded_2(): lax.ppermute(head, axis, [((i + 1) % count, i) for i in range(ends)])  11.8 us
    another operation x1, local copies, waits for them, and re-layouts, local(): surface_pair = jnp.stack([basin_state[0], basin_state[2]])  10.7 us
    ppermute x8, starting transfers between devices, padded_2(): lax.ppermute(head, axis, [((i + 1) % count, i) for i in range(ends)])  10.3 us
    mul x20, other arithmetic, rusanov(): return 0.5 * (flux_l + flux_r) - 0.5 * speed * (right - left)  9.42 us
    sub x20, other arithmetic, rusanov(): return 0.5 * (flux_l + flux_r) - 0.5 * speed * (right - left)  7.35 us
  transfers between devices with their start and end apart: 16, of which 7 were waited for; matrix products, arithmetic and copies ran while one was open for 26% of the time, Pallas kernels for 0%

commit v1 on v0

v1 whole, which is shorter than its diff:
```python
import functools

import jax
import jax.numpy as jnp
from jax import lax
from jax.experimental import pallas as pl
from jax.experimental.pallas import tpu as pltpu
from jax.sharding import PartitionSpec as P

BSTEPS = 8
CSTEPS = 10

depth_floor = 0.2
ghost_level = 2.0

RATE = 0.05
DEPTH_UNIT = RATE * RATE
FLOW_UNIT = RATE * RATE * RATE
TINY = 1e-30

HALO = BSTEPS
SUB = 8
LANES = 128


def lane_ids():
    return lax.broadcasted_iota(jnp.int32, (SUB, LANES), 1)


def row_ids():
    return lax.broadcasted_iota(jnp.int32, (SUB, LANES), 0)


def split_columns(cells):
    rows = lax.broadcasted_iota(jnp.int32, (cells, cells), 0)
    cols = lax.broadcasted_iota(jnp.int32, (cells, cells), 1)
    half = cells // 2
    source = jnp.where(cols < half, 2 * cols, 2 * (cols - half) + 1)
    return (rows == source).astype(jnp.bfloat16)


def permute(values, table, transposed=False):
    dims = (((1,), (1 if transposed else 0,)), ((), ()))
    total = None
    rest = values
    for _ in range(3):
        part = rest.astype(jnp.bfloat16)
        rest = rest - part.astype(jnp.float32)
        term = lax.dot_general(part, table, dims, preferred_element_type=jnp.float32)
        total = term if total is None else total + term
    return total


def inverse(x):
    guess = pl.reciprocal(x, approx=True)
    return guess * (2.0 - x * guess)


def cell_terms(u):
    h, mu, mv = u
    r = inverse(jnp.maximum(h, depth_floor * DEPTH_UNIT))
    vx, vy = mu * r, mv * r
    hp = jnp.maximum(h, TINY)
    c = hp * lax.rsqrt(hp)
    p = (0.5 * h) * h
    cross = mu * vy
    return {
        "u": u,
        "fx": (mu, mu * vx + p, cross),
        "fy": (mv, cross, mv * vy + p),
        "sx": jnp.abs(vx) + c,
        "sy": jnp.abs(vy) + c,
    }


def x_part(even, odd, first, last):
    left = functools.partial(pltpu.roll, shift=LANES - 1, axis=1)
    right = functools.partial(pltpu.roll, shift=1, axis=1)
    next_u = [left(a) for a in even["u"]]
    next_f = [next_u[1], left(even["fx"][1]), left(even["fx"][2])]
    a_in = jnp.maximum(even["sx"], odd["sx"])
    a_out = jnp.where(last, 0.0, jnp.maximum(odd["sx"], left(even["sx"])))
    d_in = [a_in * (o - e) for e, o in zip(even["u"], odd["u"])]
    d_out = [a_out * (n - o) for o, n in zip(odd["u"], next_u)]
    new_even, new_odd = [], []
    for i in range(3):
        f_e, f_o = even["fx"][i], odd["fx"][i]
        f_next = jnp.where(last, f_o, next_f[i])
        f_back = jnp.where(first, f_e, right(f_o))
        new_even.append(even["u"][i] + ((d_in[i] - right(d_out[i])) - (f_o - f_back)))
        new_odd.append(odd["u"][i] + ((d_out[i] - d_in[i]) - (f_next - f_e)))
    return new_even, new_odd


def y_face(above, below):
    a = jnp.maximum(above["sy"], below["sy"])
    return [
        a * (ub - ua) - (fa + fb)
        for ua, ub, fa, fb in zip(above["u"], below["u"], above["fy"], below["fy"])
    ]


def coast_steps(state, rows, steps, ghost):
    lane, sub = lane_ids(), row_ids()
    first, last = lane == 0, lane == LANES - 1
    top, bottom = sub == 0, sub == SUB - 1

    def load(k):
        return [cell_terms([state[f, half, k] for f in range(3)]) for half in range(2)]

    def store(k, both):
        for half in range(2):
            for f in range(3):
                state[f, half, k] = both[half][f]

    def wrapped(tail, head):
        down = functools.partial(pltpu.roll, shift=1, axis=0)
        out = {"sy": jnp.where(top, head["sy"], down(tail["sy"]))}
        for name in ("u", "fy"):
            out[name] = [jnp.where(top, h, down(t)) for h, t in zip(head[name], tail[name])]
        return out

    def step(_, carry):
        tails = load(rows - 1)
        prev, acc, start = None, None, None
        for k in range(rows):
            cur = load(k)
            if k == 0:
                heads = cur if ghost is None else ghost
                above = [wrapped(t, h) for t, h in zip(tails, heads)]
                start = face = [y_face(a, b) for a, b in zip(above, cur)]
            else:
                face = [y_face(a, b) for a, b in zip(prev, cur)]
                store(k - 1, [[x + g for x, g in zip(xs, gs)] for xs, gs in zip(acc, face)])
            acc = x_part(cur[0], cur[1], first, last)
            acc = [[x - g for x, g in zip(xs, gs)] for xs, gs in zip(acc, face)]
            prev = cur
        end = [
            [
                jnp.where(bottom, -(f + f), pltpu.roll(g, SUB - 1, 0))
                for f, g in zip(cell["fy"], gs)
            ]
            for cell, gs in zip(prev, start)
        ]
        store(rows - 1, [[x + g for x, g in zip(xs, gs)] for xs, gs in zip(acc, end)])
        return carry

    lax.fori_loop(0, steps, step, 0)


def fold_in(source, tmp, state, table, unit, rows):
    split = permute(source[...], table) * unit
    for half in range(2):
        tmp[half] = split[:, half * LANES : (half + 1) * LANES]
        for k in range(rows):
            state[half, k] = tmp[half, pl.ds(k, SUB, stride=rows), :]


def unfold(state, tmp, table, unit, rows):
    for half in range(2):
        for k in range(rows):
            tmp[half, pl.ds(k, SUB, stride=rows), :] = state[half, k]
    flat = jnp.concatenate([tmp[0], tmp[1]], axis=1)
    return permute(flat * (1.0 / unit), table, transposed=True)


def coast_kernel(link, depth, flow, out, state, tmp):
    rows = depth.shape[0] // SUB
    cells = depth.shape[1]
    units = (DEPTH_UNIT, FLOW_UNIT, FLOW_UNIT)

    @pl.when(link[0, 2] > 0)
    def _():
        table = split_columns(cells)
        for f in range(3):
            source = depth if f == 0 else flow.at[f - 1]
            fold_in(source, tmp, state.at[f], table, units[f], rows)
        coast_steps(state, rows, CSTEPS, None)
        for f in range(3):
            out[f] = unfold(state.at[f], tmp, table, units[f], rows)

    @pl.when(link[0, 2] <= 0)
    def _():
        out[0] = depth[...]
        out[1] = flow[0]
        out[2] = flow[1]


def coast_bulk(link, depth, flow):
    cells = depth.shape[0]
    return pl.pallas_call(
        coast_kernel,
        out_shape=jax.ShapeDtypeStruct((3, cells, cells), jnp.float32),
        in_specs=[
            pl.BlockSpec(memory_space=pltpu.SMEM),
            pl.BlockSpec(memory_space=pltpu.VMEM),
            pl.BlockSpec(memory_space=pltpu.VMEM),
        ],
        out_specs=pl.BlockSpec(memory_space=pltpu.VMEM),
        scratch_shapes=[
            pltpu.VMEM((3, 2, cells // SUB, SUB, LANES), jnp.float32),
            pltpu.VMEM((2, cells, LANES), jnp.float32),
        ],
        compiler_params=pltpu.CompilerParams(vmem_limit_bytes=32 * 1024 * 1024),
        cost_estimate=pl.CostEstimate(
            flops=CSTEPS * 70 * cells * cells, bytes_accessed=24 * cells * cells, transcendentals=0
        ),
        name="coast_bulk",
    )(link, depth, flow)


EDGE = 3
EDGE_ROWS = EDGE * SUB
EDGE_OUT = 16


def edge_kernel(strip_rows, link, strips, depth, flow, before, out, state, tmp):
    cells = depth.shape[1]
    units = (DEPTH_UNIT, FLOW_UNIT, FLOW_UNIT)
    out[...] = before[...]

    @pl.when(link[0, 2] > 0)
    def _():
        table = split_columns(cells)
        for f in range(3):
            source = depth if f == 0 else flow.at[f - 1]
            fold_in(source, tmp, state.at[f], table, units[f], EDGE)
        strip = strips[link[0, 0] // strip_rows]
        rows = lax.broadcasted_iota(jnp.int32, (LANES, cells), 0)
        cols = lax.broadcasted_iota(jnp.int32, (LANES, cells), 1)
        half = cells // 2
        cols = jnp.where(cols < half, 2 * cols, 2 * (cols - half) + 1)
        base = cols // 16
        weight = ((cols % 16).astype(jnp.float32) + 0.5) / 16.0
        mix = jnp.where(rows == base, 1.0 - weight, 0.0) + jnp.where(rows == base + 1, weight, 0.0)
        values = jnp.dot(
            strip, mix, precision=lax.Precision.HIGHEST, preferred_element_type=jnp.float32
        )
        level = (ghost_level + values[0:1]) * DEPTH_UNIT
        inflow = values[1:2] * FLOW_UNIT
        ghost = []
        for at in (0, half):
            h = jnp.broadcast_to(level[:, at : at + half], (SUB, half))
            mv = jnp.broadcast_to(inflow[:, at : at + half], (SUB, half))
            ghost.append(cell_terms([h, jnp.zeros_like(h), mv]))
        coast_steps(state, EDGE, CSTEPS, ghost)
        keep = lax.broadcasted_iota(jnp.int32, (EDGE_OUT, cells), 0) < CSTEPS
        for f in range(3):
            done = unfold(state.at[f], tmp, table, units[f], EDGE)
            out[f] = jnp.where(keep, done[:EDGE_OUT], before[f])


def coast_edge(strip_rows, link, strips, depth, flow, before):
    cells = depth.shape[0]
    return pl.pallas_call(
        functools.partial(edge_kernel, strip_rows),
        out_shape=jax.ShapeDtypeStruct(before.shape, jnp.float32),
        grid=(1,),
        in_specs=[
            pl.BlockSpec(memory_space=pltpu.SMEM),
            pl.BlockSpec(strips.shape, lambda i: (0, 0, 0)),
            pl.BlockSpec((EDGE_ROWS, cells), lambda i: (0, 0)),
            pl.BlockSpec((2, EDGE_ROWS, cells), lambda i: (0, 0, 0)),
            pl.BlockSpec((3, EDGE_OUT, cells), lambda i: (0, 0, 0)),
        ],
        out_specs=pl.BlockSpec((3, EDGE_OUT, cells), lambda i: (0, 0, 0)),
        scratch_shapes=[
            pltpu.VMEM((3, 2, EDGE, SUB, LANES), jnp.float32),
            pltpu.VMEM((2, EDGE_ROWS, LANES), jnp.float32),
        ],
        input_output_aliases={4: 0},
        cost_estimate=pl.CostEstimate(
            flops=CSTEPS * 70 * EDGE_ROWS * cells, bytes_accessed=4 * 100 * cells, transcendentals=0
        ),
        name="coast_edge",
    )(link, strips, depth, flow, before)


def basin_kernel(inside, state, depth, south, north, out, eta, hu, hv, dep):
    rows = state.shape[1]
    width = state.shape[2]
    total = rows + 2 * HALO
    chunks = width // LANES
    for ref, field, unit in ((eta, 0, 1.0), (hu, 1, 0.5), (hv, 2, 0.5), (dep, 3, 0.25)):
        ref[:HALO] = south[field] * unit
        ref[HALO : HALO + rows] = (depth[...] if field == 3 else state[field]) * unit
        ref[HALO + rows :] = north[field] * unit
    lane = lax.broadcasted_iota(jnp.int32, (total, LANES), 1)
    first, last = lane == 0, lane == LANES - 1
    row = lax.broadcasted_iota(jnp.int32, (total, LANES), 0)
    kept = jnp.where(row < HALO + rows, 1.0, inside[0].astype(jnp.float32))

    def step(_, carry):
        prev_west = jnp.zeros((total, LANES), jnp.float32)
        prev_eta, prev_east, prev_hu = None, None, None
        for c in range(chunks + 1):
            if c < chunks:
                at = slice(c * LANES, (c + 1) * LANES)
                u, v = hu[:, at], hv[:, at]
                west = pltpu.roll(u, 1, 1)
                du = u - jnp.where(first, prev_west, west)
                dv = v - pltpu.roll(v, 1, 0)
                new = (eta[:, at] - (du + dv)) * kept
                eta[:, at] = new
                east = pltpu.roll(new, LANES - 1, 1)
                hv[:, at] = v - dep[:, at] * (pltpu.roll(new, total - 1, 0) - new)
            else:
                east = jnp.zeros((total, LANES), jnp.float32)
            if c > 0:
                back = slice((c - 1) * LANES, c * LANES)
                hu[:, back] = prev_hu - dep[:, back] * (jnp.where(last, east, prev_east) - prev_eta)
            prev_west, prev_eta, prev_east, prev_hu = west, new, east, u
        return carry

    lax.fori_loop(0, BSTEPS, step, 0)
    own = slice(HALO, HALO + rows)
    out[0] = eta[own]
    out[1] = hu[own] * 2.0
    out[2] = hv[own] * 2.0


def basin_run(inside, state, depth, south, north):
    rows, width = depth.shape
    total = rows + 2 * HALO
    vmem = pl.BlockSpec(memory_space=pltpu.VMEM)
    return pl.pallas_call(
        basin_kernel,
        out_shape=jax.ShapeDtypeStruct(state.shape, jnp.float32),
        in_specs=[pl.BlockSpec(memory_space=pltpu.SMEM), vmem, vmem, vmem, vmem],
        out_specs=vmem,
        scratch_shapes=[pltpu.VMEM((total, width), jnp.float32)] * 4,
        compiler_params=pltpu.CompilerParams(vmem_limit_bytes=32 * 1024 * 1024),
        cost_estimate=pl.CostEstimate(
            flops=BSTEPS * 16 * total * width, bytes_accessed=4 * 11 * rows * width, transcendentals=0
        ),
        name="basin_steps",
    )(inside, state, depth, south, north)


def strips_kernel(first_row, links, state, out):
    rows, width = state.shape[1], state.shape[2]
    count = out.shape[0]
    span = 2 * LANES
    top = first_row[0]

    def piece(b, carry):
        row = jnp.clip(links[b, 0] - top, 0, rows - 1)
        col = links[b, 1]
        start = jnp.clip(col // LANES, 0, width // LANES - 2) * LANES
        shift = lax.rem(span - (col - start), span)
        for i, f in enumerate((0, 2)):
            chunk = state[f, pl.ds(row, 1), pl.ds(pl.multiple_of(start, LANES), span)]
            moved = pltpu.roll(chunk, shift, 1)
            out[b, pl.ds(i, 1), :] = moved[:, :LANES]
        return carry

    lax.fori_loop(0, count, piece, 0, unroll=min(count, 16))


def make_strips(first_row, links, state):
    vmem = pl.BlockSpec(memory_space=pltpu.VMEM)
    smem = pl.BlockSpec(memory_space=pltpu.SMEM)
    return pl.pallas_call(
        strips_kernel,
        out_shape=jax.ShapeDtypeStruct((links.shape[0], 2, LANES), jnp.float32),
        in_specs=[smem, smem, vmem],
        out_specs=vmem,
        name="strips",
    )(first_row, links, state)


def local(basin_state, basin_depth, coast_depth, coast_flow, coast_link):
    strip_rows = basin_state.shape[1]
    devices = lax.axis_size("row")
    position = lax.axis_index("row")

    sent = jnp.broadcast_to(coast_link, (devices, 3))
    links = lax.all_to_all(sent, "row", 0, 0, tiled=True)

    def rows_of(start):
        return jnp.concatenate(
            [basin_state[:, start : start + HALO], basin_depth[None, start : start + HALO]], axis=0
        )

    south = lax.ppermute(
        rows_of(strip_rows - HALO), "row", [(i, i + 1) for i in range(devices - 1)]
    )
    north = lax.ppermute(rows_of(0), "row", [(i + 1, i) for i in range(devices - 1)])

    first_row = (position * strip_rows).astype(jnp.int32)[None]
    pieces = make_strips(first_row, links, basin_state)
    strips = lax.all_to_all(pieces, "row", 0, 0, tiled=True)

    depth, flow = coast_depth[0], coast_flow[0]
    bulk = coast_bulk(coast_link, depth, flow)
    inside = (position < devices - 1).astype(jnp.int32)[None]
    basin_out = basin_run(inside, basin_state, basin_depth, south, north)
    coast_out = coast_edge(strip_rows, coast_link, strips, depth, flow, bulk)
    return (basin_out, coast_out[None])


def solution(mesh):
    in_specs = (
        P("scen", "row", None),
        P("row", "scen"),
        P("row", "scen", None),
        P("row", "scen", None, None),
        P("row", "scen"),
    )
    out_specs = (P("scen", "row", None), P("row", "scen", None, None))
    return jax.shard_map(local, mesh=mesh, in_specs=in_specs, out_specs=out_specs, check_vma=False)
```

time: 193 us -> 59.5 us (0.31); the launches traced: 189 us -> 59.1 us
  blocking collectives: 82.9 us -> 0 us
  other arithmetic: 34.1 us -> 0.04 us
  Pallas kernels: 0 us -> 31.5 us
  starting transfers between devices: 36.5 us -> 16.7 us
  local copies, waits for them, and re-layouts: 20.3 us -> 3.76 us
  waiting for transfers between devices: 11.8 us -> 6.33 us
    unnamed x1 -> x0, blocking collectives: 57.8 us -> none
    ppermute x16 -> x2, starting transfers between devices: 36.5 us -> 3.93 us  [the longest x1 2.5 us: local(): lax.ppermute(rows_of(strip_rows - HALO), 'row', [(i, i + 1) for i in rang...]
    pallas_call x0 -> x4, Pallas kernels: none -> 31.5 us  [the longest x1 22.3 us: coast_bulk(): pl.pallas_call(coast_kernel, out_shape=jax.ShapeDtypeStruct((3, cells, ce...]
    all_gather x1 -> x0, blocking collectives: 25.1 us -> none  [local(): all_links = lax.all_gather(coast_link, 'row', axis=0, tiled=True)]
    all_to_all x0 -> x2, starting transfers between devices: none -> 12.8 us  [the longest x1 9.28 us: local(): links = lax.all_to_all(sent, 'row', 0, 0, tiled=True)]
    mul x38 -> x0, other arithmetic: 12.3 us -> none  [the longest x20 9.42 us: rusanov(): return 0.5 * (flux_l + flux_r) - 0.5 * speed * (right - left)]
    sub x30 -> x0, other arithmetic: 12.2 us -> none  [the longest x20 7.35 us: rusanov(): return 0.5 * (flux_l + flux_r) - 0.5 * speed * (right - left)]
    ppermute x16 -> x2, waiting for transfers between devices: 11.8 us -> 0.01 us  [the longest x1 0.01 us: local(): lax.ppermute(rows_of(strip_rows - HALO), 'row', [(i, i + 1) for i in rang...]
  transfers between devices with their start and end apart: 16 -> 4, of which waited for: 7 -> 1; matrix products, arithmetic and copies ran while one was open for 26% -> 1% of each run, Pallas kernels for 0% -> 48%
where the time goes in v1:
time: 59.5 us; the launch traced here: 59.1 us
  Pallas kernels  31.5 us (53%)
  starting transfers between devices  16.7 us (28%)
  waiting for transfers between devices  6.33 us (11%)
  local copies, waits for them, and re-layouts  3.76 us (6%)
  between operations  0.77 us (1%)
    pallas_call x1, Pallas kernels, coast_bulk(): pl.pallas_call(coast_kernel, out_shape=jax.ShapeDtypeStruct((3, cells, ce...  22.3 us
    all_to_all x1, starting transfers between devices, local(): links = lax.all_to_all(sent, 'row', 0, 0, tiled=True)  9.28 us
    all_to_all x1, waiting for transfers between devices, local(): links = lax.all_to_all(sent, 'row', 0, 0, tiled=True)  6.33 us
    pallas_call x1, Pallas kernels, coast_edge(): pl.pallas_call(functools.partial(edge_kernel, strip_rows), out_shape=jax....  4.09 us
    all_to_all x1, starting transfers between devices, local(): strips = lax.all_to_all(pieces, 'row', 0, 0, tiled=True)  3.49 us
    pallas_call x1, Pallas kernels, basin_run(): pl.pallas_call(basin_kernel, out_shape=jax.ShapeDtypeStruct(state.shape,...  3.22 us
    ppermute x1, starting transfers between devices, local(): lax.ppermute(rows_of(strip_rows - HALO), 'row', [(i, i + 1) for i in rang...  2.5 us
    pallas_call x1, Pallas kernels, make_strips(): pl.pallas_call(strips_kernel, out_shape=jax.ShapeDtypeStruct((links.shape...  1.89 us
  transfers between devices with their start and end apart: 4, of which 1 were waited for; matrix products, arithmetic and copies ran while one was open for 1% of the time, Pallas kernels for 48%

profile of v1, /device:TPU:0, one launch (start us, length us, event | category | flops | bytes accessed | tf_op | source)
XLA Modules:
  0.0 59.1 jit_solution(3313439800273803741)
XLA Ops:
  0.6 0.9 %slice_bitcast_fusion = (f32[1,8,2048]{2,1,0:T(8,128)S(1)}, f32[1,8,2048]{2,1,0:T(8,128)S(1)}) fusion(f32[16,2048]{1,0:T(8,128)} %depth.1), kind=kLoop, calls=%fused_computation.2 | loop fusion | bytes 262144 | tf_op jit(solution)/shard_map/broadcast_in_dim | solution.py:382
  1.5 1.1 %fusion = (f32[3,8,2048]{2,1,0:T(8,128)S(1)}, f32[3,8,2048]{2,1,0:T(8,128)S(1)}) fusion(f32[3,16,2048]{2,1,0:T(8,128)} %state.3), kind=kLoop, calls=%fused_computation.4 | loop fusion | bytes 786432 | tf_op jit(solution)/shard_map/slice | solution.py:382
  2.6 0.0 copy-start.1
  2.6 2.5 %collective-permute-start = (f32[4,8,2048]{2,1,0:T(8,128)S(1)}, f32[4,8,2048]{2,1,0:T(8,128)S(1)}, u32[]{:S(2)}, u32[]{:S(2)}) collective-permute-start(f32[4,8,2048]{2,1,0:T(8,128)S(1)} %pad_maximum_fusion), channel_id=1, source_target_pairs={{0,1},{1,2},{2,3},{3,4},{4,5},{5,6},{6,7},{7,8},{8,9},{9,10},{10,1... | collective-permute-start | bytes 786440 | tf_op jit(solution)/shard_map/ppermute | solution.py:385
  5.1 0.0 copy-start.4
  5.2 0.0 copy-start.2
  5.2 1.4 %collective-permute-start.1 = (f32[4,8,2048]{2,1,0:T(8,128)S(1)}, f32[4,8,2048]{2,1,0:T(8,128)S(1)}, u32[]{:S(2)}, u32[]{:S(2)}) collective-permute-start(f32[4,8,2048]{2,1,0:T(8,128)S(1)} %pad_maximum_fusion.1), channel_id=1, source_target_pairs={{1,0},{2,1},{3,2},{4,3},{5,4},{6,5},{7,6},{8,7},{9,8},{10,9},{11,1... | collective-permute-start | bytes 786440 | tf_op jit(solution)/shard_map/ppermute | solution.py:388
  6.6 0.0 copy-done.4
  6.6 0.6 %broadcast_in_dim.27 = s32[16,1,3]{2,1,0:T(1,128)} broadcast(s32[3]{0:T(128)S(1)} %bitcast.15), dimensions={2} | broadcast | bytes 204 | tf_op jit(solution)/shard_map/broadcast_in_dim | solution.py:377
  7.2 9.3 %all-to-all-start = ((s32[16,1,3]{2,1,0:T(1,128)}), s32[16,1,3]{2,1,0:T(1,128)S(1)}, u32[]{:S(2)}, u32[]{:S(2)}) async-start(s32[16,1,3]{2,1,0:T(1,128)} %broadcast_in_dim.27), calls=%async_computation | async-start | bytes 16384 | tf_op jit(solution)/shard_map/all_to_all | solution.py:378
  16.5 6.3 %all-to-all-done = s32[16,1,3]{2,1,0:T(1,128)S(1)} async-done(((s32[16,1,3]{2,1,0:T(1,128)}), s32[16,1,3]{2,1,0:T(1,128)S(1)}, u32[]{:S(2)}, u32[]{:S(2)}) %all-to-all-start) | async-done | bytes 224 | tf_op jit(solution)/shard_map/all_to_all | solution.py:378
  22.8 0.0 copy-start.6
  22.8 0.6 %copy-done.6 = s32[16,1,3]{2,1,0:T(1,128)} copy-done((s32[16,1,3]{2,1,0:T(1,128)}, s32[16,1,3]{2,1,0:T(1,128)S(1)}, u32[]{:S(2)}) %copy-start.6) | copy-done | bytes 216
  23.4 1.9 %strips.1 = f32[16,2,128]{2,1,0:T(2,128)} custom-call(s32[1]{0:T(128)} %bitcast.3.first_row, s32[16,3]{1,0:T(8,128)} %bitcast.17, f32[3,16,2048]{2,1,0:T(8,128)} %state.3), custom_call_target="tpu_custom_call" | custom-call | tf_op jit(solution)/shard_map/strips/pallas_call | solution.py:363
  25.3 3.5 %all-to-all-start.1 = ((f32[16,2,128]{2,1,0:T(2,128)}), f32[16,2,128]{2,1,0:T(2,128)S(1)}, u32[]{:S(2)}, u32[]{:S(2)}) async-start(f32[16,2,128]{2,1,0:T(2,128)} %strips.1), calls=%async_computation.1 | async-start | bytes 32768 | tf_op jit(solution)/shard_map/all_to_all | solution.py:392
  28.8 0.0 copy-done.1
  28.8 0.0 copy-done.2
  28.9 22.3 %coast_bulk.1.before = f32[3,256,256]{2,1,0:T(8,128)} custom-call(s32[1,3]{1,0:T(1,128)S(1)} %copy-done.4, f32[256,256]{1,0:T(8,128)S(1)} %bitcast.14, f32[2,256,256]{2,1,0:T(8,128)S(1)} %bitcast.12), custom_call_target="tpu_custom_call" | custom-call | flops 45875200 | bytes 1572864 | tf_op jit(solution)/shard_map/coast_bulk/pallas_call | solution.py:191
  51.2 0.0 copy-start
  51.2 0.0 copy-start.3
  51.2 0.0 all-to-all-done.1.strips
  51.2 0.0 copy-start.5
  51.2 0.6 %copy-done.5 = f32[16,2,128]{2,1,0:T(2,128)} copy-done((f32[16,2,128]{2,1,0:T(2,128)}, f32[16,2,128]{2,1,0:T(2,128)S(1)}, u32[]{:S(2)}) %copy-start.5) | copy-done | bytes 16408
  51.8 4.1 %coast_edge.1 = f32[3,256,256]{2,1,0:T(8,128)} custom-call(s32[1,3]{1,0:T(1,128)} %link.3, f32[16,2,128]{2,1,0:T(2,128)} %copy-done.5, f32[256,256]{1,0:T(8,128)} %bitcast.13, f32[2,256,256]{2,1,0:T(8,128)} %bitcast.11, f32[3,256,256]{2,1,0:T(8,128)} %coast_bulk.1.before), custom_call_target="tpu_custom_call", output_to_operand_aliasing={{}: (4, {})} | custom-call | flops 4300800 | bytes 102400 | tf_op jit(solution)/shard_map/coast_edge/pallas_call | solution.py:255
  55.9 0.0 collective-permute-done.south
  55.9 0.0 collective-permute-done.1.north
  55.9 0.0 copy-done
  55.9 0.0 copy-done.3
  55.9 3.2 %basin_steps.1 = f32[3,16,2048]{2,1,0:T(8,128)} custom-call(s32[1]{0:T(128)} %bitcast.inside, f32[3,16,2048]{2,1,0:T(8,128)S(1)} %copy-done, f32[16,2048]{1,0:T(8,128)S(1)} %copy-done.3, f32[4,8,2048]{2,1,0:T(8,128)S(1)} %collective-permute-done.south, f32[4,8,2048]{2,1,0:T(8,128)S(1)} %collective-permute-done.1.north), custom_call_target="tpu_custom_call" | custom-call | flops 8388608 | bytes 1441792 | tf_op jit(solution)/shard_map/basin_steps/pallas_call | solution.py:326
  (2 shorter events, 0.0 us)
Async XLA Ops:
  2.6 26.2 %copy-start.1 = (f32[1,2,256,256]{3,2,1,0:T(8,128)S(1)}, f32[1,2,256,256]{3,2,1,0:T(8,128)}, u32[]{:S(2)}) copy-start(f32[1,2,256,256]{3,2,1,0:T(8,128)} %param.8) | copy-start | bytes 1572868
  2.6 53.3 %collective-permute-start = (f32[4,8,2048]{2,1,0:T(8,128)S(1)}, f32[4,8,2048]{2,1,0:T(8,128)S(1)}, u32[]{:S(2)}, u32[]{:S(2)}) collective-permute-start(f32[4,8,2048]{2,1,0:T(8,128)S(1)} %pad_maximum_fusion), channel_id=1, source_target_pairs={{0,1},{1,2},{2,3},{3,4},{4,5},{5,6},{6,7},{7,8},{8,9},{9,10},{10,1... | collective-permute-start | bytes 786440 | tf_op jit(solution)/shard_map/ppermute | solution.py:385
  5.1 1.5 %copy-start.4 = (s32[1,3]{1,0:T(1,128)S(1)}, s32[1,3]{1,0:T(1,128)}, u32[]{:S(2)}) copy-start(s32[1,3]{1,0:T(1,128)} %link.3) | copy-start | bytes 40
  5.2 23.7 %copy-start.2 = (f32[1,256,256]{2,1,0:T(8,128)S(1)}, f32[1,256,256]{2,1,0:T(8,128)}, u32[]{:S(2)}) copy-start(f32[1,256,256]{2,1,0:T(8,128)} %param.7) | copy-start | bytes 786436
  5.2 50.7 %collective-permute-start.1 = (f32[4,8,2048]{2,1,0:T(8,128)S(1)}, f32[4,8,2048]{2,1,0:T(8,128)S(1)}, u32[]{:S(2)}, u32[]{:S(2)}) collective-permute-start(f32[4,8,2048]{2,1,0:T(8,128)S(1)} %pad_maximum_fusion.1), channel_id=1, source_target_pairs={{1,0},{2,1},{3,2},{4,3},{5,4},{6,5},{7,6},{8,7},{9,8},{10,9},{11,1... | collective-permute-start | bytes 786440 | tf_op jit(solution)/shard_map/ppermute | solution.py:388
  7.2 15.6 %all-to-all-start = ((s32[16,1,3]{2,1,0:T(1,128)}), s32[16,1,3]{2,1,0:T(1,128)S(1)}, u32[]{:S(2)}, u32[]{:S(2)}) async-start(s32[16,1,3]{2,1,0:T(1,128)} %broadcast_in_dim.27), calls=%async_computation | async-start | bytes 16384 | tf_op jit(solution)/shard_map/all_to_all | solution.py:378
  22.8 0.6 %copy-start.6 = (s32[16,1,3]{2,1,0:T(1,128)}, s32[16,1,3]{2,1,0:T(1,128)S(1)}, u32[]{:S(2)}) copy-start(s32[16,1,3]{2,1,0:T(1,128)S(1)} %all-to-all-done) | copy-start | bytes 580
  25.3 25.9 %all-to-all-start.1 = ((f32[16,2,128]{2,1,0:T(2,128)}), f32[16,2,128]{2,1,0:T(2,128)S(1)}, u32[]{:S(2)}, u32[]{:S(2)}) async-start(f32[16,2,128]{2,1,0:T(2,128)} %strips.1), calls=%async_computation.1 | async-start | bytes 32768 | tf_op jit(solution)/shard_map/all_to_all | solution.py:392
  51.2 4.7 %copy-start = (f32[3,16,2048]{2,1,0:T(8,128)S(1)}, f32[3,16,2048]{2,1,0:T(8,128)}, u32[]{:S(2)}) copy-start(f32[3,16,2048]{2,1,0:T(8,128)} %state.3) | copy-start | bytes 1179652
  51.2 4.7 %copy-start.3 = (f32[16,2048]{1,0:T(8,128)S(1)}, f32[16,2048]{1,0:T(8,128)}, u32[]{:S(2)}) copy-start(f32[16,2048]{1,0:T(8,128)} %depth.1) | copy-start | bytes 393220
  51.2 0.6 %copy-start.5 = (f32[16,2,128]{2,1,0:T(2,128)}, f32[16,2,128]{2,1,0:T(2,128)S(1)}, u32[]{:S(2)}) copy-start(f32[16,2,128]{2,1,0:T(2,128)S(1)} %all-to-all-done.1.strips) | copy-start | bytes 49156

commit v2 on v1

--- a/solution.py
+++ b/solution.py
@@ -100,15 +100,15 @@
     ]
 
 
-def coast_steps(state, rows, steps, ghost):
+def coast_steps(here, there, rows, steps, ghost):
     lane, sub = lane_ids(), row_ids()
     first, last = lane == 0, lane == LANES - 1
     top, bottom = sub == 0, sub == SUB - 1
 
-    def load(k):
+    def load(state, k):
         return [cell_terms([state[f, half, k] for f in range(3)]) for half in range(2)]
 
-    def store(k, both):
+    def store(state, k, both):
         for half in range(2):
             for f in range(3):
                 state[f, half, k] = both[half][f]
@@ -120,18 +120,18 @@
             out[name] = [jnp.where(top, h, down(t)) for h, t in zip(head[name], tail[name])]
         return out
 
-    def step(_, carry):
-        tails = load(rows - 1)
+    def step(old, new):
+        tails = load(old, rows - 1)
         prev, acc, start = None, None, None
         for k in range(rows):
-            cur = load(k)
+            cur = load(old, k)
             if k == 0:
                 heads = cur if ghost is None else ghost
                 above = [wrapped(t, h) for t, h in zip(tails, heads)]
                 start = face = [y_face(a, b) for a, b in zip(above, cur)]
             else:
                 face = [y_face(a, b) for a, b in zip(prev, cur)]
-                store(k - 1, [[x + g for x, g in zip(xs, gs)] for xs, gs in zip(acc, face)])
+                store(new, k - 1, [[x + g for x, g in zip(xs, gs)] for xs, gs in zip(acc, face)])
             acc = x_part(cur[0], cur[1], first, last)
             acc = [[x - g for x, g in zip(xs, gs)] for xs, gs in zip(acc, face)]
             prev = cur
@@ -142,18 +142,20 @@
             ]
             for cell, gs in zip(prev, start)
         ]
-        store(rows - 1, [[x + g for x, g in zip(xs, gs)] for xs, gs in zip(acc, end)])
+        store(new, rows - 1, [[x + g for x, g in zip(xs, gs)] for xs, gs in zip(acc, end)])
+
+    def pair(_, carry):
+        step(here, there)
+        step(there, here)
         return carry
 
-    lax.fori_loop(0, steps, step, 0)
-
-
-def fold_in(source, tmp, state, table, unit, rows):
-    split = permute(source[...], table) * unit
-    for half in range(2):
-        tmp[half] = split[:, half * LANES : (half + 1) * LANES]
-        for k in range(rows):
-            state[half, k] = tmp[half, pl.ds(k, SUB, stride=rows), :]
+    lax.fori_loop(0, steps // 2, pair, 0)
+
+
+EDGE = 3
+EDGE_ROWS = EDGE * SUB
+EDGE_OUT = 16
+UNITS = (DEPTH_UNIT, FLOW_UNIT, FLOW_UNIT)
 
 
 def unfold(state, tmp, table, unit, rows):
@@ -164,23 +166,31 @@
     return permute(flat * (1.0 / unit), table, transposed=True)
 
 
-def coast_kernel(link, depth, flow, out, state, tmp):
+def coast_kernel(link, depth, flow, out, edge, keep, here, there, tmp):
     rows = depth.shape[0] // SUB
     cells = depth.shape[1]
-    units = (DEPTH_UNIT, FLOW_UNIT, FLOW_UNIT)
-
-    @pl.when(link[0, 2] > 0)
+    wet = link[0, 2] > 0
+    kept = lax.broadcasted_iota(jnp.int32, keep.shape, 0) < jnp.where(wet, CSTEPS, 0)
+    keep[...] = kept.astype(jnp.float32)
+
+    @pl.when(wet)
     def _():
         table = split_columns(cells)
         for f in range(3):
-            source = depth if f == 0 else flow.at[f - 1]
-            fold_in(source, tmp, state.at[f], table, units[f], rows)
-        coast_steps(state, rows, CSTEPS, None)
+            split = permute(depth[...] if f == 0 else flow[f - 1], table) * UNITS[f]
+            for half in range(2):
+                tmp[half] = split[:, half * LANES : (half + 1) * LANES]
+                for k in range(rows):
+                    here[f, half, k] = tmp[half, pl.ds(k, SUB, stride=rows), :]
+                for k in range(EDGE):
+                    edge[f, half, k] = tmp[half, pl.ds(k, SUB, stride=EDGE), :]
+        coast_steps(here, there, rows, CSTEPS, None)
         for f in range(3):
-            out[f] = unfold(state.at[f], tmp, table, units[f], rows)
-
-    @pl.when(link[0, 2] <= 0)
+            out[f] = unfold(here.at[f], tmp, table, UNITS[f], rows)
+
+    @pl.when(jnp.logical_not(wet))
     def _():
+        edge[...] = jnp.zeros_like(edge)
         out[0] = depth[...]
         out[1] = flow[0]
         out[2] = flow[1]
@@ -188,16 +198,18 @@
 
 def coast_bulk(link, depth, flow):
     cells = depth.shape[0]
+    vmem = pl.BlockSpec(memory_space=pltpu.VMEM)
     return pl.pallas_call(
         coast_kernel,
-        out_shape=jax.ShapeDtypeStruct((3, cells, cells), jnp.float32),
-        in_specs=[
-            pl.BlockSpec(memory_space=pltpu.SMEM),
-            pl.BlockSpec(memory_space=pltpu.VMEM),
-            pl.BlockSpec(memory_space=pltpu.VMEM),
-        ],
-        out_specs=pl.BlockSpec(memory_space=pltpu.VMEM),
+        out_shape=(
+            jax.ShapeDtypeStruct((3, cells, cells), jnp.float32),
+            jax.ShapeDtypeStruct((3, 2, EDGE, SUB, LANES), jnp.float32),
+            jax.ShapeDtypeStruct((EDGE_OUT, cells), jnp.float32),
+        ),
+        in_specs=[pl.BlockSpec(memory_space=pltpu.SMEM), vmem, vmem],
+        out_specs=(vmem, vmem, vmem),
         scratch_shapes=[
+            pltpu.VMEM((3, 2, cells // SUB, SUB, LANES), jnp.float32),
             pltpu.VMEM((3, 2, cells // SUB, SUB, LANES), jnp.float32),
             pltpu.VMEM((2, cells, LANES), jnp.float32),
         ],
@@ -209,71 +221,46 @@
     )(link, depth, flow)
 
 
-EDGE = 3
-EDGE_ROWS = EDGE * SUB
-EDGE_OUT = 16
-
-
-def edge_kernel(strip_rows, link, strips, depth, flow, before, out, state, tmp):
-    cells = depth.shape[1]
-    units = (DEPTH_UNIT, FLOW_UNIT, FLOW_UNIT)
-    out[...] = before[...]
-
-    @pl.when(link[0, 2] > 0)
-    def _():
-        table = split_columns(cells)
-        for f in range(3):
-            source = depth if f == 0 else flow.at[f - 1]
-            fold_in(source, tmp, state.at[f], table, units[f], EDGE)
-        strip = strips[link[0, 0] // strip_rows]
-        rows = lax.broadcasted_iota(jnp.int32, (LANES, cells), 0)
-        cols = lax.broadcasted_iota(jnp.int32, (LANES, cells), 1)
-        half = cells // 2
-        cols = jnp.where(cols < half, 2 * cols, 2 * (cols - half) + 1)
-        base = cols // 16
-        weight = ((cols % 16).astype(jnp.float32) + 0.5) / 16.0
-        mix = jnp.where(rows == base, 1.0 - weight, 0.0) + jnp.where(rows == base + 1, weight, 0.0)
-        values = jnp.dot(
-            strip, mix, precision=lax.Precision.HIGHEST, preferred_element_type=jnp.float32
-        )
-        level = (ghost_level + values[0:1]) * DEPTH_UNIT
-        inflow = values[1:2] * FLOW_UNIT
-        ghost = []
-        for at in (0, half):
-            h = jnp.broadcast_to(level[:, at : at + half], (SUB, half))
-            mv = jnp.broadcast_to(inflow[:, at : at + half], (SUB, half))
-            ghost.append(cell_terms([h, jnp.zeros_like(h), mv]))
-        coast_steps(state, EDGE, CSTEPS, ghost)
-        keep = lax.broadcasted_iota(jnp.int32, (EDGE_OUT, cells), 0) < CSTEPS
-        for f in range(3):
-            done = unfold(state.at[f], tmp, table, units[f], EDGE)
-            out[f] = jnp.where(keep, done[:EDGE_OUT], before[f])
-
-
-def coast_edge(strip_rows, link, strips, depth, flow, before):
-    cells = depth.shape[0]
+def edge_kernel(ghosts, edge, keep, before, out, here, there, tmp):
+    cells = keep.shape[1]
+    half = cells // 2
+    values = jnp.sum(ghosts[...], axis=0)
+    level = (ghost_level + values[0:1]) * DEPTH_UNIT
+    inflow = values[1:2] * FLOW_UNIT
+    ghost = []
+    for at in (0, half):
+        h = jnp.broadcast_to(level[:, at : at + half], (SUB, half))
+        mv = jnp.broadcast_to(inflow[:, at : at + half], (SUB, half))
+        ghost.append(cell_terms([h, jnp.zeros_like(h), mv]))
+    here[...] = edge[...]
+    coast_steps(here, there, EDGE, CSTEPS, ghost)
+    table = split_columns(cells)
+    for f in range(3):
+        done = unfold(here.at[f], tmp, table, UNITS[f], EDGE)
+        out[f] = jnp.where(keep[...] > 0.0, done[:EDGE_OUT], before[f])
+
+
+def coast_edge(ghosts, edge, keep, before):
+    cells = before.shape[2]
+    vmem = pl.BlockSpec(memory_space=pltpu.VMEM)
+    top = pl.BlockSpec((3, EDGE_OUT, cells), lambda i: (0, 0, 0))
     return pl.pallas_call(
-        functools.partial(edge_kernel, strip_rows),
+        edge_kernel,
         out_shape=jax.ShapeDtypeStruct(before.shape, jnp.float32),
         grid=(1,),
-        in_specs=[
-            pl.BlockSpec(memory_space=pltpu.SMEM),
-            pl.BlockSpec(strips.shape, lambda i: (0, 0, 0)),
-            pl.BlockSpec((EDGE_ROWS, cells), lambda i: (0, 0)),
-            pl.BlockSpec((2, EDGE_ROWS, cells), lambda i: (0, 0, 0)),
-            pl.BlockSpec((3, EDGE_OUT, cells), lambda i: (0, 0, 0)),
-        ],
-        out_specs=pl.BlockSpec((3, EDGE_OUT, cells), lambda i: (0, 0, 0)),
+        in_specs=[vmem, vmem, vmem, top],
+        out_specs=top,
         scratch_shapes=[
+            pltpu.VMEM((3, 2, EDGE, SUB, LANES), jnp.float32),
             pltpu.VMEM((3, 2, EDGE, SUB, LANES), jnp.float32),
             pltpu.VMEM((2, EDGE_ROWS, LANES), jnp.float32),
         ],
-        input_output_aliases={4: 0},
+        input_output_aliases={3: 0},
         cost_estimate=pl.CostEstimate(
             flops=CSTEPS * 70 * EDGE_ROWS * cells, bytes_accessed=4 * 100 * cells, transcendentals=0
         ),
         name="coast_edge",
-    )(link, strips, depth, flow, before)
+    )(ghosts, edge, keep, before)
 
 
 def basin_kernel(inside, state, depth, south, north, out, eta, hu, hv, dep):
@@ -337,36 +324,56 @@
     )(inside, state, depth, south, north)
 
 
-def strips_kernel(first_row, links, state, out):
+def send_kernel(first_row, links, state, depth, ghosts, up, down, strips):
     rows, width = state.shape[1], state.shape[2]
-    count = out.shape[0]
+    count, cells = ghosts.shape[0], ghosts.shape[2]
     span = 2 * LANES
-    top = first_row[0]
+    for f in range(3):
+        up[f] = state[f, rows - HALO :]
+        down[f] = state[f, :HALO]
+    up[3] = depth[rows - HALO :]
+    down[3] = depth[:HALO]
 
     def piece(b, carry):
-        row = jnp.clip(links[b, 0] - top, 0, rows - 1)
+        row = links[b, 0] - first_row[0]
+        owned = jnp.logical_and(row >= 0, row < rows).astype(jnp.float32)
+        row = jnp.clip(row, 0, rows - 1)
         col = links[b, 1]
         start = jnp.clip(col // LANES, 0, width // LANES - 2) * LANES
         shift = lax.rem(span - (col - start), span)
         for i, f in enumerate((0, 2)):
             chunk = state[f, pl.ds(row, 1), pl.ds(pl.multiple_of(start, LANES), span)]
-            moved = pltpu.roll(chunk, shift, 1)
-            out[b, pl.ds(i, 1), :] = moved[:, :LANES]
+            strips[pl.ds(2 * b + i, 1), :] = pltpu.roll(chunk, shift, 1)[:, :LANES] * owned
         return carry
 
     lax.fori_loop(0, count, piece, 0, unroll=min(count, 16))
-
-
-def make_strips(first_row, links, state):
+    at = lax.broadcasted_iota(jnp.int32, (LANES, cells), 0)
+    cols = lax.broadcasted_iota(jnp.int32, (LANES, cells), 1)
+    half = cells // 2
+    cols = jnp.where(cols < half, 2 * cols, 2 * (cols - half) + 1)
+    base = cols // 16
+    weight = ((cols % 16).astype(jnp.float32) + 0.5) / 16.0
+    mix = jnp.where(at == base, 1.0 - weight, 0.0) + jnp.where(at == base + 1, weight, 0.0)
+    values = jnp.dot(
+        strips[...], mix, precision=lax.Precision.HIGHEST, preferred_element_type=jnp.float32
+    )
+    for b in range(count):
+        ghosts[b] = values[2 * b : 2 * b + 2]
+
+
+def to_send(first_row, links, state, depth, cells):
+    count, width = links.shape[0], depth.shape[1]
     vmem = pl.BlockSpec(memory_space=pltpu.VMEM)
     smem = pl.BlockSpec(memory_space=pltpu.SMEM)
+    halo = jax.ShapeDtypeStruct((4, HALO, width), jnp.float32)
     return pl.pallas_call(
-        strips_kernel,
-        out_shape=jax.ShapeDtypeStruct((links.shape[0], 2, LANES), jnp.float32),
-        in_specs=[smem, smem, vmem],
-        out_specs=vmem,
-        name="strips",
-    )(first_row, links, state)
+        send_kernel,
+        out_shape=(jax.ShapeDtypeStruct((count, 2, cells), jnp.float32), halo, halo),
+        in_specs=[smem, smem, vmem, vmem],
+        out_specs=(vmem, vmem, vmem),
+        scratch_shapes=[pltpu.VMEM((2 * count, LANES), jnp.float32)],
+        name="to_send",
+    )(first_row, links, state, depth)
 
 
 def local(basin_state, basin_depth, coast_depth, coast_flow, coast_link):
@@ -377,25 +384,17 @@
     sent = jnp.broadcast_to(coast_link, (devices, 3))
     links = lax.all_to_all(sent, "row", 0, 0, tiled=True)
 
-    def rows_of(start):
-        return jnp.concatenate(
-            [basin_state[:, start : start + HALO], basin_depth[None, start : start + HALO]], axis=0
-        )
-
-    south = lax.ppermute(
-        rows_of(strip_rows - HALO), "row", [(i, i + 1) for i in range(devices - 1)]
-    )
-    north = lax.ppermute(rows_of(0), "row", [(i + 1, i) for i in range(devices - 1)])
-
     first_row = (position * strip_rows).astype(jnp.int32)[None]
-    pieces = make_strips(first_row, links, basin_state)
-    strips = lax.all_to_all(pieces, "row", 0, 0, tiled=True)
-
     depth, flow = coast_depth[0], coast_flow[0]
-    bulk = coast_bulk(coast_link, depth, flow)
+    ghosts, up, down = to_send(first_row, links, basin_state, basin_depth, depth.shape[1])
+    ghosts = lax.all_to_all(ghosts, "row", 0, 0, tiled=True)
+    south = lax.ppermute(up, "row", [(i, i + 1) for i in range(devices - 1)])
+    north = lax.ppermute(down, "row", [(i + 1, i) for i in range(devices - 1)])
+
+    bulk, edge, keep = coast_bulk(coast_link, depth, flow)
     inside = (position < devices - 1).astype(jnp.int32)[None]
     basin_out = basin_run(inside, basin_state, basin_depth, south, north)
-    coast_out = coast_edge(strip_rows, coast_link, strips, depth, flow, bulk)
+    coast_out = coast_edge(ghosts, edge, keep, bulk)
     return (basin_out, coast_out[None])
 
 

time: 59.5 us -> 62.7 us (1.054)
  the two profiles are of different devices: /device:TPU:0 before, /device:TPU:1 now
where the time goes in v2:
time: 62.7 us; the launch traced here: 62.4 us
  Pallas kernels  34.9 us (56%)
  starting transfers between devices  16.4 us (26%)
  waiting for transfers between devices  5.72 us (9%)
  local copies, waits for them, and re-layouts  4.64 us (7%)
  between operations  0.7 us (1%)
    pallas_call x1, Pallas kernels, coast_bulk(): pl.pallas_call(coast_kernel, out_shape=(jax.ShapeDtypeStruct((3, cells, c...  25.8 us
    all_to_all x1, starting transfers between devices, local(): links = lax.all_to_all(sent, 'row', 0, 0, tiled=True)  7.35 us
    all_to_all x1, waiting for transfers between devices, local(): links = lax.all_to_all(sent, 'row', 0, 0, tiled=True)  5.71 us
    all_to_all x1, starting transfers between devices, local(): ghosts = lax.all_to_all(ghosts, 'row', 0, 0, tiled=True)  4.37 us
    unnamed x18, local copies, waits for them, and re-layouts  4.03 us
    pallas_call x1, Pallas kernels, coast_edge(): pl.pallas_call(edge_kernel, out_shape=jax.ShapeDtypeStruct(before.shape,...  3.74 us
    pallas_call x1, Pallas kernels, basin_run(): pl.pallas_call(basin_kernel, out_shape=jax.ShapeDtypeStruct(state.shape,...  3.22 us
    ppermute x1, starting transfers between devices, local(): south = lax.ppermute(up, 'row', [(i, i + 1) for i in range(devices - 1)])  2.73 us
  transfers between devices with their start and end apart: 4, of which 1 were waited for; matrix products, arithmetic and copies ran while one was open for 0% of the time, Pallas kernels for 47%

profile of v2, /device:TPU:1, one launch (start us, length us, event | category | flops | bytes accessed | tf_op | source)
XLA Modules:
  0.0 62.4 jit_solution(2488018981820009909)
XLA Ops:
  0.6 0.0 copy-start.6
  0.6 0.0 copy-start.1
  0.6 0.6 %copy-done.6 = s32[1,3]{1,0:T(1,128)S(1)} copy-done((s32[1,3]{1,0:T(1,128)S(1)}, s32[1,3]{1,0:T(1,128)}, u32[]{:S(2)}) %copy-start.6) | copy-done | bytes 36
  1.3 0.6 broadcast_in_dim.19
  1.9 7.3 %all-to-all-start = ((s32[16,1,3]{2,1,0:T(1,128)}), s32[16,1,3]{2,1,0:T(1,128)S(1)}, u32[]{:S(2)}, u32[]{:S(2)}) async-start(s32[16,1,3]{2,1,0:T(1,128)} %broadcast_in_dim.19), calls=%async_computation | async-start | bytes 16384 | tf_op jit(solution)/shard_map/all_to_all | solution.py:385
  9.2 5.7 %all-to-all-done = s32[16,1,3]{2,1,0:T(1,128)S(1)} async-done(((s32[16,1,3]{2,1,0:T(1,128)}), s32[16,1,3]{2,1,0:T(1,128)S(1)}, u32[]{:S(2)}, u32[]{:S(2)}) %all-to-all-start) | async-done | bytes 224 | tf_op jit(solution)/shard_map/all_to_all | solution.py:385
  14.9 0.0 copy-start.8
  15.0 0.6 copy-done.8
  15.5 2.1 %to_send.1 = (f32[16,2,256]{2,1,0:T(2,128)}, f32[4,8,2048]{2,1,0:T(8,128)}, f32[4,8,2048]{2,1,0:T(8,128)}) custom-call(s32[1]{0:T(128)} %bitcast.1.first_row, s32[16,3]{1,0:T(8,128)} %bitcast.11, f32[3,16,2048]{2,1,0:T(8,128)} %state.3, f32[16,2048]{1,0:T(8,128)} %depth.3), custom_call_target="tpu_custom_call" | custom-call | tf_op jit(solution)/shard_map/to_send/pallas_call | solution.py:369
  17.7 2.7 %collective-permute-start = (f32[4,8,2048]{2,1,0:T(8,128)}, f32[4,8,2048]{2,1,0:T(8,128)S(1)}, u32[]{:S(2)}, u32[]{:S(2)}) collective-permute-start(f32[4,8,2048]{2,1,0:T(8,128)} %get-tuple-element.8), channel_id=1, source_target_pairs={{0,1},{1,2},{2,3},{3,4},{4,5},{5,6},{6,7},{7,8},{8,9},{9,10},{10,1... | collective-permute-start | bytes 786440 | tf_op jit(solution)/shard_map/ppermute | solution.py:391
  20.4 1.9 %collective-permute-start.1 = (f32[4,8,2048]{2,1,0:T(8,128)}, f32[4,8,2048]{2,1,0:T(8,128)S(1)}, u32[]{:S(2)}, u32[]{:S(2)}) collective-permute-start(f32[4,8,2048]{2,1,0:T(8,128)} %get-tuple-element.9), channel_id=1, source_target_pairs={{1,0},{2,1},{3,2},{4,3},{5,4},{6,5},{7,6},{8,7},{9,8},{10,9},{11,1... | collective-permute-start | bytes 786440 | tf_op jit(solution)/shard_map/ppermute | solution.py:392
  22.4 4.4 %all-to-all-start.1 = ((f32[16,2,256]{2,1,0:T(2,128)}), f32[16,2,256]{2,1,0:T(2,128)S(1)}, u32[]{:S(2)}, u32[]{:S(2)}) async-start(f32[16,2,256]{2,1,0:T(2,128)} %get-tuple-element.10), calls=%async_computation.1 | async-start | bytes 65536 | tf_op jit(solution)/shard_map/all_to_all | solution.py:390
  26.7 0.0 copy-done.1
  26.7 0.0 copy-start.3
  26.8 0.9 %copy-done.3 = f32[1,256,256]{2,1,0:T(8,128)S(1)} copy-done((f32[1,256,256]{2,1,0:T(8,128)S(1)}, f32[1,256,256]{2,1,0:T(8,128)}, u32[]{:S(2)}) %copy-start.3) | copy-done | bytes 262168
  27.7 25.8 %coast_bulk.1 = (f32[3,256,256]{2,1,0:T(8,128)}, f32[3,2,3,8,128]{4,3,2,1,0:T(8,128)S(1)}, f32[16,256]{1,0:T(8,128)S(1)}) custom-call(s32[1,3]{1,0:T(1,128)S(1)} %copy-done.6, f32[256,256]{1,0:T(8,128)S(1)} %bitcast.8, f32[2,256,256]{2,1,0:T(8,128)S(1)} %bitcast.7), custom_call_target="tpu_custom_call" | custom-call | flops 45875200 | bytes 1572864 | tf_op jit(solution)/shard_map/coast_bulk/pallas_call | solution.py:202
  53.5 0.0 copy-start.4
  53.5 0.6 %copy-done.4 = f32[3,2,3,8,128]{4,3,2,1,0:T(8,128)} copy-done((f32[3,2,3,8,128]{4,3,2,1,0:T(8,128)}, f32[3,2,3,8,128]{4,3,2,1,0:T(8,128)S(1)}, u32[]{:S(2)}) %copy-start.4) | copy-done | bytes 73752
  54.2 0.0 copy-start.5
  54.2 0.6 copy-done.5
  54.8 0.0 all-to-all-done.1.ghosts
  54.8 0.0 copy-start.7
  54.8 0.6 copy-done.7
  55.4 0.0 copy-start
  55.4 0.0 copy-start.2
  55.4 3.7 %coast_edge.1 = f32[3,256,256]{2,1,0:T(8,128)} custom-call(f32[16,2,256]{2,1,0:T(2,128)} %copy-done.7, f32[3,2,3,8,128]{4,3,2,1,0:T(8,128)} %copy-done.4, f32[16,256]{1,0:T(8,128)} %copy-done.5, f32[3,256,256]{2,1,0:T(8,128)} %get-tuple-element.13.before), custom_call_target="tpu_custom_call", output_to_operand_aliasing={{}: (3, {})} | custom-call | flops 4300800 | bytes 102400 | tf_op jit(solution)/shard_map/coast_edge/pallas_call | solution.py:247
  59.1 0.0 collective-permute-done.south
  59.1 0.0 collective-permute-done.1.north
  59.1 0.0 copy-done
  59.1 0.0 copy-done.2
  59.1 3.2 %basin_steps.1 = f32[3,16,2048]{2,1,0:T(8,128)} custom-call(s32[1]{0:T(128)} %bitcast.inside, f32[3,16,2048]{2,1,0:T(8,128)S(1)} %copy-done, f32[16,2048]{1,0:T(8,128)S(1)} %copy-done.2, f32[4,8,2048]{2,1,0:T(8,128)S(1)} %collective-permute-done.south, f32[4,8,2048]{2,1,0:T(8,128)S(1)} %collective-permute-done.1.north), custom_call_target="tpu_custom_call" | custom-call | flops 8388608 | bytes 1441792 | tf_op jit(solution)/shard_map/basin_steps/pallas_call | solution.py:313
Async XLA Ops:
  0.6 0.7 %copy-start.6 = (s32[1,3]{1,0:T(1,128)S(1)}, s32[1,3]{1,0:T(1,128)}, u32[]{:S(2)}) copy-start(s32[1,3]{1,0:T(1,128)} %link.1) | copy-start | bytes 40
  0.6 26.1 %copy-start.1 = (f32[1,2,256,256]{3,2,1,0:T(8,128)S(1)}, f32[1,2,256,256]{3,2,1,0:T(8,128)}, u32[]{:S(2)}) copy-start(f32[1,2,256,256]{3,2,1,0:T(8,128)} %param.8) | copy-start | bytes 1572868
  1.9 13.1 %all-to-all-start = ((s32[16,1,3]{2,1,0:T(1,128)}), s32[16,1,3]{2,1,0:T(1,128)S(1)}, u32[]{:S(2)}, u32[]{:S(2)}) async-start(s32[16,1,3]{2,1,0:T(1,128)} %broadcast_in_dim.19), calls=%async_computation | async-start | bytes 16384 | tf_op jit(solution)/shard_map/all_to_all | solution.py:385
  14.9 0.6 copy-start.8
  17.7 41.4 %collective-permute-start = (f32[4,8,2048]{2,1,0:T(8,128)}, f32[4,8,2048]{2,1,0:T(8,128)S(1)}, u32[]{:S(2)}, u32[]{:S(2)}) collective-permute-start(f32[4,8,2048]{2,1,0:T(8,128)} %get-tuple-element.8), channel_id=1, source_target_pairs={{0,1},{1,2},{2,3},{3,4},{4,5},{5,6},{6,7},{7,8},{8,9},{9,10},{10,1... | collective-permute-start | bytes 786440 | tf_op jit(solution)/shard_map/ppermute | solution.py:391
  20.4 38.7 %collective-permute-start.1 = (f32[4,8,2048]{2,1,0:T(8,128)}, f32[4,8,2048]{2,1,0:T(8,128)S(1)}, u32[]{:S(2)}, u32[]{:S(2)}) collective-permute-start(f32[4,8,2048]{2,1,0:T(8,128)} %get-tuple-element.9), channel_id=1, source_target_pairs={{1,0},{2,1},{3,2},{4,3},{5,4},{6,5},{7,6},{8,7},{9,8},{10,9},{11,1... | collective-permute-start | bytes 786440 | tf_op jit(solution)/shard_map/ppermute | solution.py:392
  22.4 32.4 %all-to-all-start.1 = ((f32[16,2,256]{2,1,0:T(2,128)}), f32[16,2,256]{2,1,0:T(2,128)S(1)}, u32[]{:S(2)}, u32[]{:S(2)}) async-start(f32[16,2,256]{2,1,0:T(2,128)} %get-tuple-element.10), calls=%async_computation.1 | async-start | bytes 65536 | tf_op jit(solution)/shard_map/all_to_all | solution.py:390
  26.7 1.0 %copy-start.3 = (f32[1,256,256]{2,1,0:T(8,128)S(1)}, f32[1,256,256]{2,1,0:T(8,128)}, u32[]{:S(2)}) copy-start(f32[1,256,256]{2,1,0:T(8,128)} %param.7) | copy-start | bytes 786436
  53.5 0.6 %copy-start.4 = (f32[3,2,3,8,128]{4,3,2,1,0:T(8,128)}, f32[3,2,3,8,128]{4,3,2,1,0:T(8,128)S(1)}, u32[]{:S(2)}) copy-start(f32[3,2,3,8,128]{4,3,2,1,0:T(8,128)S(1)} %get-tuple-element.11.edge) | copy-start | bytes 221188
  54.2 0.6 copy-start.5
  54.8 0.6 copy-start.7
  55.4 3.8 %copy-start = (f32[3,16,2048]{2,1,0:T(8,128)S(1)}, f32[3,16,2048]{2,1,0:T(8,128)}, u32[]{:S(2)}) copy-start(f32[3,16,2048]{2,1,0:T(8,128)} %state.3) | copy-start | bytes 1179652
  55.4 3.8 %copy-start.2 = (f32[16,2048]{1,0:T(8,128)S(1)}, f32[16,2048]{1,0:T(8,128)}, u32[]{:S(2)}) copy-start(f32[16,2048]{1,0:T(8,128)} %depth.3) | copy-start | bytes 393220

commit v3 on v2

--- a/solution.py
+++ b/solution.py
@@ -100,18 +100,24 @@
     ]
 
 
-def coast_steps(here, there, rows, steps, ghost):
+def coast_steps(state, rows, group, steps, ghost):
     lane, sub = lane_ids(), row_ids()
     first, last = lane == 0, lane == LANES - 1
     top, bottom = sub == 0, sub == SUB - 1
-
-    def load(state, k):
-        return [cell_terms([state[f, half, k] for f in range(3)]) for half in range(2)]
-
-    def store(state, k, both):
+    zero = jnp.zeros((SUB, LANES), jnp.float32)
+
+    def load(k):
+        return [cell_terms([state[f, half, 1 + k] for f in range(3)]) for half in range(2)]
+
+    def store(k, both):
         for half in range(2):
             for f in range(3):
-                state[f, half, k] = both[half][f]
+                state[f, half, 1 + k] = both[half][f]
+
+    def faces_of(cells):
+        return [
+            {"u": list(cell["u"]), "fy": list(cell["fy"]), "sy": cell["sy"]} for cell in cells
+        ]
 
     def wrapped(tail, head):
         down = functools.partial(pltpu.roll, shift=1, axis=0)
@@ -120,21 +126,27 @@
             out[name] = [jnp.where(top, h, down(t)) for h, t in zip(head[name], tail[name])]
         return out
 
-    def step(old, new):
-        tails = load(old, rows - 1)
-        prev, acc, start = None, None, None
-        for k in range(rows):
-            cur = load(old, k)
-            if k == 0:
-                heads = cur if ghost is None else ghost
-                above = [wrapped(t, h) for t, h in zip(tails, heads)]
-                start = face = [y_face(a, b) for a, b in zip(above, cur)]
-            else:
+    def step(_, carry):
+        tails, heads = load(rows - 1), load(0)
+        above = [wrapped(t, h) for t, h in zip(tails, heads if ghost is None else ghost)]
+        start = [y_face(a, b) for a, b in zip(above, heads)]
+
+        def rows_from(begin, prev, acc):
+            for k in range(group):
+                cur = load(begin + k)
                 face = [y_face(a, b) for a, b in zip(prev, cur)]
-                store(new, k - 1, [[x + g for x, g in zip(xs, gs)] for xs, gs in zip(acc, face)])
-            acc = x_part(cur[0], cur[1], first, last)
-            acc = [[x - g for x, g in zip(xs, gs)] for xs, gs in zip(acc, face)]
-            prev = cur
+                store(begin + k - 1, [[x + g for x, g in zip(*pair)] for pair in zip(acc, face)])
+                acc = x_part(cur[0], cur[1], first, last)
+                acc = [[x - g for x, g in zip(*pair)] for pair in zip(acc, face)]
+                prev = faces_of(cur)
+            return prev, acc
+
+        prev, acc = lax.fori_loop(
+            0,
+            rows // group,
+            lambda i, c: rows_from(i * group, *c),
+            (above, [[zero] * 3 for _ in range(2)]),
+        )
         end = [
             [
                 jnp.where(bottom, -(f + f), pltpu.roll(g, SUB - 1, 0))
@@ -142,16 +154,13 @@
             ]
             for cell, gs in zip(prev, start)
         ]
-        store(new, rows - 1, [[x + g for x, g in zip(xs, gs)] for xs, gs in zip(acc, end)])
-
-    def pair(_, carry):
-        step(here, there)
-        step(there, here)
+        store(rows - 1, [[x + g for x, g in zip(*pair)] for pair in zip(acc, end)])
         return carry
 
-    lax.fori_loop(0, steps // 2, pair, 0)
-
-
+    lax.fori_loop(0, steps, step, 0)
+
+
+GROUP = 8
 EDGE = 3
 EDGE_ROWS = EDGE * SUB
 EDGE_OUT = 16
@@ -161,12 +170,12 @@
 def unfold(state, tmp, table, unit, rows):
     for half in range(2):
         for k in range(rows):
-            tmp[half, pl.ds(k, SUB, stride=rows), :] = state[half, k]
+            tmp[half, pl.ds(k, SUB, stride=rows), :] = state[half, 1 + k]
     flat = jnp.concatenate([tmp[0], tmp[1]], axis=1)
     return permute(flat * (1.0 / unit), table, transposed=True)
 
 
-def coast_kernel(link, depth, flow, out, edge, keep, here, there, tmp):
+def coast_kernel(link, depth, flow, out, edge, keep, state, tmp):
     rows = depth.shape[0] // SUB
     cells = depth.shape[1]
     wet = link[0, 2] > 0
@@ -181,12 +190,12 @@
             for half in range(2):
                 tmp[half] = split[:, half * LANES : (half + 1) * LANES]
                 for k in range(rows):
-                    here[f, half, k] = tmp[half, pl.ds(k, SUB, stride=rows), :]
+                    state[f, half, 1 + k] = tmp[half, pl.ds(k, SUB, stride=rows), :]
                 for k in range(EDGE):
                     edge[f, half, k] = tmp[half, pl.ds(k, SUB, stride=EDGE), :]
-        coast_steps(here, there, rows, CSTEPS, None)
+        coast_steps(state, rows, GROUP, CSTEPS, None)
         for f in range(3):
-            out[f] = unfold(here.at[f], tmp, table, UNITS[f], rows)
+            out[f] = unfold(state.at[f], tmp, table, UNITS[f], rows)
 
     @pl.when(jnp.logical_not(wet))
     def _():
@@ -209,8 +218,7 @@
         in_specs=[pl.BlockSpec(memory_space=pltpu.SMEM), vmem, vmem],
         out_specs=(vmem, vmem, vmem),
         scratch_shapes=[
-            pltpu.VMEM((3, 2, cells // SUB, SUB, LANES), jnp.float32),
-            pltpu.VMEM((3, 2, cells // SUB, SUB, LANES), jnp.float32),
+            pltpu.VMEM((3, 2, 1 + cells // SUB, SUB, LANES), jnp.float32),
             pltpu.VMEM((2, cells, LANES), jnp.float32),
         ],
         compiler_params=pltpu.CompilerParams(vmem_limit_bytes=32 * 1024 * 1024),
@@ -221,7 +229,7 @@
     )(link, depth, flow)
 
 
-def edge_kernel(ghosts, edge, keep, before, out, here, there, tmp):
+def edge_kernel(ghosts, edge, keep, before, out, state, tmp):
     cells = keep.shape[1]
     half = cells // 2
     values = jnp.sum(ghosts[...], axis=0)
@@ -232,11 +240,11 @@
         h = jnp.broadcast_to(level[:, at : at + half], (SUB, half))
         mv = jnp.broadcast_to(inflow[:, at : at + half], (SUB, half))
         ghost.append(cell_terms([h, jnp.zeros_like(h), mv]))
-    here[...] = edge[...]
-    coast_steps(here, there, EDGE, CSTEPS, ghost)
+    state[:, :, 1:] = edge[...]
+    coast_steps(state, EDGE, EDGE, CSTEPS, ghost)
     table = split_columns(cells)
     for f in range(3):
-        done = unfold(here.at[f], tmp, table, UNITS[f], EDGE)
+        done = unfold(state.at[f], tmp, table, UNITS[f], EDGE)
         out[f] = jnp.where(keep[...] > 0.0, done[:EDGE_OUT], before[f])
 
 
@@ -251,8 +259,7 @@
         in_specs=[vmem, vmem, vmem, top],
         out_specs=top,
         scratch_shapes=[
-            pltpu.VMEM((3, 2, EDGE, SUB, LANES), jnp.float32),
-            pltpu.VMEM((3, 2, EDGE, SUB, LANES), jnp.float32),
+            pltpu.VMEM((3, 2, 1 + EDGE, SUB, LANES), jnp.float32),
             pltpu.VMEM((2, EDGE_ROWS, LANES), jnp.float32),
         ],
         input_output_aliases={3: 0},

time: 62.7 us -> 49 us (0.78)
  the two profiles are of different devices: /device:TPU:1 before, /device:TPU:0 now
where the time goes in v3:
time: 49 us; the launch traced here: 48.7 us
  Pallas kernels  21.2 us (43%)
  starting transfers between devices  15.8 us (32%)
  waiting for transfers between devices  6.33 us (13%)
  local copies, waits for them, and re-layouts  4.64 us (9%)
  between operations  0.72 us (1%)
    pallas_call x1, Pallas kernels, coast_bulk(): pl.pallas_call(coast_kernel, out_shape=(jax.ShapeDtypeStruct((3, cells, c...  12.1 us
    all_to_all x1, starting transfers between devices, local(): links = lax.all_to_all(sent, 'row', 0, 0, tiled=True)  7.39 us
    all_to_all x1, waiting for transfers between devices, local(): links = lax.all_to_all(sent, 'row', 0, 0, tiled=True)  6.33 us
    all_to_all x1, starting transfers between devices, local(): ghosts = lax.all_to_all(ghosts, 'row', 0, 0, tiled=True)  5.41 us
    unnamed x18, local copies, waits for them, and re-layouts  4.03 us
    pallas_call x1, Pallas kernels, coast_edge(): pl.pallas_call(edge_kernel, out_shape=jax.ShapeDtypeStruct(before.shape,...  3.77 us
    pallas_call x1, Pallas kernels, basin_run(): pl.pallas_call(basin_kernel, out_shape=jax.ShapeDtypeStruct(state.shape,...  3.22 us
    pallas_call x1, Pallas kernels, to_send(): pl.pallas_call(send_kernel, out_shape=(jax.ShapeDtypeStruct((count, 2, ce...  2.15 us
  transfers between devices with their start and end apart: 4, of which 1 were waited for; matrix products, arithmetic and copies ran while one was open for 0% of the time, Pallas kernels for 33%

profile of v3, /device:TPU:0, one launch (start us, length us, event | category | flops | bytes accessed | tf_op | source)
XLA Modules:
  0.0 48.7 jit_solution(5015640929247966379)
XLA Ops:
  0.6 0.0 copy-start.6
  0.6 0.0 copy-start.1
  0.6 0.6 %copy-done.6 = s32[1,3]{1,0:T(1,128)S(1)} copy-done((s32[1,3]{1,0:T(1,128)S(1)}, s32[1,3]{1,0:T(1,128)}, u32[]{:S(2)}) %copy-start.6) | copy-done | bytes 36
  1.3 0.6 %broadcast_in_dim.19 = s32[16,1,3]{2,1,0:T(1,128)} broadcast(s32[3]{0:T(128)S(1)} %bitcast.9), dimensions={2} | broadcast | bytes 204 | tf_op jit(solution)/shard_map/broadcast_in_dim | solution.py:391
  1.9 7.4 %all-to-all-start = ((s32[16,1,3]{2,1,0:T(1,128)}), s32[16,1,3]{2,1,0:T(1,128)S(1)}, u32[]{:S(2)}, u32[]{:S(2)}) async-start(s32[16,1,3]{2,1,0:T(1,128)} %broadcast_in_dim.19), calls=%async_computation | async-start | bytes 16384 | tf_op jit(solution)/shard_map/all_to_all | solution.py:392
  9.3 6.3 %all-to-all-done = s32[16,1,3]{2,1,0:T(1,128)S(1)} async-done(((s32[16,1,3]{2,1,0:T(1,128)}), s32[16,1,3]{2,1,0:T(1,128)S(1)}, u32[]{:S(2)}, u32[]{:S(2)}) %all-to-all-start) | async-done | bytes 224 | tf_op jit(solution)/shard_map/all_to_all | solution.py:392
  15.6 0.0 copy-start.8
  15.6 0.6 %copy-done.8 = s32[16,1,3]{2,1,0:T(1,128)} copy-done((s32[16,1,3]{2,1,0:T(1,128)}, s32[16,1,3]{2,1,0:T(1,128)S(1)}, u32[]{:S(2)}) %copy-start.8) | copy-done | bytes 216
  16.2 2.1 %to_send.1 = (f32[16,2,256]{2,1,0:T(2,128)}, f32[4,8,2048]{2,1,0:T(8,128)}, f32[4,8,2048]{2,1,0:T(8,128)}) custom-call(s32[1]{0:T(128)} %bitcast.1.first_row, s32[16,3]{1,0:T(8,128)} %bitcast.11, f32[3,16,2048]{2,1,0:T(8,128)} %state.3, f32[16,2048]{1,0:T(8,128)} %depth.3), custom_call_target="tpu_custom_call" | custom-call | tf_op jit(solution)/shard_map/to_send/pallas_call | solution.py:376
  18.4 1.7 %collective-permute-start = (f32[4,8,2048]{2,1,0:T(8,128)}, f32[4,8,2048]{2,1,0:T(8,128)S(1)}, u32[]{:S(2)}, u32[]{:S(2)}) collective-permute-start(f32[4,8,2048]{2,1,0:T(8,128)} %get-tuple-element.8), channel_id=1, source_target_pairs={{0,1},{1,2},{2,3},{3,4},{4,5},{5,6},{6,7},{7,8},{8,9},{9,10},{10,1... | collective-permute-start | bytes 786440 | tf_op jit(solution)/shard_map/ppermute | solution.py:398
  20.1 1.3 %collective-permute-start.1 = (f32[4,8,2048]{2,1,0:T(8,128)}, f32[4,8,2048]{2,1,0:T(8,128)S(1)}, u32[]{:S(2)}, u32[]{:S(2)}) collective-permute-start(f32[4,8,2048]{2,1,0:T(8,128)} %get-tuple-element.9), channel_id=1, source_target_pairs={{1,0},{2,1},{3,2},{4,3},{5,4},{6,5},{7,6},{8,7},{9,8},{10,9},{11,1... | collective-permute-start | bytes 786440 | tf_op jit(solution)/shard_map/ppermute | solution.py:399
  21.4 5.4 %all-to-all-start.1 = ((f32[16,2,256]{2,1,0:T(2,128)}), f32[16,2,256]{2,1,0:T(2,128)S(1)}, u32[]{:S(2)}, u32[]{:S(2)}) async-start(f32[16,2,256]{2,1,0:T(2,128)} %get-tuple-element.10), calls=%async_computation.1 | async-start | bytes 65536 | tf_op jit(solution)/shard_map/all_to_all | solution.py:397
  26.8 0.0 copy-done.1
  26.8 0.0 copy-start.3
  26.8 0.9 %copy-done.3 = f32[1,256,256]{2,1,0:T(8,128)S(1)} copy-done((f32[1,256,256]{2,1,0:T(8,128)S(1)}, f32[1,256,256]{2,1,0:T(8,128)}, u32[]{:S(2)}) %copy-start.3) | copy-done | bytes 262168
  27.7 12.1 %coast_bulk.1 = (f32[3,256,256]{2,1,0:T(8,128)}, f32[3,2,3,8,128]{4,3,2,1,0:T(8,128)S(1)}, f32[16,256]{1,0:T(8,128)S(1)}) custom-call(s32[1,3]{1,0:T(1,128)S(1)} %copy-done.6, f32[256,256]{1,0:T(8,128)S(1)} %bitcast.8, f32[2,256,256]{2,1,0:T(8,128)S(1)} %bitcast.7), custom_call_target="tpu_custom_call" | custom-call | flops 45875200 | bytes 1572864 | tf_op jit(solution)/shard_map/coast_bulk/pallas_call | solution.py:211
  39.8 0.0 copy-start.4
  39.8 0.6 %copy-done.4 = f32[3,2,3,8,128]{4,3,2,1,0:T(8,128)} copy-done((f32[3,2,3,8,128]{4,3,2,1,0:T(8,128)}, f32[3,2,3,8,128]{4,3,2,1,0:T(8,128)S(1)}, u32[]{:S(2)}) %copy-start.4) | copy-done | bytes 73752
  40.5 0.0 copy-start.5
  40.5 0.6 %copy-done.5 = f32[16,256]{1,0:T(8,128)} copy-done((f32[16,256]{1,0:T(8,128)}, f32[16,256]{1,0:T(8,128)S(1)}, u32[]{:S(2)}) %copy-start.5) | copy-done | bytes 16408
  41.1 0.0 all-to-all-done.1.ghosts
  41.1 0.0 copy-start.7
  41.1 0.6 %copy-done.7 = f32[16,2,256]{2,1,0:T(2,128)} copy-done((f32[16,2,256]{2,1,0:T(2,128)}, f32[16,2,256]{2,1,0:T(2,128)S(1)}, u32[]{:S(2)}) %copy-start.7) | copy-done | bytes 32792
  41.7 0.0 copy-start
  41.7 0.0 copy-start.2
  41.7 3.8 %coast_edge.1 = f32[3,256,256]{2,1,0:T(8,128)} custom-call(f32[16,2,256]{2,1,0:T(2,128)} %copy-done.7, f32[3,2,3,8,128]{4,3,2,1,0:T(8,128)} %copy-done.4, f32[16,256]{1,0:T(8,128)} %copy-done.5, f32[3,256,256]{2,1,0:T(8,128)} %get-tuple-element.13.before), custom_call_target="tpu_custom_call", output_to_operand_aliasing={{}: (3, {})} | custom-call | flops 4300800 | bytes 102400 | tf_op jit(solution)/shard_map/coast_edge/pallas_call | solution.py:255
  45.5 0.0 collective-permute-done.south
  45.5 0.0 collective-permute-done.1.north
  45.5 0.0 copy-done
  45.5 0.0 copy-done.2
  45.5 3.2 %basin_steps.1 = f32[3,16,2048]{2,1,0:T(8,128)} custom-call(s32[1]{0:T(128)} %bitcast.inside, f32[3,16,2048]{2,1,0:T(8,128)S(1)} %copy-done, f32[16,2048]{1,0:T(8,128)S(1)} %copy-done.2, f32[4,8,2048]{2,1,0:T(8,128)S(1)} %collective-permute-done.south, f32[4,8,2048]{2,1,0:T(8,128)S(1)} %collective-permute-done.1.north), custom_call_target="tpu_custom_call" | custom-call | flops 8388608 | bytes 1441792 | tf_op jit(solution)/shard_map/basin_steps/pallas_call | solution.py:320
Async XLA Ops:
  0.6 0.7 %copy-start.6 = (s32[1,3]{1,0:T(1,128)S(1)}, s32[1,3]{1,0:T(1,128)}, u32[]{:S(2)}) copy-start(s32[1,3]{1,0:T(1,128)} %link.1) | copy-start | bytes 40
  0.6 26.1 %copy-start.1 = (f32[1,2,256,256]{3,2,1,0:T(8,128)S(1)}, f32[1,2,256,256]{3,2,1,0:T(8,128)}, u32[]{:S(2)}) copy-start(f32[1,2,256,256]{3,2,1,0:T(8,128)} %param.8) | copy-start | bytes 1572868
  1.9 13.7 %all-to-all-start = ((s32[16,1,3]{2,1,0:T(1,128)}), s32[16,1,3]{2,1,0:T(1,128)S(1)}, u32[]{:S(2)}, u32[]{:S(2)}) async-start(s32[16,1,3]{2,1,0:T(1,128)} %broadcast_in_dim.19), calls=%async_computation | async-start | bytes 16384 | tf_op jit(solution)/shard_map/all_to_all | solution.py:392
  15.6 0.6 %copy-start.8 = (s32[16,1,3]{2,1,0:T(1,128)}, s32[16,1,3]{2,1,0:T(1,128)S(1)}, u32[]{:S(2)}) copy-start(s32[16,1,3]{2,1,0:T(1,128)S(1)} %all-to-all-done) | copy-start | bytes 580
  18.4 27.1 %collective-permute-start = (f32[4,8,2048]{2,1,0:T(8,128)}, f32[4,8,2048]{2,1,0:T(8,128)S(1)}, u32[]{:S(2)}, u32[]{:S(2)}) collective-permute-start(f32[4,8,2048]{2,1,0:T(8,128)} %get-tuple-element.8), channel_id=1, source_target_pairs={{0,1},{1,2},{2,3},{3,4},{4,5},{5,6},{6,7},{7,8},{8,9},{9,10},{10,1... | collective-permute-start | bytes 786440 | tf_op jit(solution)/shard_map/ppermute | solution.py:398
  20.1 25.4 %collective-permute-start.1 = (f32[4,8,2048]{2,1,0:T(8,128)}, f32[4,8,2048]{2,1,0:T(8,128)S(1)}, u32[]{:S(2)}, u32[]{:S(2)}) collective-permute-start(f32[4,8,2048]{2,1,0:T(8,128)} %get-tuple-element.9), channel_id=1, source_target_pairs={{1,0},{2,1},{3,2},{4,3},{5,4},{6,5},{7,6},{8,7},{9,8},{10,9},{11,1... | collective-permute-start | bytes 786440 | tf_op jit(solution)/shard_map/ppermute | solution.py:399
  21.4 19.7 %all-to-all-start.1 = ((f32[16,2,256]{2,1,0:T(2,128)}), f32[16,2,256]{2,1,0:T(2,128)S(1)}, u32[]{:S(2)}, u32[]{:S(2)}) async-start(f32[16,2,256]{2,1,0:T(2,128)} %get-tuple-element.10), calls=%async_computation.1 | async-start | bytes 65536 | tf_op jit(solution)/shard_map/all_to_all | solution.py:397
  26.8 1.0 %copy-start.3 = (f32[1,256,256]{2,1,0:T(8,128)S(1)}, f32[1,256,256]{2,1,0:T(8,128)}, u32[]{:S(2)}) copy-start(f32[1,256,256]{2,1,0:T(8,128)} %param.7) | copy-start | bytes 786436
  39.8 0.6 %copy-start.4 = (f32[3,2,3,8,128]{4,3,2,1,0:T(8,128)}, f32[3,2,3,8,128]{4,3,2,1,0:T(8,128)S(1)}, u32[]{:S(2)}) copy-start(f32[3,2,3,8,128]{4,3,2,1,0:T(8,128)S(1)} %get-tuple-element.11.edge) | copy-start | bytes 221188
  40.5 0.6 %copy-start.5 = (f32[16,256]{1,0:T(8,128)}, f32[16,256]{1,0:T(8,128)S(1)}, u32[]{:S(2)}) copy-start(f32[16,256]{1,0:T(8,128)S(1)} %get-tuple-element.12.keep) | copy-start | bytes 49156
  41.1 0.6 %copy-start.7 = (f32[16,2,256]{2,1,0:T(2,128)}, f32[16,2,256]{2,1,0:T(2,128)S(1)}, u32[]{:S(2)}) copy-start(f32[16,2,256]{2,1,0:T(2,128)S(1)} %all-to-all-done.1.ghosts) | copy-start | bytes 98308
  41.7 3.8 %copy-start = (f32[3,16,2048]{2,1,0:T(8,128)S(1)}, f32[3,16,2048]{2,1,0:T(8,128)}, u32[]{:S(2)}) copy-start(f32[3,16,2048]{2,1,0:T(8,128)} %state.3) | copy-start | bytes 1179652
  41.7 3.8 %copy-start.2 = (f32[16,2048]{1,0:T(8,128)S(1)}, f32[16,2048]{1,0:T(8,128)}, u32[]{:S(2)}) copy-start(f32[16,2048]{1,0:T(8,128)} %depth.3) | copy-start | bytes 393220

commit v4 on v3

--- a/solution.py
+++ b/solution.py
@@ -29,26 +29,6 @@
 
 def row_ids():
     return lax.broadcasted_iota(jnp.int32, (SUB, LANES), 0)
-
-
-def split_columns(cells):
-    rows = lax.broadcasted_iota(jnp.int32, (cells, cells), 0)
-    cols = lax.broadcasted_iota(jnp.int32, (cells, cells), 1)
-    half = cells // 2
-    source = jnp.where(cols < half, 2 * cols, 2 * (cols - half) + 1)
-    return (rows == source).astype(jnp.bfloat16)
-
-
-def permute(values, table, transposed=False):
-    dims = (((1,), (1 if transposed else 0,)), ((), ()))
-    total = None
-    rest = values
-    for _ in range(3):
-        part = rest.astype(jnp.bfloat16)
-        rest = rest - part.astype(jnp.float32)
-        term = lax.dot_general(part, table, dims, preferred_element_type=jnp.float32)
-        total = term if total is None else total + term
-    return total
 
 
 def inverse(x):
@@ -73,23 +53,27 @@
     }
 
 
-def x_part(even, odd, first, last):
+def x_part(west, east, first, last):
     left = functools.partial(pltpu.roll, shift=LANES - 1, axis=1)
     right = functools.partial(pltpu.roll, shift=1, axis=1)
-    next_u = [left(a) for a in even["u"]]
-    next_f = [next_u[1], left(even["fx"][1]), left(even["fx"][2])]
-    a_in = jnp.maximum(even["sx"], odd["sx"])
-    a_out = jnp.where(last, 0.0, jnp.maximum(odd["sx"], left(even["sx"])))
-    d_in = [a_in * (o - e) for e, o in zip(even["u"], odd["u"])]
-    d_out = [a_out * (n - o) for o, n in zip(odd["u"], next_u)]
-    new_even, new_odd = [], []
+
+    def following(w, e):
+        lw, le = left(w), left(e)
+        return jnp.where(last, le, lw), jnp.where(last, e, le)
+
+    next_s = following(west["sx"], east["sx"])
+    next_u = [following(w, e) for w, e in zip(west["u"], east["u"])]
+    next_f = [next_u[1]] + [following(west["fx"][i], east["fx"][i]) for i in (1, 2)]
+    a_w = jnp.maximum(west["sx"], next_s[0])
+    a_e = jnp.maximum(east["sx"], next_s[1])
+    new_west, new_east = [], []
     for i in range(3):
-        f_e, f_o = even["fx"][i], odd["fx"][i]
-        f_next = jnp.where(last, f_o, next_f[i])
-        f_back = jnp.where(first, f_e, right(f_o))
-        new_even.append(even["u"][i] + ((d_in[i] - right(d_out[i])) - (f_o - f_back)))
-        new_odd.append(odd["u"][i] + ((d_out[i] - d_in[i]) - (f_next - f_e)))
-    return new_even, new_odd
+        g_w = a_w * (next_u[i][0] - west["u"][i]) - (west["fx"][i] + next_f[i][0])
+        g_e = a_e * (next_u[i][1] - east["u"][i]) - (east["fx"][i] + next_f[i][1])
+        rw, re = right(g_w), right(g_e)
+        new_west.append(west["u"][i] + (g_w - jnp.where(first, -2.0 * west["fx"][i], rw)))
+        new_east.append(east["u"][i] + (g_e - jnp.where(first, rw, re)))
+    return new_west, new_east
 
 
 def y_face(above, below):
@@ -167,42 +151,57 @@
 UNITS = (DEPTH_UNIT, FLOW_UNIT, FLOW_UNIT)
 
 
-def unfold(state, tmp, table, unit, rows):
-    for half in range(2):
-        for k in range(rows):
-            tmp[half, pl.ds(k, SUB, stride=rows), :] = state[half, 1 + k]
-    flat = jnp.concatenate([tmp[0], tmp[1]], axis=1)
-    return permute(flat * (1.0 / unit), table, transposed=True)
-
-
 def coast_kernel(link, depth, flow, out, edge, keep, state, tmp):
     rows = depth.shape[0] // SUB
-    cells = depth.shape[1]
     wet = link[0, 2] > 0
     kept = lax.broadcasted_iota(jnp.int32, keep.shape, 0) < jnp.where(wet, CSTEPS, 0)
     keep[...] = kept.astype(jnp.float32)
+    halves = (slice(0, LANES), slice(LANES, 2 * LANES))
+    tall = 32
+
+    def copy_in(i, carry):
+        at = pl.ds(pl.multiple_of(i * tall, tall), tall)
+        for f in range(3):
+            raw = depth[at] if f == 0 else flow[f - 1, at]
+            out[f, at] = raw
+            for p in range(2):
+                tmp[f, p, at] = raw[:, halves[p]] * UNITS[f]
+        return carry
+
+    def fold(k, carry):
+        for f in range(3):
+            for p in range(2):
+                state[f, p, 1 + k] = tmp[f, p, pl.ds(k, SUB, stride=rows), :]
+        return carry
+
+    def unfold(k, carry):
+        for f in range(3):
+            for p in range(2):
+                tmp[f, p, pl.ds(k, SUB, stride=rows), :] = state[f, p, 1 + k]
+        return carry
+
+    def copy_out(i, carry):
+        at = pl.ds(pl.multiple_of(i * tall, tall), tall)
+        for f in range(3):
+            for p in range(2):
+                out[f, at, halves[p]] = tmp[f, p, at] * (1.0 / UNITS[f])
+        return carry
+
+    lax.fori_loop(0, depth.shape[0] // tall, copy_in, 0)
+    for f in range(3):
+        for p in range(2):
+            for k in range(EDGE):
+                edge[f, p, k] = tmp[f, p, pl.ds(k, SUB, stride=EDGE), :]
 
     @pl.when(wet)
     def _():
-        table = split_columns(cells)
-        for f in range(3):
-            split = permute(depth[...] if f == 0 else flow[f - 1], table) * UNITS[f]
-            for half in range(2):
-                tmp[half] = split[:, half * LANES : (half + 1) * LANES]
-                for k in range(rows):
-                    state[f, half, 1 + k] = tmp[half, pl.ds(k, SUB, stride=rows), :]
-                for k in range(EDGE):
-                    edge[f, half, k] = tmp[half, pl.ds(k, SUB, stride=EDGE), :]
+        lax.fori_loop(0, rows, fold, 0, unroll=2)
         coast_steps(state, rows, GROUP, CSTEPS, None)
-        for f in range(3):
-            out[f] = unfold(state.at[f], tmp, table, UNITS[f], rows)
-
-    @pl.when(jnp.logical_not(wet))
-    def _():
-        edge[...] = jnp.zeros_like(edge)
-        out[0] = depth[...]
-        out[1] = flow[0]
-        out[2] = flow[1]
+        lax.fori_loop(0, rows, unfold, 0, unroll=2)
+        lax.fori_loop(0, depth.shape[0] // tall, copy_out, 0)
+
+
+VMEM_LIMIT = 12 * 1024 * 1024
 
 
 def coast_bulk(link, depth, flow):
@@ -219,9 +218,9 @@
         out_specs=(vmem, vmem, vmem),
         scratch_shapes=[
             pltpu.VMEM((3, 2, 1 + cells // SUB, SUB, LANES), jnp.float32),
-            pltpu.VMEM((2, cells, LANES), jnp.float32),
+            pltpu.VMEM((3, 2, cells, LANES), jnp.float32),
         ],
-        compiler_params=pltpu.CompilerParams(vmem_limit_bytes=32 * 1024 * 1024),
+        compiler_params=pltpu.CompilerParams(vmem_limit_bytes=VMEM_LIMIT),
         cost_estimate=pl.CostEstimate(
             flops=CSTEPS * 70 * cells * cells, bytes_accessed=24 * cells * cells, transcendentals=0
         ),
@@ -230,22 +229,23 @@
 
 
 def edge_kernel(ghosts, edge, keep, before, out, state, tmp):
-    cells = keep.shape[1]
-    half = cells // 2
     values = jnp.sum(ghosts[...], axis=0)
     level = (ghost_level + values[0:1]) * DEPTH_UNIT
     inflow = values[1:2] * FLOW_UNIT
+    halves = (slice(0, LANES), slice(LANES, 2 * LANES))
     ghost = []
-    for at in (0, half):
-        h = jnp.broadcast_to(level[:, at : at + half], (SUB, half))
-        mv = jnp.broadcast_to(inflow[:, at : at + half], (SUB, half))
+    for half in halves:
+        h = jnp.broadcast_to(level[:, half], (SUB, LANES))
+        mv = jnp.broadcast_to(inflow[:, half], (SUB, LANES))
         ghost.append(cell_terms([h, jnp.zeros_like(h), mv]))
     state[:, :, 1:] = edge[...]
     coast_steps(state, EDGE, EDGE, CSTEPS, ghost)
-    table = split_columns(cells)
     for f in range(3):
-        done = unfold(state.at[f], tmp, table, UNITS[f], EDGE)
-        out[f] = jnp.where(keep[...] > 0.0, done[:EDGE_OUT], before[f])
+        for p, half in enumerate(halves):
+            for k in range(EDGE):
+                tmp[pl.ds(k, SUB, stride=EDGE), :] = state[f, p, 1 + k]
+            done = tmp[:EDGE_OUT] * (1.0 / UNITS[f])
+            out[f, :, half] = jnp.where(keep[:, half] > 0.0, done, before[f, :, half])
 
 
 def coast_edge(ghosts, edge, keep, before):
@@ -260,9 +260,10 @@
         out_specs=top,
         scratch_shapes=[
             pltpu.VMEM((3, 2, 1 + EDGE, SUB, LANES), jnp.float32),
-            pltpu.VMEM((2, EDGE_ROWS, LANES), jnp.float32),
+            pltpu.VMEM((EDGE_ROWS, LANES), jnp.float32),
         ],
         input_output_aliases={3: 0},
+        compiler_params=pltpu.CompilerParams(vmem_limit_bytes=VMEM_LIMIT),
         cost_estimate=pl.CostEstimate(
             flops=CSTEPS * 70 * EDGE_ROWS * cells, bytes_accessed=4 * 100 * cells, transcendentals=0
         ),
@@ -323,7 +324,7 @@
         in_specs=[pl.BlockSpec(memory_space=pltpu.SMEM), vmem, vmem, vmem, vmem],
         out_specs=vmem,
         scratch_shapes=[pltpu.VMEM((total, width), jnp.float32)] * 4,
-        compiler_params=pltpu.CompilerParams(vmem_limit_bytes=32 * 1024 * 1024),
+        compiler_params=pltpu.CompilerParams(vmem_limit_bytes=VMEM_LIMIT),
         cost_estimate=pl.CostEstimate(
             flops=BSTEPS * 16 * total * width, bytes_accessed=4 * 11 * rows * width, transcendentals=0
         ),
@@ -356,8 +357,6 @@
     lax.fori_loop(0, count, piece, 0, unroll=min(count, 16))
     at = lax.broadcasted_iota(jnp.int32, (LANES, cells), 0)
     cols = lax.broadcasted_iota(jnp.int32, (LANES, cells), 1)
-    half = cells // 2
-    cols = jnp.where(cols < half, 2 * cols, 2 * (cols - half) + 1)
     base = cols // 16
     weight = ((cols % 16).astype(jnp.float32) + 0.5) / 16.0
     mix = jnp.where(at == base, 1.0 - weight, 0.0) + jnp.where(at == base + 1, weight, 0.0)
@@ -379,6 +378,7 @@
         in_specs=[smem, smem, vmem, vmem],
         out_specs=(vmem, vmem, vmem),
         scratch_shapes=[pltpu.VMEM((2 * count, LANES), jnp.float32)],
+        compiler_params=pltpu.CompilerParams(vmem_limit_bytes=VMEM_LIMIT),
         name="to_send",
     )(first_row, links, state, depth)
 
@@ -390,15 +390,16 @@
 
     sent = jnp.broadcast_to(coast_link, (devices, 3))
     links = lax.all_to_all(sent, "row", 0, 0, tiled=True)
+    depth, flow = coast_depth[0], coast_flow[0]
+    bulk, edge, keep = coast_bulk(coast_link, depth, flow)
 
     first_row = (position * strip_rows).astype(jnp.int32)[None]
-    depth, flow = coast_depth[0], coast_flow[0]
+    first_row, bulk = lax.optimization_barrier((first_row, bulk))
     ghosts, up, down = to_send(first_row, links, basin_state, basin_depth, depth.shape[1])
     ghosts = lax.all_to_all(ghosts, "row", 0, 0, tiled=True)
     south = lax.ppermute(up, "row", [(i, i + 1) for i in range(devices - 1)])
     north = lax.ppermute(down, "row", [(i + 1, i) for i in range(devices - 1)])
 
-    bulk, edge, keep = coast_bulk(coast_link, depth, flow)
     inside = (position < devices - 1).astype(jnp.int32)[None]
     basin_out = basin_run(inside, basin_state, basin_depth, south, north)
     coast_out = coast_edge(ghosts, edge, keep, bulk)

time: 49 us -> 53.8 us (1.098)
  starting transfers between devices: 15.8 us -> 30.2 us
  Pallas kernels: 21.2 us -> 9.93 us
  waiting for transfers between devices: 6.33 us -> 9.4 us
  local copies, waits for them, and re-layouts: 4.64 us -> 3.24 us
    ppermute x1, starting transfers between devices: 1.69 us -> 13.5 us  [local(): south = lax.ppermute(up, 'row', [(i, i + 1) for i in range(devices - 1)])]
    pallas_call x1, Pallas kernels: 12.1 us -> 1.56 us  [coast_bulk(): pl.pallas_call(coast_kernel, out_shape=(jax.ShapeDtypeStruct((3, cells, c...]
    all_to_all x1, waiting for transfers between devices: 0.01 us -> 6.63 us  [local(): ghosts = lax.all_to_all(ghosts, 'row', 0, 0, tiled=True)]
    all_to_all x1, waiting for transfers between devices: 6.33 us -> 2.77 us  [local(): links = lax.all_to_all(sent, 'row', 0, 0, tiled=True)]
    all_to_all x1, starting transfers between devices: 5.41 us -> 7.96 us  [local(): ghosts = lax.all_to_all(ghosts, 'row', 0, 0, tiled=True)]
    unnamed x18 -> x10, local copies, waits for them, and re-layouts: 4.03 us -> 2.64 us
  transfers between devices with their start and end apart: 4 -> 4, of which waited for: 1 -> 2; matrix products, arithmetic and copies ran while one was open for 0% -> 0% of each run, Pallas kernels for 33% -> 9%
where the time goes in v4:
time: 53.8 us; the launch traced here: 53.4 us
  starting transfers between devices  30.2 us (56%)
  Pallas kernels  9.93 us (18%)
  waiting for transfers between devices  9.4 us (17%)
  local copies, waits for them, and re-layouts  3.24 us (6%)
  between operations  0.69 us (1%)
    ppermute x1, starting transfers between devices, local(): south = lax.ppermute(up, 'row', [(i, i + 1) for i in range(devices - 1)])  13.5 us
    all_to_all x1, starting transfers between devices, local(): ghosts = lax.all_to_all(ghosts, 'row', 0, 0, tiled=True)  7.96 us
    all_to_all x1, starting transfers between devices, local(): links = lax.all_to_all(sent, 'row', 0, 0, tiled=True)  7.39 us
    all_to_all x1, waiting for transfers between devices, local(): ghosts = lax.all_to_all(ghosts, 'row', 0, 0, tiled=True)  6.63 us
    pallas_call x1, Pallas kernels, coast_edge(): pl.pallas_call(edge_kernel, out_shape=jax.ShapeDtypeStruct(before.shape,...  3.41 us
    pallas_call x1, Pallas kernels, basin_run(): pl.pallas_call(basin_kernel, out_shape=jax.ShapeDtypeStruct(state.shape,...  3.21 us
    all_to_all x1, waiting for transfers between devices, local(): links = lax.all_to_all(sent, 'row', 0, 0, tiled=True)  2.77 us
    unnamed x10, local copies, waits for them, and re-layouts  2.64 us
  transfers between devices with their start and end apart: 4, of which 2 were waited for; matrix products, arithmetic and copies ran while one was open for 0% of the time, Pallas kernels for 9%

profile of v4, /device:TPU:0, one launch (start us, length us, event | category | flops | bytes accessed | tf_op | source)
XLA Modules:
  0.0 53.4 jit_solution(1350560349747683870)
XLA Ops:
  0.6 0.0 copy-start.4
  0.6 0.6 %copy-done.4 = s32[1,3]{1,0:T(1,128)S(1)} copy-done((s32[1,3]{1,0:T(1,128)S(1)}, s32[1,3]{1,0:T(1,128)}, u32[]{:S(2)}) %copy-start.4) | copy-done | bytes 36
  1.3 0.6 %broadcast_in_dim.19 = s32[16,1,3]{2,1,0:T(1,128)} broadcast(s32[3]{0:T(128)S(1)} %bitcast.10), dimensions={2} | broadcast | bytes 204 | tf_op jit(solution)/shard_map/broadcast_in_dim | solution.py:391
  1.9 7.4 %all-to-all-start = ((s32[16,1,3]{2,1,0:T(1,128)}), s32[16,1,3]{2,1,0:T(1,128)S(1)}, u32[]{:S(2)}, u32[]{:S(2)}) async-start(s32[16,1,3]{2,1,0:T(1,128)} %broadcast_in_dim.19), calls=%async_computation | async-start | bytes 16384 | tf_op jit(solution)/shard_map/all_to_all | solution.py:392
  9.3 0.0 copy-start.1
  9.3 1.0 %copy-done.1 = f32[1,2,256,256]{3,2,1,0:T(8,128)S(1)} copy-done((f32[1,2,256,256]{3,2,1,0:T(8,128)S(1)}, f32[1,2,256,256]{3,2,1,0:T(8,128)}, u32[]{:S(2)}) %copy-start.1) | copy-done | bytes 524312
  10.3 0.0 copy-start.3
  10.3 0.9 %copy-done.3 = f32[1,256,256]{2,1,0:T(8,128)S(1)} copy-done((f32[1,256,256]{2,1,0:T(8,128)S(1)}, f32[1,256,256]{2,1,0:T(8,128)}, u32[]{:S(2)}) %copy-start.3) | copy-done | bytes 262168
  11.3 0.0 copy-start
  11.3 0.0 copy-start.2
  11.3 1.6 %coast_bulk.1 = (f32[3,256,256]{2,1,0:T(8,128)}, f32[3,2,3,8,128]{4,3,2,1,0:T(8,128)S(1)}, f32[16,256]{1,0:T(8,128)S(1)}) custom-call(s32[1,3]{1,0:T(1,128)S(1)} %copy-done.4, f32[256,256]{1,0:T(8,128)S(1)} %bitcast.8, f32[2,256,256]{2,1,0:T(8,128)S(1)} %bitcast.7), custom_call_target="tpu_custom_call" | custom-call | flops 45875200 | bytes 1572864 | tf_op jit(solution)/shard_map/coast_bulk/pallas_call | solution.py:210
  12.8 2.8 %all-to-all-done = s32[16,1,3]{2,1,0:T(1,128)S(1)} async-done(((s32[16,1,3]{2,1,0:T(1,128)}), s32[16,1,3]{2,1,0:T(1,128)S(1)}, u32[]{:S(2)}, u32[]{:S(2)}) %all-to-all-start) | async-done | bytes 224 | tf_op jit(solution)/shard_map/all_to_all | solution.py:392
  15.6 0.0 copy-done
  15.6 0.0 copy-done.2
  15.6 1.7 %to_send.1 = (f32[16,2,256]{2,1,0:T(2,128)}, f32[4,8,2048]{2,1,0:T(8,128)S(1)}, f32[4,8,2048]{2,1,0:T(8,128)S(1)}) custom-call(s32[1]{0:T(128)} %bitcast.1.first_row, s32[16,3]{1,0:T(8,128)S(1)} %bitcast.9, f32[3,16,2048]{2,1,0:T(8,128)S(1)} %copy-done, f32[16,2048]{1,0:T(8,128)S(1)} %copy-done.2), custom_call_target="tpu_custom_call" | custom-call | tf_op jit(solution)/shard_map/to_send/pallas_call | solution.py:375
  17.4 13.5 %collective-permute-start = (f32[4,8,2048]{2,1,0:T(8,128)S(1)}, f32[4,8,2048]{2,1,0:T(8,128)S(1)}, u32[]{:S(2)}, u32[]{:S(2)}) collective-permute-start(f32[4,8,2048]{2,1,0:T(8,128)S(1)} %get-tuple-element.12), channel_id=1, source_target_pairs={{0,1},{1,2},{2,3},{3,4},{4,5},{5,6},{6,7},{7,8},{8,9},{9,10},{10,1... | collective-permute-start | bytes 786440 | tf_op jit(solution)/shard_map/ppermute | solution.py:400
  30.9 1.3 %collective-permute-start.1 = (f32[4,8,2048]{2,1,0:T(8,128)S(1)}, f32[4,8,2048]{2,1,0:T(8,128)S(1)}, u32[]{:S(2)}, u32[]{:S(2)}) collective-permute-start(f32[4,8,2048]{2,1,0:T(8,128)S(1)} %get-tuple-element.13), channel_id=1, source_target_pairs={{1,0},{2,1},{3,2},{4,3},{5,4},{6,5},{7,6},{8,7},{9,8},{10,9},{11,1... | collective-permute-start | bytes 786440 | tf_op jit(solution)/shard_map/ppermute | solution.py:401
  32.2 8.0 %all-to-all-start.1 = ((f32[16,2,256]{2,1,0:T(2,128)}), f32[16,2,256]{2,1,0:T(2,128)S(1)}, u32[]{:S(2)}, u32[]{:S(2)}) async-start(f32[16,2,256]{2,1,0:T(2,128)} %get-tuple-element.14), calls=%async_computation.1 | async-start | bytes 65536 | tf_op jit(solution)/shard_map/all_to_all | solution.py:399
  40.2 6.6 %all-to-all-done.1.ghosts = f32[16,2,256]{2,1,0:T(2,128)S(1)} async-done(((f32[16,2,256]{2,1,0:T(2,128)}), f32[16,2,256]{2,1,0:T(2,128)S(1)}, u32[]{:S(2)}, u32[]{:S(2)}) %all-to-all-start.1) | async-done | bytes 32800 | tf_op jit(solution)/shard_map/all_to_all | solution.py:399
  46.8 3.4 %coast_edge.1 = f32[3,256,256]{2,1,0:T(8,128)} custom-call(f32[16,2,256]{2,1,0:T(2,128)S(1)} %all-to-all-done.1.ghosts, f32[3,2,3,8,128]{4,3,2,1,0:T(8,128)S(1)} %get-tuple-element.15.edge, f32[16,256]{1,0:T(8,128)S(1)} %get-tuple-element.16.keep, f32[3,256,256]{2,1,0:T(8,128)} %get-tuple-element.17.before), custom_call_target="tpu_custom_call", output_to_operand_aliasing={{}: (3, {})} | custom-call | flops 4300800 | bytes 102400 | tf_op jit(solution)/shard_map/coast_edge/pallas_call | solution.py:255
  50.2 0.0 collective-permute-done.south
  50.2 0.0 collective-permute-done.1.north
  50.2 3.2 %basin_steps.1 = f32[3,16,2048]{2,1,0:T(8,128)} custom-call(s32[1]{0:T(128)} %bitcast.inside, f32[3,16,2048]{2,1,0:T(8,128)S(1)} %copy-done, f32[16,2048]{1,0:T(8,128)S(1)} %copy-done.2, f32[4,8,2048]{2,1,0:T(8,128)S(1)} %collective-permute-done.south, f32[4,8,2048]{2,1,0:T(8,128)S(1)} %collective-permute-done.1.north), custom_call_target="tpu_custom_call" | custom-call | flops 8388608 | bytes 1441792 | tf_op jit(solution)/shard_map/basin_steps/pallas_call | solution.py:321
Async XLA Ops:
  0.6 0.7 %copy-start.4 = (s32[1,3]{1,0:T(1,128)S(1)}, s32[1,3]{1,0:T(1,128)}, u32[]{:S(2)}) copy-start(s32[1,3]{1,0:T(1,128)} %link.1) | copy-start | bytes 40
  1.9 13.7 %all-to-all-start = ((s32[16,1,3]{2,1,0:T(1,128)}), s32[16,1,3]{2,1,0:T(1,128)S(1)}, u32[]{:S(2)}, u32[]{:S(2)}) async-start(s32[16,1,3]{2,1,0:T(1,128)} %broadcast_in_dim.19), calls=%async_computation | async-start | bytes 16384 | tf_op jit(solution)/shard_map/all_to_all | solution.py:392
  9.3 1.0 %copy-start.1 = (f32[1,2,256,256]{3,2,1,0:T(8,128)S(1)}, f32[1,2,256,256]{3,2,1,0:T(8,128)}, u32[]{:S(2)}) copy-start(f32[1,2,256,256]{3,2,1,0:T(8,128)} %param.8) | copy-start | bytes 1572868
  10.3 0.9 %copy-start.3 = (f32[1,256,256]{2,1,0:T(8,128)S(1)}, f32[1,256,256]{2,1,0:T(8,128)}, u32[]{:S(2)}) copy-start(f32[1,256,256]{2,1,0:T(8,128)} %param.7) | copy-start | bytes 786436
  11.3 4.3 %copy-start = (f32[3,16,2048]{2,1,0:T(8,128)S(1)}, f32[3,16,2048]{2,1,0:T(8,128)}, u32[]{:S(2)}) copy-start(f32[3,16,2048]{2,1,0:T(8,128)} %state.3) | copy-start | bytes 1179652
  11.3 4.3 %copy-start.2 = (f32[16,2048]{1,0:T(8,128)S(1)}, f32[16,2048]{1,0:T(8,128)}, u32[]{:S(2)}) copy-start(f32[16,2048]{1,0:T(8,128)} %depth.3) | copy-start | bytes 393220
  17.4 32.9 %collective-permute-start = (f32[4,8,2048]{2,1,0:T(8,128)S(1)}, f32[4,8,2048]{2,1,0:T(8,128)S(1)}, u32[]{:S(2)}, u32[]{:S(2)}) collective-permute-start(f32[4,8,2048]{2,1,0:T(8,128)S(1)} %get-tuple-element.12), channel_id=1, source_target_pairs={{0,1},{1,2},{2,3},{3,4},{4,5},{5,6},{6,7},{7,8},{8,9},{9,10},{10,1... | collective-permute-start | bytes 786440 | tf_op jit(solution)/shard_map/ppermute | solution.py:400
  30.9 19.3 %collective-permute-start.1 = (f32[4,8,2048]{2,1,0:T(8,128)S(1)}, f32[4,8,2048]{2,1,0:T(8,128)S(1)}, u32[]{:S(2)}, u32[]{:S(2)}) collective-permute-start(f32[4,8,2048]{2,1,0:T(8,128)S(1)} %get-tuple-element.13), channel_id=1, source_target_pairs={{1,0},{2,1},{3,2},{4,3},{5,4},{6,5},{7,6},{8,7},{9,8},{10,9},{11,1... | collective-permute-start | bytes 786440 | tf_op jit(solution)/shard_map/ppermute | solution.py:401
  32.2 14.6 %all-to-all-start.1 = ((f32[16,2,256]{2,1,0:T(2,128)}), f32[16,2,256]{2,1,0:T(2,128)S(1)}, u32[]{:S(2)}, u32[]{:S(2)}) async-start(f32[16,2,256]{2,1,0:T(2,128)} %get-tuple-element.14), calls=%async_computation.1 | async-start | bytes 65536 | tf_op jit(solution)/shard_map/all_to_all | solution.py:399

commit v5 on v4

--- a/solution.py
+++ b/solution.py
@@ -31,14 +31,9 @@
     return lax.broadcasted_iota(jnp.int32, (SUB, LANES), 0)
 
 
-def inverse(x):
-    guess = pl.reciprocal(x, approx=True)
-    return guess * (2.0 - x * guess)
-
-
 def cell_terms(u):
     h, mu, mv = u
-    r = inverse(jnp.maximum(h, depth_floor * DEPTH_UNIT))
+    r = pl.reciprocal(jnp.maximum(h, depth_floor * DEPTH_UNIT), approx=True)
     vx, vy = mu * r, mv * r
     hp = jnp.maximum(h, TINY)
     c = hp * lax.rsqrt(hp)
@@ -53,27 +48,22 @@
     }
 
 
-def x_part(west, east, first, last):
+def x_part(even, odd, first, last):
     left = functools.partial(pltpu.roll, shift=LANES - 1, axis=1)
     right = functools.partial(pltpu.roll, shift=1, axis=1)
-
-    def following(w, e):
-        lw, le = left(w), left(e)
-        return jnp.where(last, le, lw), jnp.where(last, e, le)
-
-    next_s = following(west["sx"], east["sx"])
-    next_u = [following(w, e) for w, e in zip(west["u"], east["u"])]
-    next_f = [next_u[1]] + [following(west["fx"][i], east["fx"][i]) for i in (1, 2)]
-    a_w = jnp.maximum(west["sx"], next_s[0])
-    a_e = jnp.maximum(east["sx"], next_s[1])
-    new_west, new_east = [], []
+    after = cell_terms([jnp.where(last, o, left(e)) for e, o in zip(even["u"], odd["u"])])
+    a_in = jnp.maximum(even["sx"], odd["sx"])
+    a_out = jnp.maximum(odd["sx"], after["sx"])
+    new_even, new_odd = [], []
     for i in range(3):
-        g_w = a_w * (next_u[i][0] - west["u"][i]) - (west["fx"][i] + next_f[i][0])
-        g_e = a_e * (next_u[i][1] - east["u"][i]) - (east["fx"][i] + next_f[i][1])
-        rw, re = right(g_w), right(g_e)
-        new_west.append(west["u"][i] + (g_w - jnp.where(first, -2.0 * west["fx"][i], rw)))
-        new_east.append(east["u"][i] + (g_e - jnp.where(first, rw, re)))
-    return new_west, new_east
+        e, o, n = even["u"][i], odd["u"][i], after["u"][i]
+        f_e, f_o, f_n = even["fx"][i], odd["fx"][i], after["fx"][i]
+        g_in = a_in * (o - e) - (f_e + f_o)
+        g_out = a_out * (n - o) - (f_o + f_n)
+        g_back = jnp.where(first, -2.0 * f_e, right(g_out))
+        new_even.append(e + (g_in - g_back))
+        new_odd.append(o + (g_out - g_in))
+    return new_even, new_odd
 
 
 def y_face(above, below):
@@ -112,7 +102,7 @@
 
     def step(_, carry):
         tails, heads = load(rows - 1), load(0)
-        above = [wrapped(t, h) for t, h in zip(tails, heads if ghost is None else ghost)]
+        above = [wrapped(t, h) for t, h in zip(tails, ghost)]
         start = [y_face(a, b) for a, b in zip(above, heads)]
 
         def rows_from(begin, prev, acc):
@@ -145,17 +135,35 @@
 
 
 GROUP = 8
-EDGE = 3
-EDGE_ROWS = EDGE * SUB
-EDGE_OUT = 16
 UNITS = (DEPTH_UNIT, FLOW_UNIT, FLOW_UNIT)
-
-
-def coast_kernel(link, depth, flow, out, edge, keep, state, tmp):
+VMEM_LIMIT = 12 * 1024 * 1024
+HALF = LANES // 2
+
+
+def pick(values, ids):
+    return jnp.take_along_axis(values, ids, axis=1, mode="promise_in_bounds")
+
+
+def split_columns(west, east):
+    lane = lane_ids()
+    low = lane < HALF
+    twice = 2 * jnp.where(low, lane, lane - HALF)
+    w = pick(west, jnp.where(low, twice, twice + 1))
+    e = pick(east, jnp.where(low, twice + 1, twice))
+    return jnp.where(low, w, e), pltpu.roll(jnp.where(low, e, w), HALF, 1)
+
+
+def join_columns(even, odd):
+    lane = lane_ids()
+    low = lane < HALF
+    odd = pltpu.roll(odd, HALF, 1)
+    w, e = jnp.where(low, even, odd), jnp.where(low, odd, even)
+    half, is_odd = lane // 2, lane % 2
+    return pick(w, half + HALF * is_odd), pick(e, half + HALF * (1 - is_odd))
+
+
+def coast_kernel(link, ghosts, depth, flow, out, state, tmp):
     rows = depth.shape[0] // SUB
-    wet = link[0, 2] > 0
-    kept = lax.broadcasted_iota(jnp.int32, keep.shape, 0) < jnp.where(wet, CSTEPS, 0)
-    keep[...] = kept.astype(jnp.float32)
     halves = (slice(0, LANES), slice(LANES, 2 * LANES))
     tall = 32
 
@@ -170,14 +178,16 @@
 
     def fold(k, carry):
         for f in range(3):
+            both = split_columns(*[tmp[f, p, pl.ds(k, SUB, stride=rows), :] for p in range(2)])
             for p in range(2):
-                state[f, p, 1 + k] = tmp[f, p, pl.ds(k, SUB, stride=rows), :]
+                state[f, p, 1 + k] = both[p]
         return carry
 
     def unfold(k, carry):
         for f in range(3):
+            both = join_columns(state[f, 0, 1 + k], state[f, 1, 1 + k])
             for p in range(2):
-                tmp[f, p, pl.ds(k, SUB, stride=rows), :] = state[f, p, 1 + k]
+                tmp[f, p, pl.ds(k, SUB, stride=rows), :] = both[p]
         return carry
 
     def copy_out(i, carry):
@@ -188,34 +198,29 @@
         return carry
 
     lax.fori_loop(0, depth.shape[0] // tall, copy_in, 0)
-    for f in range(3):
-        for p in range(2):
-            for k in range(EDGE):
-                edge[f, p, k] = tmp[f, p, pl.ds(k, SUB, stride=EDGE), :]
-
-    @pl.when(wet)
+
+    @pl.when(link[0, 2] > 0)
     def _():
-        lax.fori_loop(0, rows, fold, 0, unroll=2)
-        coast_steps(state, rows, GROUP, CSTEPS, None)
-        lax.fori_loop(0, rows, unfold, 0, unroll=2)
+        lax.fori_loop(0, rows, fold, 0, unroll=4)
+        values = jnp.sum(ghosts[...], axis=0)
+        level = (ghost_level + values[0:1]) * DEPTH_UNIT
+        inflow = values[1:2] * FLOW_UNIT
+        spread = [jnp.broadcast_to(v[:, half], (SUB, LANES)) for v in (level, inflow) for half in halves]
+        h, mv = split_columns(*spread[:2]), split_columns(*spread[2:])
+        ghost = [cell_terms([h[p], jnp.zeros_like(h[p]), mv[p]]) for p in range(2)]
+        coast_steps(state, rows, GROUP, CSTEPS, ghost)
+        lax.fori_loop(0, rows, unfold, 0, unroll=4)
         lax.fori_loop(0, depth.shape[0] // tall, copy_out, 0)
 
 
-VMEM_LIMIT = 12 * 1024 * 1024
-
-
-def coast_bulk(link, depth, flow):
+def coast_run(link, ghosts, depth, flow):
     cells = depth.shape[0]
     vmem = pl.BlockSpec(memory_space=pltpu.VMEM)
     return pl.pallas_call(
         coast_kernel,
-        out_shape=(
-            jax.ShapeDtypeStruct((3, cells, cells), jnp.float32),
-            jax.ShapeDtypeStruct((3, 2, EDGE, SUB, LANES), jnp.float32),
-            jax.ShapeDtypeStruct((EDGE_OUT, cells), jnp.float32),
-        ),
-        in_specs=[pl.BlockSpec(memory_space=pltpu.SMEM), vmem, vmem],
-        out_specs=(vmem, vmem, vmem),
+        out_shape=jax.ShapeDtypeStruct((3, cells, cells), jnp.float32),
+        in_specs=[pl.BlockSpec(memory_space=pltpu.SMEM), vmem, vmem, vmem],
+        out_specs=vmem,
         scratch_shapes=[
             pltpu.VMEM((3, 2, 1 + cells // SUB, SUB, LANES), jnp.float32),
             pltpu.VMEM((3, 2, cells, LANES), jnp.float32),
@@ -224,51 +229,8 @@
         cost_estimate=pl.CostEstimate(
             flops=CSTEPS * 70 * cells * cells, bytes_accessed=24 * cells * cells, transcendentals=0
         ),
-        name="coast_bulk",
-    )(link, depth, flow)
-
-
-def edge_kernel(ghosts, edge, keep, before, out, state, tmp):
-    values = jnp.sum(ghosts[...], axis=0)
-    level = (ghost_level + values[0:1]) * DEPTH_UNIT
-    inflow = values[1:2] * FLOW_UNIT
-    halves = (slice(0, LANES), slice(LANES, 2 * LANES))
-    ghost = []
-    for half in halves:
-        h = jnp.broadcast_to(level[:, half], (SUB, LANES))
-        mv = jnp.broadcast_to(inflow[:, half], (SUB, LANES))
-        ghost.append(cell_terms([h, jnp.zeros_like(h), mv]))
-    state[:, :, 1:] = edge[...]
-    coast_steps(state, EDGE, EDGE, CSTEPS, ghost)
-    for f in range(3):
-        for p, half in enumerate(halves):
-            for k in range(EDGE):
-                tmp[pl.ds(k, SUB, stride=EDGE), :] = state[f, p, 1 + k]
-            done = tmp[:EDGE_OUT] * (1.0 / UNITS[f])
-            out[f, :, half] = jnp.where(keep[:, half] > 0.0, done, before[f, :, half])
-
-
-def coast_edge(ghosts, edge, keep, before):
-    cells = before.shape[2]
-    vmem = pl.BlockSpec(memory_space=pltpu.VMEM)
-    top = pl.BlockSpec((3, EDGE_OUT, cells), lambda i: (0, 0, 0))
-    return pl.pallas_call(
-        edge_kernel,
-        out_shape=jax.ShapeDtypeStruct(before.shape, jnp.float32),
-        grid=(1,),
-        in_specs=[vmem, vmem, vmem, top],
-        out_specs=top,
-        scratch_shapes=[
-            pltpu.VMEM((3, 2, 1 + EDGE, SUB, LANES), jnp.float32),
-            pltpu.VMEM((EDGE_ROWS, LANES), jnp.float32),
-        ],
-        input_output_aliases={3: 0},
-        compiler_params=pltpu.CompilerParams(vmem_limit_bytes=VMEM_LIMIT),
-        cost_estimate=pl.CostEstimate(
-            flops=CSTEPS * 70 * EDGE_ROWS * cells, bytes_accessed=4 * 100 * cells, transcendentals=0
-        ),
-        name="coast_edge",
-    )(ghosts, edge, keep, before)
+        name="coast_steps",
+    )(link, ghosts, depth, flow)
 
 
 def basin_kernel(inside, state, depth, south, north, out, eta, hu, hv, dep):
@@ -332,21 +294,37 @@
     )(inside, state, depth, south, north)
 
 
-def send_kernel(first_row, links, state, depth, ghosts, up, down, strips):
+def pack_kernel(after, state, depth, up, down):
+    rows = depth.shape[0]
+    for f in range(4):
+        source = depth if f == 3 else state.at[f]
+        up[f] = source[rows - HALO :]
+        down[f] = source[:HALO]
+
+
+def pack_halos(after, state, depth):
+    vmem = pl.BlockSpec(memory_space=pltpu.VMEM)
+    halo = jax.ShapeDtypeStruct((4, HALO, depth.shape[1]), jnp.float32)
+    return pl.pallas_call(
+        pack_kernel,
+        out_shape=(halo, halo),
+        in_specs=[pl.BlockSpec(memory_space=pl.ANY), vmem, vmem],
+        out_specs=(vmem, vmem),
+        compiler_params=pltpu.CompilerParams(vmem_limit_bytes=VMEM_LIMIT),
+        name="pack_halos",
+    )(after, state, depth)
+
+
+def strips_kernel(first_row, links, state, ghosts, strips):
     rows, width = state.shape[1], state.shape[2]
     count, cells = ghosts.shape[0], ghosts.shape[2]
     span = 2 * LANES
-    for f in range(3):
-        up[f] = state[f, rows - HALO :]
-        down[f] = state[f, :HALO]
-    up[3] = depth[rows - HALO :]
-    down[3] = depth[:HALO]
 
     def piece(b, carry):
-        row = links[b, 0] - first_row[0]
+        row = links[b, 0, 0] - first_row[0]
         owned = jnp.logical_and(row >= 0, row < rows).astype(jnp.float32)
         row = jnp.clip(row, 0, rows - 1)
-        col = links[b, 1]
+        col = links[b, 0, 1]
         start = jnp.clip(col // LANES, 0, width // LANES - 2) * LANES
         shift = lax.rem(span - (col - start), span)
         for i, f in enumerate((0, 2)):
@@ -367,20 +345,19 @@
         ghosts[b] = values[2 * b : 2 * b + 2]
 
 
-def to_send(first_row, links, state, depth, cells):
-    count, width = links.shape[0], depth.shape[1]
+def make_strips(first_row, links, state, cells):
+    count = links.shape[0]
     vmem = pl.BlockSpec(memory_space=pltpu.VMEM)
     smem = pl.BlockSpec(memory_space=pltpu.SMEM)
-    halo = jax.ShapeDtypeStruct((4, HALO, width), jnp.float32)
     return pl.pallas_call(
-        send_kernel,
-        out_shape=(jax.ShapeDtypeStruct((count, 2, cells), jnp.float32), halo, halo),
-        in_specs=[smem, smem, vmem, vmem],
-        out_specs=(vmem, vmem, vmem),
+        strips_kernel,
+        out_shape=jax.ShapeDtypeStruct((count, 2, cells), jnp.float32),
+        in_specs=[smem, smem, vmem],
+        out_specs=vmem,
         scratch_shapes=[pltpu.VMEM((2 * count, LANES), jnp.float32)],
         compiler_params=pltpu.CompilerParams(vmem_limit_bytes=VMEM_LIMIT),
-        name="to_send",
-    )(first_row, links, state, depth)
+        name="strips",
+    )(first_row, links, state)
 
 
 def local(basin_state, basin_depth, coast_depth, coast_flow, coast_link):
@@ -388,21 +365,21 @@
     devices = lax.axis_size("row")
     position = lax.axis_index("row")
 
-    sent = jnp.broadcast_to(coast_link, (devices, 3))
+    sent = jnp.broadcast_to(coast_link, (devices,) + coast_link.shape)
     links = lax.all_to_all(sent, "row", 0, 0, tiled=True)
-    depth, flow = coast_depth[0], coast_flow[0]
-    bulk, edge, keep = coast_bulk(coast_link, depth, flow)
-
-    first_row = (position * strip_rows).astype(jnp.int32)[None]
-    first_row, bulk = lax.optimization_barrier((first_row, bulk))
-    ghosts, up, down = to_send(first_row, links, basin_state, basin_depth, depth.shape[1])
-    ghosts = lax.all_to_all(ghosts, "row", 0, 0, tiled=True)
+
+    up, down = pack_halos(sent, basin_state, basin_depth)
     south = lax.ppermute(up, "row", [(i, i + 1) for i in range(devices - 1)])
     north = lax.ppermute(down, "row", [(i + 1, i) for i in range(devices - 1)])
 
+    first_row = (position * strip_rows).astype(jnp.int32)[None]
+    ghosts = make_strips(first_row, links, basin_state, coast_depth.shape[2])
+    ghosts = lax.all_to_all(ghosts, "row", 0, 0, tiled=True)
+
     inside = (position < devices - 1).astype(jnp.int32)[None]
     basin_out = basin_run(inside, basin_state, basin_depth, south, north)
-    coast_out = coast_edge(ghosts, edge, keep, bulk)
+    coast_link, basin_out = lax.optimization_barrier((coast_link, basin_out))
+    coast_out = coast_run(coast_link, ghosts, coast_depth[0], coast_flow[0])
     return (basin_out, coast_out[None])
 
 

time: 53.8 us -> 48.3 us (0.90)
  starting transfers between devices: 30.2 us -> 16.6 us
  Pallas kernels: 9.93 us -> 17.8 us
    ppermute x1, starting transfers between devices: 13.5 us -> 2.5 us  [local(): south = lax.ppermute(up, 'row', [(i, i + 1) for i in range(devices - 1)])]
    pallas_call x3, Pallas kernels: 6.72 us -> 14.6 us  [the longest x1 12.8 us: coast_run(): pl.pallas_call(coast_kernel, out_shape=jax.ShapeDtypeStruct((3, cells, ce...]
    all_to_all x1, starting transfers between devices: 7.96 us -> 3.5 us  [local(): ghosts = lax.all_to_all(ghosts, 'row', 0, 0, tiled=True)]
    all_to_all x1, waiting for transfers between devices: 2.77 us -> 6.33 us  [local(): links = lax.all_to_all(sent, 'row', 0, 0, tiled=True)]
    all_to_all x1, waiting for transfers between devices: 6.63 us -> 3.32 us  [local(): ghosts = lax.all_to_all(ghosts, 'row', 0, 0, tiled=True)]
    all_to_all x1, starting transfers between devices: 7.39 us -> 9.3 us  [local(): links = lax.all_to_all(sent, 'row', 0, 0, tiled=True)]
    unnamed x10 -> x14, local copies, waits for them, and re-layouts: 2.64 us -> 2.57 us
  transfers between devices with their start and end apart: 4 -> 4, of which waited for: 2 -> 2; matrix products, arithmetic and copies ran while one was open for 0% -> 0% of each run, Pallas kernels for 9% -> 10%
where the time goes in v5:
time: 48.3 us; the launch traced here: 47.9 us
  Pallas kernels  17.8 us (37%)
  starting transfers between devices  16.6 us (34%)
  waiting for transfers between devices  9.65 us (20%)
  local copies, waits for them, and re-layouts  3.17 us (7%)
  between operations  0.73 us (2%)
    pallas_call x1, Pallas kernels, coast_run(): pl.pallas_call(coast_kernel, out_shape=jax.ShapeDtypeStruct((3, cells, ce...  12.8 us
    all_to_all x1, starting transfers between devices, local(): links = lax.all_to_all(sent, 'row', 0, 0, tiled=True)  9.3 us
    all_to_all x1, waiting for transfers between devices, local(): links = lax.all_to_all(sent, 'row', 0, 0, tiled=True)  6.33 us
    all_to_all x1, starting transfers between devices, local(): ghosts = lax.all_to_all(ghosts, 'row', 0, 0, tiled=True)  3.5 us
    all_to_all x1, waiting for transfers between devices, local(): ghosts = lax.all_to_all(ghosts, 'row', 0, 0, tiled=True)  3.32 us
    pallas_call x1, Pallas kernels, basin_run(): pl.pallas_call(basin_kernel, out_shape=jax.ShapeDtypeStruct(state.shape,...  3.21 us
    unnamed x14, local copies, waits for them, and re-layouts  2.57 us
    ppermute x1, starting transfers between devices, local(): south = lax.ppermute(up, 'row', [(i, i + 1) for i in range(devices - 1)])  2.5 us
  transfers between devices with their start and end apart: 4, of which 2 were waited for; matrix products, arithmetic and copies ran while one was open for 0% of the time, Pallas kernels for 10%

profile of v5, /device:TPU:0, one launch (start us, length us, event | category | flops | bytes accessed | tf_op | source)
XLA Modules:
  0.0 47.9 jit_solution(1367433831070480648)
XLA Ops:
  0.6 0.0 copy-start.6
  0.6 0.6 %copy-done.6 = s32[1,3]{1,0:T(1,128)S(1)} copy-done((s32[1,3]{1,0:T(1,128)S(1)}, s32[1,3]{1,0:T(1,128)}, u32[]{:S(2)}) %copy-start.6) | copy-done | bytes 36
  1.3 0.6 %broadcast_in_dim.16.after = s32[16,1,3]{2,1,0:T(1,128)} broadcast(s32[3]{0:T(128)S(1)} %bitcast.8), dimensions={2} | broadcast | bytes 204 | tf_op jit(solution)/shard_map/broadcast_in_dim | solution.py:368
  1.9 0.0 copy-start
  1.9 1.0 %copy-done = f32[3,16,2048]{2,1,0:T(8,128)S(1)} copy-done((f32[3,16,2048]{2,1,0:T(8,128)S(1)}, f32[3,16,2048]{2,1,0:T(8,128)}, u32[]{:S(2)}) %copy-start) | copy-done | bytes 393240
  2.9 0.0 copy-start.3
  2.9 0.9 %copy-done.3 = f32[16,2048]{1,0:T(8,128)S(1)} copy-done((f32[16,2048]{1,0:T(8,128)S(1)}, f32[16,2048]{1,0:T(8,128)}, u32[]{:S(2)}) %copy-start.3) | copy-done | bytes 131096
  3.8 0.0 copy-start.1
  3.8 2.5 %collective-permute-start = (f32[4,8,2048]{2,1,0:T(8,128)S(1)}, f32[4,8,2048]{2,1,0:T(8,128)S(1)}, u32[]{:S(2)}, u32[]{:S(2)}) collective-permute-start(f32[4,8,2048]{2,1,0:T(8,128)S(1)} %get-tuple-element.6), channel_id=1, source_target_pairs={{0,1},{1,2},{2,3},{3,4},{4,5},{5,6},{6,7},{7,8},{8,9},{9,10},{10,1... | collective-permute-start | bytes 786440 | tf_op jit(solution)/shard_map/ppermute | solution.py:372
  6.3 1.3 %collective-permute-start.1 = (f32[4,8,2048]{2,1,0:T(8,128)S(1)}, f32[4,8,2048]{2,1,0:T(8,128)S(1)}, u32[]{:S(2)}, u32[]{:S(2)}) collective-permute-start(f32[4,8,2048]{2,1,0:T(8,128)S(1)} %get-tuple-element.7), channel_id=1, source_target_pairs={{1,0},{2,1},{3,2},{4,3},{5,4},{6,5},{7,6},{8,7},{9,8},{10,9},{11,1... | collective-permute-start | bytes 786440 | tf_op jit(solution)/shard_map/ppermute | solution.py:373
  7.6 9.3 %all-to-all-start = ((s32[16,1,3]{2,1,0:T(1,128)}), s32[16,1,3]{2,1,0:T(1,128)S(1)}, u32[]{:S(2)}, u32[]{:S(2)}) async-start(s32[16,1,3]{2,1,0:T(1,128)} %broadcast_in_dim.16.after), calls=%async_computation | async-start | bytes 16384 | tf_op jit(solution)/shard_map/all_to_all | solution.py:369
  16.9 6.3 %all-to-all-done.links = s32[16,1,3]{2,1,0:T(1,128)S(1)} async-done(((s32[16,1,3]{2,1,0:T(1,128)}), s32[16,1,3]{2,1,0:T(1,128)S(1)}, u32[]{:S(2)}, u32[]{:S(2)}) %all-to-all-start) | async-done | bytes 224 | tf_op jit(solution)/shard_map/all_to_all | solution.py:369
  23.3 0.0 copy-done.1
  23.3 0.0 copy-start.4
  23.3 1.7 %strips.1 = f32[16,2,256]{2,1,0:T(2,128)} custom-call(s32[1]{0:T(128)} %bitcast.2.first_row, s32[16,1,3]{2,1,0:T(1,128)S(1)} %all-to-all-done.links, f32[3,16,2048]{2,1,0:T(8,128)S(1)} %copy-done.1), custom_call_target="tpu_custom_call" | custom-call | tf_op jit(solution)/shard_map/strips/pallas_call | solution.py:352
  25.0 3.5 %all-to-all-start.1 = ((f32[16,2,256]{2,1,0:T(2,128)}), f32[16,2,256]{2,1,0:T(2,128)S(1)}, u32[]{:S(2)}, u32[]{:S(2)}) async-start(f32[16,2,256]{2,1,0:T(2,128)} %strips.1), calls=%async_computation.1 | async-start | bytes 65536 | tf_op jit(solution)/shard_map/all_to_all | solution.py:377
  28.5 0.0 collective-permute-done.south
  28.5 0.0 collective-permute-done.1.north
  28.5 0.0 copy-done.4
  28.6 0.0 copy-start.2
  28.6 0.0 copy-start.5
  28.6 3.2 %basin_steps.1 = f32[3,16,2048]{2,1,0:T(8,128)} custom-call(s32[1]{0:T(128)} %bitcast.inside, f32[3,16,2048]{2,1,0:T(8,128)S(1)} %copy-done.1, f32[16,2048]{1,0:T(8,128)S(1)} %copy-done.4, f32[4,8,2048]{2,1,0:T(8,128)S(1)} %collective-permute-done.south, f32[4,8,2048]{2,1,0:T(8,128)S(1)} %collective-permute-done.1.north), custom_call_target="tpu_custom_call" | custom-call | flops 8388608 | bytes 1441792 | tf_op jit(solution)/shard_map/basin_steps/pallas_call | solution.py:283
  31.8 3.3 %all-to-all-done.1.ghosts = f32[16,2,256]{2,1,0:T(2,128)S(1)} async-done(((f32[16,2,256]{2,1,0:T(2,128)}), f32[16,2,256]{2,1,0:T(2,128)S(1)}, u32[]{:S(2)}, u32[]{:S(2)}) %all-to-all-start.1) | async-done | bytes 32800 | tf_op jit(solution)/shard_map/all_to_all | solution.py:377
  35.1 0.0 copy-done.2
  35.1 0.0 copy-done.5
  35.1 12.8 %coast_steps.1 = f32[3,256,256]{2,1,0:T(8,128)} custom-call(s32[1,3]{1,0:T(1,128)S(1)} %copy-done.6, f32[16,2,256]{2,1,0:T(2,128)S(1)} %all-to-all-done.1.ghosts, f32[256,256]{1,0:T(8,128)S(1)} %bitcast.7, f32[2,256,256]{2,1,0:T(8,128)S(1)} %bitcast.6), custom_call_target="tpu_custom_call" | custom-call | flops 45875200 | bytes 1572864 | tf_op jit(solution)/shard_map/coast_steps/pallas_call | solution.py:219
  (1 shorter events, 0.0 us)
Async XLA Ops:
  0.6 0.7 %copy-start.6 = (s32[1,3]{1,0:T(1,128)S(1)}, s32[1,3]{1,0:T(1,128)}, u32[]{:S(2)}) copy-start(s32[1,3]{1,0:T(1,128)} %link) | copy-start | bytes 40
  1.9 1.0 %copy-start = (f32[3,16,2048]{2,1,0:T(8,128)S(1)}, f32[3,16,2048]{2,1,0:T(8,128)}, u32[]{:S(2)}) copy-start(f32[3,16,2048]{2,1,0:T(8,128)} %state.5) | copy-start | bytes 1179652
  2.9 0.9 %copy-start.3 = (f32[16,2048]{1,0:T(8,128)S(1)}, f32[16,2048]{1,0:T(8,128)}, u32[]{:S(2)}) copy-start(f32[16,2048]{1,0:T(8,128)} %depth.3) | copy-start | bytes 393220
  3.8 19.5 %copy-start.1 = (f32[3,16,2048]{2,1,0:T(8,128)S(1)}, f32[3,16,2048]{2,1,0:T(8,128)}, u32[]{:S(2)}) copy-start(f32[3,16,2048]{2,1,0:T(8,128)} %state.5) | copy-start | bytes 1179652
  3.8 24.7 %collective-permute-start = (f32[4,8,2048]{2,1,0:T(8,128)S(1)}, f32[4,8,2048]{2,1,0:T(8,128)S(1)}, u32[]{:S(2)}, u32[]{:S(2)}) collective-permute-start(f32[4,8,2048]{2,1,0:T(8,128)S(1)} %get-tuple-element.6), channel_id=1, source_target_pairs={{0,1},{1,2},{2,3},{3,4},{4,5},{5,6},{6,7},{7,8},{8,9},{9,10},{10,1... | collective-permute-start | bytes 786440 | tf_op jit(solution)/shard_map/ppermute | solution.py:372
  6.3 22.2 %collective-permute-start.1 = (f32[4,8,2048]{2,1,0:T(8,128)S(1)}, f32[4,8,2048]{2,1,0:T(8,128)S(1)}, u32[]{:S(2)}, u32[]{:S(2)}) collective-permute-start(f32[4,8,2048]{2,1,0:T(8,128)S(1)} %get-tuple-element.7), channel_id=1, source_target_pairs={{1,0},{2,1},{3,2},{4,3},{5,4},{6,5},{7,6},{8,7},{9,8},{10,9},{11,1... | collective-permute-start | bytes 786440 | tf_op jit(solution)/shard_map/ppermute | solution.py:373
  7.6 15.6 %all-to-all-start = ((s32[16,1,3]{2,1,0:T(1,128)}), s32[16,1,3]{2,1,0:T(1,128)S(1)}, u32[]{:S(2)}, u32[]{:S(2)}) async-start(s32[16,1,3]{2,1,0:T(1,128)} %broadcast_in_dim.16.after), calls=%async_computation | async-start | bytes 16384 | tf_op jit(solution)/shard_map/all_to_all | solution.py:369
  23.3 5.3 %copy-start.4 = (f32[16,2048]{1,0:T(8,128)S(1)}, f32[16,2048]{1,0:T(8,128)}, u32[]{:S(2)}) copy-start(f32[16,2048]{1,0:T(8,128)} %depth.3) | copy-start | bytes 393220
  25.0 10.1 %all-to-all-start.1 = ((f32[16,2,256]{2,1,0:T(2,128)}), f32[16,2,256]{2,1,0:T(2,128)S(1)}, u32[]{:S(2)}, u32[]{:S(2)}) async-start(f32[16,2,256]{2,1,0:T(2,128)} %strips.1), calls=%async_computation.1 | async-start | bytes 65536 | tf_op jit(solution)/shard_map/all_to_all | solution.py:377
  28.6 6.6 %copy-start.2 = (f32[1,2,256,256]{3,2,1,0:T(8,128)S(1)}, f32[1,2,256,256]{3,2,1,0:T(8,128)}, u32[]{:S(2)}) copy-start(f32[1,2,256,256]{3,2,1,0:T(8,128)} %param.8) | copy-start | bytes 1572868
  28.6 6.6 %copy-start.5 = (f32[1,256,256]{2,1,0:T(8,128)S(1)}, f32[1,256,256]{2,1,0:T(8,128)}, u32[]{:S(2)}) copy-start(f32[1,256,256]{2,1,0:T(8,128)} %param.7) | copy-start | bytes 786436

commit v6 on v5

--- a/solution.py
+++ b/solution.py
@@ -102,7 +102,7 @@
 
     def step(_, carry):
         tails, heads = load(rows - 1), load(0)
-        above = [wrapped(t, h) for t, h in zip(tails, ghost)]
+        above = [wrapped(t, h) for t, h in zip(tails, heads if ghost is None else ghost)]
         start = [y_face(a, b) for a, b in zip(above, heads)]
 
         def rows_from(begin, prev, acc):
@@ -162,9 +162,17 @@
     return pick(w, half + HALF * is_odd), pick(e, half + HALF * (1 - is_odd))
 
 
-def coast_kernel(link, ghosts, depth, flow, out, state, tmp):
+EDGE = 3
+EDGE_ROWS = EDGE * SUB
+EDGE_OUT = 16
+HALVES = (slice(0, LANES), slice(LANES, 2 * LANES))
+
+
+def coast_kernel(link, depth, flow, out, edge, keep, state, tmp):
     rows = depth.shape[0] // SUB
-    halves = (slice(0, LANES), slice(LANES, 2 * LANES))
+    wet = link[0, 2] > 0
+    kept = lax.broadcasted_iota(jnp.int32, keep.shape, 0) < jnp.where(wet, CSTEPS, 0)
+    keep[...] = kept.astype(jnp.float32)
     tall = 32
 
     def copy_in(i, carry):
@@ -173,7 +181,7 @@
             raw = depth[at] if f == 0 else flow[f - 1, at]
             out[f, at] = raw
             for p in range(2):
-                tmp[f, p, at] = raw[:, halves[p]] * UNITS[f]
+                tmp[f, p, at] = raw[:, HALVES[p]] * UNITS[f]
         return carry
 
     def fold(k, carry):
@@ -183,6 +191,13 @@
                 state[f, p, 1 + k] = both[p]
         return carry
 
+    def fold_edge(k, carry):
+        for f in range(3):
+            both = split_columns(*[tmp[f, p, pl.ds(k, SUB, stride=EDGE), :] for p in range(2)])
+            for p in range(2):
+                edge[f, p, k] = both[p]
+        return carry
+
     def unfold(k, carry):
         for f in range(3):
             both = join_columns(state[f, 0, 1 + k], state[f, 1, 1 + k])
@@ -194,33 +209,32 @@
         at = pl.ds(pl.multiple_of(i * tall, tall), tall)
         for f in range(3):
             for p in range(2):
-                out[f, at, halves[p]] = tmp[f, p, at] * (1.0 / UNITS[f])
+                out[f, at, HALVES[p]] = tmp[f, p, at] * (1.0 / UNITS[f])
         return carry
 
     lax.fori_loop(0, depth.shape[0] // tall, copy_in, 0)
-
-    @pl.when(link[0, 2] > 0)
+    lax.fori_loop(0, EDGE, fold_edge, 0)
+
+    @pl.when(wet)
     def _():
         lax.fori_loop(0, rows, fold, 0, unroll=4)
-        values = jnp.sum(ghosts[...], axis=0)
-        level = (ghost_level + values[0:1]) * DEPTH_UNIT
-        inflow = values[1:2] * FLOW_UNIT
-        spread = [jnp.broadcast_to(v[:, half], (SUB, LANES)) for v in (level, inflow) for half in halves]
-        h, mv = split_columns(*spread[:2]), split_columns(*spread[2:])
-        ghost = [cell_terms([h[p], jnp.zeros_like(h[p]), mv[p]]) for p in range(2)]
-        coast_steps(state, rows, GROUP, CSTEPS, ghost)
+        coast_steps(state, rows, GROUP, CSTEPS, None)
         lax.fori_loop(0, rows, unfold, 0, unroll=4)
         lax.fori_loop(0, depth.shape[0] // tall, copy_out, 0)
 
 
-def coast_run(link, ghosts, depth, flow):
+def coast_bulk(link, depth, flow):
     cells = depth.shape[0]
     vmem = pl.BlockSpec(memory_space=pltpu.VMEM)
     return pl.pallas_call(
         coast_kernel,
-        out_shape=jax.ShapeDtypeStruct((3, cells, cells), jnp.float32),
-        in_specs=[pl.BlockSpec(memory_space=pltpu.SMEM), vmem, vmem, vmem],
-        out_specs=vmem,
+        out_shape=(
+            jax.ShapeDtypeStruct((3, cells, cells), jnp.float32),
+            jax.ShapeDtypeStruct((3, 2, EDGE, SUB, LANES), jnp.float32),
+            jax.ShapeDtypeStruct((EDGE_OUT, cells), jnp.float32),
+        ),
+        in_specs=[pl.BlockSpec(memory_space=pltpu.SMEM), vmem, vmem],
+        out_specs=(vmem, vmem, vmem),
         scratch_shapes=[
             pltpu.VMEM((3, 2, 1 + cells // SUB, SUB, LANES), jnp.float32),
             pltpu.VMEM((3, 2, cells, LANES), jnp.float32),
@@ -229,8 +243,75 @@
         cost_estimate=pl.CostEstimate(
             flops=CSTEPS * 70 * cells * cells, bytes_accessed=24 * cells * cells, transcendentals=0
         ),
-        name="coast_steps",
-    )(link, ghosts, depth, flow)
+        name="coast_bulk",
+    )(link, depth, flow)
+
+
+SLOT = 32
+
+
+def edge_kernel(strip_rows, link, block, strips, edge, keep, before, out, state, tmp, tile, sem):
+    cells = keep.shape[1]
+    per_device = strips.shape[1]
+    row = block[0] // 2
+    copy = pltpu.make_async_copy(
+        strips.at[link[0, 0] // strip_rows, pl.ds(pl.multiple_of(row // SUB * SUB, SUB), SUB)], tile, sem
+    )
+    copy.start()
+    at = lax.broadcasted_iota(jnp.int32, (LANES, cells), 0)
+    place = lax.broadcasted_iota(jnp.int32, (LANES, cells), 1)
+    cols = jnp.where(place < LANES, 2 * place, 2 * (place - LANES) + 1)
+    base = cols // 16
+    weight = ((cols % 16).astype(jnp.float32) + 0.5) / 16.0
+    mix = jnp.where(at == base, 1.0 - weight, 0.0) + jnp.where(at == base + 1, weight, 0.0)
+    state[:, :, 1:] = edge[...]
+    copy.wait()
+    mine = tile[pl.ds(row % SUB, 1), :]
+    mine = jnp.where(block[0] % 2 == 0, mine, pltpu.roll(mine, 2 * SLOT, 1))
+    pair = jnp.concatenate([mine, pltpu.roll(mine, LANES - SLOT, 1)] + [mine] * (SUB - 2), axis=0)
+    values = jnp.dot(pair, mix, precision=lax.Precision.HIGHEST, preferred_element_type=jnp.float32)
+    level = (ghost_level + values[0:1]) * DEPTH_UNIT
+    inflow = values[1:2] * FLOW_UNIT
+    ghost = []
+    for half in HALVES:
+        h = jnp.broadcast_to(level[:, half], (SUB, LANES))
+        mv = jnp.broadcast_to(inflow[:, half], (SUB, LANES))
+        ghost.append(cell_terms([h, jnp.zeros_like(h), mv]))
+    coast_steps(state, EDGE, EDGE, CSTEPS, ghost)
+    for f in range(3):
+        for k in range(EDGE):
+            both = join_columns(state[f, 0, 1 + k], state[f, 1, 1 + k])
+            for p in range(2):
+                tmp[p, pl.ds(k, SUB, stride=EDGE), :] = both[p]
+        for p, half in enumerate(HALVES):
+            done = tmp[p, :EDGE_OUT] * (1.0 / UNITS[f])
+            out[f, :, half] = jnp.where(keep[:, half] > 0.0, done, before[f, :, half])
+
+
+def coast_edge(strip_rows, link, block, strips, edge, keep, before):
+    cells = before.shape[2]
+    vmem = pl.BlockSpec(memory_space=pltpu.VMEM)
+    smem = pl.BlockSpec(memory_space=pltpu.SMEM)
+    top = pl.BlockSpec((3, EDGE_OUT, cells), lambda i: (0, 0, 0))
+    return pl.pallas_call(
+        functools.partial(edge_kernel, strip_rows),
+        out_shape=jax.ShapeDtypeStruct(before.shape, jnp.float32),
+        grid=(1,),
+        in_specs=[smem, smem, pl.BlockSpec(memory_space=pl.ANY), vmem, vmem, top],
+        out_specs=top,
+        scratch_shapes=[
+            pltpu.VMEM((3, 2, 1 + EDGE, SUB, LANES), jnp.float32),
+            pltpu.VMEM((2, EDGE_ROWS, LANES), jnp.float32),
+            pltpu.VMEM((SUB, LANES), jnp.float32),
+            pltpu.SemaphoreType.DMA,
+        ],
+        input_output_aliases={5: 0},
+        compiler_params=pltpu.CompilerParams(vmem_limit_bytes=VMEM_LIMIT),
+        cost_estimate=pl.CostEstimate(
+            flops=CSTEPS * 70 * EDGE_ROWS * cells, bytes_accessed=4 * 100 * cells, transcendentals=0
+        ),
+        name="coast_edge",
+    )(link, block, strips, edge, keep, before)
 
 
 def basin_kernel(inside, state, depth, south, north, out, eta, hu, hv, dep):
@@ -315,46 +396,41 @@
     )(after, state, depth)
 
 
-def strips_kernel(first_row, links, state, ghosts, strips):
+def strips_kernel(count, first_row, links, state, out):
     rows, width = state.shape[1], state.shape[2]
-    count, cells = ghosts.shape[0], ghosts.shape[2]
     span = 2 * LANES
-
-    def piece(b, carry):
-        row = links[b, 0, 0] - first_row[0]
-        owned = jnp.logical_and(row >= 0, row < rows).astype(jnp.float32)
-        row = jnp.clip(row, 0, rows - 1)
-        col = links[b, 0, 1]
-        start = jnp.clip(col // LANES, 0, width // LANES - 2) * LANES
-        shift = lax.rem(span - (col - start), span)
-        for i, f in enumerate((0, 2)):
-            chunk = state[f, pl.ds(row, 1), pl.ds(pl.multiple_of(start, LANES), span)]
-            strips[pl.ds(2 * b + i, 1), :] = pltpu.roll(chunk, shift, 1)[:, :LANES] * owned
-        return carry
-
-    lax.fori_loop(0, count, piece, 0, unroll=min(count, 16))
-    at = lax.broadcasted_iota(jnp.int32, (LANES, cells), 0)
-    cols = lax.broadcasted_iota(jnp.int32, (LANES, cells), 1)
-    base = cols // 16
-    weight = ((cols % 16).astype(jnp.float32) + 0.5) / 16.0
-    mix = jnp.where(at == base, 1.0 - weight, 0.0) + jnp.where(at == base + 1, weight, 0.0)
-    values = jnp.dot(
-        strips[...], mix, precision=lax.Precision.HIGHEST, preferred_element_type=jnp.float32
-    )
-    for b in range(count):
-        ghosts[b] = values[2 * b : 2 * b + 2]
-
-
-def make_strips(first_row, links, state, cells):
-    count = links.shape[0]
+    lane = lax.broadcasted_iota(jnp.int32, (1, LANES), 1)
+
+    def pair(i, carry):
+        total = jnp.zeros((1, LANES), jnp.float32)
+        for j in range(2):
+            b = 2 * i + j
+            row = links[b, 0] - first_row[0]
+            owned = jnp.logical_and(row >= 0, row < rows).astype(jnp.float32)
+            row = jnp.clip(row, 0, rows - 1)
+            col = links[b, 1]
+            start = jnp.clip(col // LANES, 0, width // LANES - 2) * LANES
+            for f in range(2):
+                slot = (2 * j + f) * SLOT
+                shift = lax.rem(span - (col - start) + slot, span)
+                chunk = state[2 * f, pl.ds(row, 1), pl.ds(pl.multiple_of(start, LANES), span)]
+                moved = pltpu.roll(chunk, shift, 1)[:, :LANES] * owned
+                inside = jnp.logical_and(lane >= slot, lane < slot + SLOT)
+                total = jnp.where(inside, moved, total)
+        out[pl.ds(i, 1), :] = total
+        return carry
+
+    lax.fori_loop(0, count // 2, pair, 0, unroll=min(count // 2, 8))
+
+
+def make_strips(count, first_row, links, state):
     vmem = pl.BlockSpec(memory_space=pltpu.VMEM)
     smem = pl.BlockSpec(memory_space=pltpu.SMEM)
     return pl.pallas_call(
-        strips_kernel,
-        out_shape=jax.ShapeDtypeStruct((count, 2, cells), jnp.float32),
+        functools.partial(strips_kernel, count),
+        out_shape=jax.ShapeDtypeStruct((count // 2, LANES), jnp.float32),
         in_specs=[smem, smem, vmem],
         out_specs=vmem,
-        scratch_shapes=[pltpu.VMEM((2 * count, LANES), jnp.float32)],
         compiler_params=pltpu.CompilerParams(vmem_limit_bytes=VMEM_LIMIT),
         name="strips",
     )(first_row, links, state)
@@ -365,21 +441,24 @@
     devices = lax.axis_size("row")
     position = lax.axis_index("row")
 
-    sent = jnp.broadcast_to(coast_link, (devices,) + coast_link.shape)
-    links = lax.all_to_all(sent, "row", 0, 0, tiled=True)
-
-    up, down = pack_halos(sent, basin_state, basin_depth)
+    sent = jnp.pad(coast_link, ((0, SUB - 1), (0, LANES - coast_link.shape[1])))
+    links = lax.all_gather(sent, "row", axis=0, tiled=True)
+    links = links.reshape(devices, SUB, LANES)[:, 0, :2]
+
+    bulk, edge, keep = coast_bulk(coast_link, coast_depth[0], coast_flow[0])
+    first_row = (position * strip_rows).astype(jnp.int32)[None]
+    first_row, bulk = lax.optimization_barrier((first_row, bulk))
+    strips = make_strips(devices, first_row, links, basin_state)
+    all_strips = lax.all_gather(strips, "row", axis=0, tiled=False)
+
+    up, down = pack_halos(strips, basin_state, basin_depth)
     south = lax.ppermute(up, "row", [(i, i + 1) for i in range(devices - 1)])
     north = lax.ppermute(down, "row", [(i + 1, i) for i in range(devices - 1)])
-
-    first_row = (position * strip_rows).astype(jnp.int32)[None]
-    ghosts = make_strips(first_row, links, basin_state, coast_depth.shape[2])
-    ghosts = lax.all_to_all(ghosts, "row", 0, 0, tiled=True)
-
     inside = (position < devices - 1).astype(jnp.int32)[None]
     basin_out = basin_run(inside, basin_state, basin_depth, south, north)
-    coast_link, basin_out = lax.optimization_barrier((coast_link, basin_out))
-    coast_out = coast_run(coast_link, ghosts, coast_depth[0], coast_flow[0])
+    block = position.astype(jnp.int32)[None]
+    block, basin_out = lax.optimization_barrier((block, basin_out))
+    coast_out = coast_edge(strip_rows, coast_link, block, all_strips, edge, keep, bulk)
     return (basin_out, coast_out[None])
 
 

time: 48.3 us -> 71.2 us (1.47)
  blocking collectives: 0 us -> 42.8 us
  starting transfers between devices: 16.6 us -> 3.56 us
  waiting for transfers between devices: 9.65 us -> 0.01 us
  Pallas kernels: 17.8 us -> 21.1 us
    all_gather x0 -> x2, blocking collectives: none -> 42.8 us  [the longest x1 23.2 us: local(): links = lax.all_gather(sent, 'row', axis=0, tiled=True)]
    all_to_all x2 -> x0, starting transfers between devices: 12.8 us -> none  [the longest x1 9.3 us: local(): links = lax.all_to_all(sent, 'row', 0, 0, tiled=True)]
    all_to_all x2 -> x0, waiting for transfers between devices: 9.65 us -> none  [the longest x1 6.33 us: local(): links = lax.all_to_all(sent, 'row', 0, 0, tiled=True)]
    pallas_call x2 -> x3, Pallas kernels: 14.5 us -> 17.8 us  [the longest x1 13.1 us: coast_bulk(): pl.pallas_call(coast_kernel, out_shape=(jax.ShapeDtypeStruct((3, cells, c...]
    unnamed x14 -> x11, local copies, waits for them, and re-layouts: 2.57 us -> 2.73 us
  transfers between devices with their start and end apart: 4 -> 2, of which waited for: 2 -> 0; matrix products, arithmetic and copies ran while one was open for 0% -> 0% of each run, Pallas kernels for 10% -> 0%
where the time goes in v6:
time: 71.2 us; the launch traced here: 70.9 us
  blocking collectives  42.8 us (60%)
  Pallas kernels  21.1 us (30%)
  starting transfers between devices  3.56 us (5%)
  local copies, waits for them, and re-layouts  2.83 us (4%)
    all_gather x1, blocking collectives, local(): links = lax.all_gather(sent, 'row', axis=0, tiled=True)  23.2 us
    all_gather x1, blocking collectives, local(): all_strips = lax.all_gather(strips, 'row', axis=0, tiled=False)  19.5 us
    pallas_call x1, Pallas kernels, coast_bulk(): pl.pallas_call(coast_kernel, out_shape=(jax.ShapeDtypeStruct((3, cells, c...  13.1 us
    pallas_call x1, Pallas kernels, coast_edge(): pl.pallas_call(functools.partial(edge_kernel, strip_rows), out_shape=jax....  3.67 us
    pallas_call x1, Pallas kernels, basin_run(): pl.pallas_call(basin_kernel, out_shape=jax.ShapeDtypeStruct(state.shape,...  3.21 us
    unnamed x11, local copies, waits for them, and re-layouts  2.73 us
    ppermute x1, starting transfers between devices, local(): south = lax.ppermute(up, 'row', [(i, i + 1) for i in range(devices - 1)])  2.26 us
  transfers between devices with their start and end apart: 2, of which 0 were waited for; matrix products, arithmetic and copies ran while one was open for 0% of the time, Pallas kernels for 0%

profile of v6, /device:TPU:0, one launch (start us, length us, event | category | flops | bytes accessed | tf_op | source)
XLA Modules:
  0.0 70.9 jit_solution(11798990740438828469)
XLA Ops:
  0.6 0.0 copy-start.4
  0.6 0.6 copy-done.4
  1.3 0.0 copy-start.1
  1.3 1.0 %copy-done.1 = f32[1,2,256,256]{3,2,1,0:T(8,128)S(1)} copy-done((f32[1,2,256,256]{3,2,1,0:T(8,128)S(1)}, f32[1,2,256,256]{3,2,1,0:T(8,128)}, u32[]{:S(2)}) %copy-start.1) | copy-done | bytes 524312
  2.3 0.0 copy-start.3
  2.3 0.9 %copy-done.3 = f32[1,256,256]{2,1,0:T(8,128)S(1)} copy-done((f32[1,256,256]{2,1,0:T(8,128)S(1)}, f32[1,256,256]{2,1,0:T(8,128)}, u32[]{:S(2)}) %copy-start.3) | copy-done | bytes 262168
  3.3 0.0 copy-start
  3.3 13.1 %coast_bulk.1 = (f32[3,256,256]{2,1,0:T(8,128)}, f32[3,2,3,8,128]{4,3,2,1,0:T(8,128)S(1)}, f32[16,256]{1,0:T(8,128)S(1)}) custom-call(s32[1,3]{1,0:T(1,128)S(1)} %copy-done.4, f32[256,256]{1,0:T(8,128)S(1)} %bitcast.11, f32[2,256,256]{2,1,0:T(8,128)S(1)} %bitcast.9), custom_call_target="tpu_custom_call" | custom-call | flops 45875200 | bytes 1572864 | tf_op jit(solution)/shard_map/coast_bulk/pallas_call | solution.py:229
  16.4 23.2 %all_gather.9 = s32[128,128]{1,0:T(8,128)S(1)} all-gather(s32[8,128]{1,0:T(8,128)S(1)} %pad.4), channel_id=1, replica_groups=mesh['scen'=2,'row'=16] {'row'}, dimensions={0}, use_global_device_ids=true | all-gather | bytes 69632 | tf_op jit(solution)/shard_map/all_gather | solution.py:445
  39.7 0.1 copy.10
  39.7 0.1 copy.9.links
  39.8 0.0 copy-done
  39.8 0.0 copy-start.2
  39.8 1.0 %strips.1.after = f32[8,128]{1,0:T(8,128)S(1)} custom-call(s32[1]{0:T(128)} %bitcast.2.first_row, s32[16,2]{1,0:T(8,128)S(1)} %copy.9.links, f32[3,16,2048]{2,1,0:T(8,128)S(1)} %copy-done), custom_call_target="tpu_custom_call" | custom-call | tf_op jit(solution)/shard_map/strips/pallas_call | solution.py:429
  40.9 0.0 copy-done.2
  40.9 2.3 %collective-permute-start = (f32[4,8,2048]{2,1,0:T(8,128)S(1)}, f32[4,8,2048]{2,1,0:T(8,128)S(1)}, u32[]{:S(2)}, u32[]{:S(2)}) collective-permute-start(f32[4,8,2048]{2,1,0:T(8,128)S(1)} %get-tuple-element.13), channel_id=1, source_target_pairs={{0,1},{1,2},{2,3},{3,4},{4,5},{5,6},{6,7},{7,8},{8,9},{9,10},{10,1... | collective-permute-start | bytes 786440 | tf_op jit(solution)/shard_map/ppermute | solution.py:455
  43.2 1.3 %collective-permute-start.1 = (f32[4,8,2048]{2,1,0:T(8,128)S(1)}, f32[4,8,2048]{2,1,0:T(8,128)S(1)}, u32[]{:S(2)}, u32[]{:S(2)}) collective-permute-start(f32[4,8,2048]{2,1,0:T(8,128)S(1)} %get-tuple-element.14), channel_id=1, source_target_pairs={{1,0},{2,1},{3,2},{4,3},{5,4},{6,5},{7,6},{8,7},{9,8},{10,9},{11,1... | collective-permute-start | bytes 786440 | tf_op jit(solution)/shard_map/ppermute | solution.py:456
  44.5 19.5 %all-gather = f32[128,128]{1,0:T(8,128)S(1)} all-gather(f32[8,128]{1,0:T(8,128)S(1)} %strips.1.after), channel_id=2, replica_groups=mesh['scen'=2,'row'=16] {'row'}, dimensions={0}, use_global_device_ids=true | all-gather | bytes 69632 | tf_op jit(solution)/shard_map/all_gather | solution.py:452
  64.0 0.0 collective-permute-done.south
  64.0 0.0 collective-permute-done.1.north
  64.0 3.2 %basin_steps.1 = f32[3,16,2048]{2,1,0:T(8,128)} custom-call(s32[1]{0:T(128)} %bitcast.1.inside, f32[3,16,2048]{2,1,0:T(8,128)S(1)} %copy-done, f32[16,2048]{1,0:T(8,128)S(1)} %copy-done.2, f32[4,8,2048]{2,1,0:T(8,128)S(1)} %collective-permute-done.south, f32[4,8,2048]{2,1,0:T(8,128)S(1)} %collective-permute-done.1.north), custom_call_target="tpu_custom_call" | custom-call | flops 8388608 | bytes 1441792 | tf_op jit(solution)/shard_map/basin_steps/pallas_call | solution.py:364
  67.2 3.7 %coast_edge.1 = f32[3,256,256]{2,1,0:T(8,128)} custom-call(s32[1,3]{1,0:T(1,128)S(1)} %copy-done.4, s32[1]{0:T(128)} %bitcast.block, f32[16,8,128]{2,1,0:T(8,128)S(1)} %bitcast.10, f32[3,2,3,8,128]{4,3,2,1,0:T(8,128)S(1)} %get-tuple-element.17.edge, f32[16,256]{1,0:T(8,128)S(1)} %get-tuple-element.18.keep, ...), custom_call_target="tpu_custom_call", output_to_operand_aliasing={{}: (5, {})} | custom-call | flops 4300800 | bytes 102400 | tf_op jit(solution)/shard_map/coast_edge/pallas_call | solution.py:296
  (3 shorter events, 0.0 us)
Async XLA Ops:
  0.6 0.7 copy-start.4
  1.3 1.0 %copy-start.1 = (f32[1,2,256,256]{3,2,1,0:T(8,128)S(1)}, f32[1,2,256,256]{3,2,1,0:T(8,128)}, u32[]{:S(2)}) copy-start(f32[1,2,256,256]{3,2,1,0:T(8,128)} %param.8) | copy-start | bytes 1572868
  2.3 0.9 %copy-start.3 = (f32[1,256,256]{2,1,0:T(8,128)S(1)}, f32[1,256,256]{2,1,0:T(8,128)}, u32[]{:S(2)}) copy-start(f32[1,256,256]{2,1,0:T(8,128)} %param.7) | copy-start | bytes 786436
  3.3 36.5 %copy-start = (f32[3,16,2048]{2,1,0:T(8,128)S(1)}, f32[3,16,2048]{2,1,0:T(8,128)}, u32[]{:S(2)}) copy-start(f32[3,16,2048]{2,1,0:T(8,128)} %state.5) | copy-start | bytes 1179652
  39.8 1.0 %copy-start.2 = (f32[16,2048]{1,0:T(8,128)S(1)}, f32[16,2048]{1,0:T(8,128)}, u32[]{:S(2)}) copy-start(f32[16,2048]{1,0:T(8,128)} %depth.3) | copy-start | bytes 393220
  40.9 23.1 %collective-permute-start = (f32[4,8,2048]{2,1,0:T(8,128)S(1)}, f32[4,8,2048]{2,1,0:T(8,128)S(1)}, u32[]{:S(2)}, u32[]{:S(2)}) collective-permute-start(f32[4,8,2048]{2,1,0:T(8,128)S(1)} %get-tuple-element.13), channel_id=1, source_target_pairs={{0,1},{1,2},{2,3},{3,4},{4,5},{5,6},{6,7},{7,8},{8,9},{9,10},{10,1... | collective-permute-start | bytes 786440 | tf_op jit(solution)/shard_map/ppermute | solution.py:455
  43.2 20.8 %collective-permute-start.1 = (f32[4,8,2048]{2,1,0:T(8,128)S(1)}, f32[4,8,2048]{2,1,0:T(8,128)S(1)}, u32[]{:S(2)}, u32[]{:S(2)}) collective-permute-start(f32[4,8,2048]{2,1,0:T(8,128)S(1)} %get-tuple-element.14), channel_id=1, source_target_pairs={{1,0},{2,1},{3,2},{4,3},{5,4},{6,5},{7,6},{8,7},{9,8},{10,9},{11,1... | collective-permute-start | bytes 786440 | tf_op jit(solution)/shard_map/ppermute | solution.py:456

commit v7 on v5

--- a/solution.py
+++ b/solution.py
@@ -134,7 +134,7 @@
     lax.fori_loop(0, steps, step, 0)
 
 
-GROUP = 8
+GROUP = 16
 UNITS = (DEPTH_UNIT, FLOW_UNIT, FLOW_UNIT)
 VMEM_LIMIT = 12 * 1024 * 1024
 HALF = LANES // 2
@@ -233,19 +233,24 @@
     )(link, ghosts, depth, flow)
 
 
-def basin_kernel(inside, state, depth, south, north, out, eta, hu, hv, dep):
-    rows = state.shape[1]
-    width = state.shape[2]
+def basin_kernel(own, pair, edge, out, eta, hu, hv, dep):
+    rows, width = own.shape[1], own.shape[2]
     total = rows + 2 * HALO
     chunks = width // LANES
+    position = lax.axis_index("row")
+    odd = position % 2
+    north_inside = (position < lax.axis_size("row") - 1).astype(jnp.float32)
+    pair_from = pl.multiple_of(odd * (rows - HALO), HALO)
+    pair_at = pl.multiple_of((1 - odd) * (HALO + rows), HALO)
+    edge_at = pl.multiple_of(odd * (HALO + rows), HALO)
     for ref, field, unit in ((eta, 0, 1.0), (hu, 1, 0.5), (hv, 2, 0.5), (dep, 3, 0.25)):
-        ref[:HALO] = south[field] * unit
-        ref[HALO : HALO + rows] = (depth[...] if field == 3 else state[field]) * unit
-        ref[HALO + rows :] = north[field] * unit
+        ref[HALO : HALO + rows] = own[field] * unit
+        ref[pl.ds(pair_at, HALO)] = pair[field, pl.ds(pair_from, HALO)] * unit
+        ref[pl.ds(edge_at, HALO)] = edge[field] * unit
     lane = lax.broadcasted_iota(jnp.int32, (total, LANES), 1)
     first, last = lane == 0, lane == LANES - 1
     row = lax.broadcasted_iota(jnp.int32, (total, LANES), 0)
-    kept = jnp.where(row < HALO + rows, 1.0, inside[0].astype(jnp.float32))
+    kept = jnp.where(row < HALO + rows, 1.0, north_inside)
 
     def step(_, carry):
         prev_west = jnp.zeros((total, LANES), jnp.float32)
@@ -276,14 +281,14 @@
     out[2] = hv[own] * 2.0
 
 
-def basin_run(inside, state, depth, south, north):
-    rows, width = depth.shape
+def basin_run(own, pair, edge):
+    rows, width = own.shape[1:]
     total = rows + 2 * HALO
     vmem = pl.BlockSpec(memory_space=pltpu.VMEM)
     return pl.pallas_call(
         basin_kernel,
-        out_shape=jax.ShapeDtypeStruct(state.shape, jnp.float32),
-        in_specs=[pl.BlockSpec(memory_space=pltpu.SMEM), vmem, vmem, vmem, vmem],
+        out_shape=jax.ShapeDtypeStruct((3, rows, width), jnp.float32),
+        in_specs=[vmem, vmem, vmem],
         out_specs=vmem,
         scratch_shapes=[pltpu.VMEM((total, width), jnp.float32)] * 4,
         compiler_params=pltpu.CompilerParams(vmem_limit_bytes=VMEM_LIMIT),
@@ -291,48 +296,69 @@
             flops=BSTEPS * 16 * total * width, bytes_accessed=4 * 11 * rows * width, transcendentals=0
         ),
         name="basin_steps",
-    )(inside, state, depth, south, north)
-
-
-def pack_kernel(after, state, depth, up, down):
+    )(own, pair, edge)
+
+
+def pack_kernel(link, state, depth, own, edge, sent, sems):
     rows = depth.shape[0]
-    for f in range(4):
-        source = depth if f == 3 else state.at[f]
-        up[f] = source[rows - HALO :]
-        down[f] = source[:HALO]
-
-
-def pack_halos(after, state, depth):
+    odd = lax.axis_index("row") % 2
+    edge_rows = pl.ds(pl.multiple_of(odd * (rows - HALO), HALO), HALO)
+    copies = [
+        pltpu.make_async_copy(state, own.at[:3], sems.at[0]),
+        pltpu.make_async_copy(depth, own.at[3], sems.at[1]),
+        pltpu.make_async_copy(state.at[:, edge_rows], edge.at[:3], sems.at[2]),
+        pltpu.make_async_copy(depth.at[edge_rows], edge.at[3], sems.at[3]),
+    ]
+    for copy in copies:
+        copy.start()
+    for b in range(sent.shape[0]):
+        sent[b] = link[...]
+    for copy in copies:
+        copy.wait()
+
+
+def pack(link, state, depth, peers):
     vmem = pl.BlockSpec(memory_space=pltpu.VMEM)
-    halo = jax.ShapeDtypeStruct((4, HALO, depth.shape[1]), jnp.float32)
+    hbm = pl.BlockSpec(memory_space=pltpu.HBM)
+    rows, width = depth.shape
     return pl.pallas_call(
         pack_kernel,
-        out_shape=(halo, halo),
-        in_specs=[pl.BlockSpec(memory_space=pl.ANY), vmem, vmem],
-        out_specs=(vmem, vmem),
+        out_shape=(
+            jax.ShapeDtypeStruct((4, rows, width), jnp.float32),
+            jax.ShapeDtypeStruct((4, HALO, width), jnp.float32),
+            jax.ShapeDtypeStruct((peers,) + link.shape, link.dtype),
+        ),
+        in_specs=[vmem, hbm, hbm],
+        out_specs=(vmem, vmem, vmem),
+        scratch_shapes=[pltpu.SemaphoreType.DMA((4,))],
         compiler_params=pltpu.CompilerParams(vmem_limit_bytes=VMEM_LIMIT),
-        name="pack_halos",
-    )(after, state, depth)
-
-
-def strips_kernel(first_row, links, state, ghosts, strips):
-    rows, width = state.shape[1], state.shape[2]
+        name="pack",
+    )(link, state, depth)
+
+
+def strips_kernel(links, own, pair, ghosts, strips):
+    rows, width = own.shape[1], own.shape[2]
     count, cells = ghosts.shape[0], ghosts.shape[2]
     span = 2 * LANES
+    position = lax.axis_index("row")
+    tops = (position * rows, (position + 1 - 2 * (position % 2)) * rows)
 
     def piece(b, carry):
-        row = links[b, 0, 0] - first_row[0]
-        owned = jnp.logical_and(row >= 0, row < rows).astype(jnp.float32)
-        row = jnp.clip(row, 0, rows - 1)
         col = links[b, 0, 1]
         start = jnp.clip(col // LANES, 0, width // LANES - 2) * LANES
         shift = lax.rem(span - (col - start), span)
+        at = pl.ds(pl.multiple_of(start, LANES), span)
         for i, f in enumerate((0, 2)):
-            chunk = state[f, pl.ds(row, 1), pl.ds(pl.multiple_of(start, LANES), span)]
-            strips[pl.ds(2 * b + i, 1), :] = pltpu.roll(chunk, shift, 1)[:, :LANES] * owned
-        return carry
-
-    lax.fori_loop(0, count, piece, 0, unroll=min(count, 16))
+            chunk = None
+            for source, top in zip((own, pair), tops):
+                row = links[b, 0, 0] - top
+                owned = jnp.logical_and(row >= 0, row < rows).astype(jnp.float32)
+                part = source[f, pl.ds(jnp.clip(row, 0, rows - 1), 1), at] * owned
+                chunk = part if chunk is None else chunk + part
+            strips[pl.ds(2 * b + i, 1), :] = pltpu.roll(chunk, shift, 1)[:, :LANES]
+        return carry
+
+    lax.fori_loop(0, count, piece, 0, unroll=8)
     at = lax.broadcasted_iota(jnp.int32, (LANES, cells), 0)
     cols = lax.broadcasted_iota(jnp.int32, (LANES, cells), 1)
     base = cols // 16
@@ -345,40 +371,37 @@
         ghosts[b] = values[2 * b : 2 * b + 2]
 
 
-def make_strips(first_row, links, state, cells):
+def make_strips(links, own, pair, cells):
     count = links.shape[0]
     vmem = pl.BlockSpec(memory_space=pltpu.VMEM)
     smem = pl.BlockSpec(memory_space=pltpu.SMEM)
     return pl.pallas_call(
         strips_kernel,
         out_shape=jax.ShapeDtypeStruct((count, 2, cells), jnp.float32),
-        in_specs=[smem, smem, vmem],
+        in_specs=[smem, vmem, vmem],
         out_specs=vmem,
         scratch_shapes=[pltpu.VMEM((2 * count, LANES), jnp.float32)],
         compiler_params=pltpu.CompilerParams(vmem_limit_bytes=VMEM_LIMIT),
         name="strips",
-    )(first_row, links, state)
+    )(links, own, pair)
 
 
 def local(basin_state, basin_depth, coast_depth, coast_flow, coast_link):
-    strip_rows = basin_state.shape[1]
     devices = lax.axis_size("row")
-    position = lax.axis_index("row")
-
-    sent = jnp.broadcast_to(coast_link, (devices,) + coast_link.shape)
-    links = lax.all_to_all(sent, "row", 0, 0, tiled=True)
-
-    up, down = pack_halos(sent, basin_state, basin_depth)
-    south = lax.ppermute(up, "row", [(i, i + 1) for i in range(devices - 1)])
-    north = lax.ppermute(down, "row", [(i + 1, i) for i in range(devices - 1)])
-
-    first_row = (position * strip_rows).astype(jnp.int32)[None]
-    ghosts = make_strips(first_row, links, basin_state, coast_depth.shape[2])
-    ghosts = lax.all_to_all(ghosts, "row", 0, 0, tiled=True)
-
-    inside = (position < devices - 1).astype(jnp.int32)[None]
-    basin_out = basin_run(inside, basin_state, basin_depth, south, north)
-    coast_link, basin_out = lax.optimization_barrier((coast_link, basin_out))
+    parity = [list(range(p, devices, 2)) for p in range(2)]
+    swap = [(i, i ^ 1) for i in range(devices)]
+    across = [(i, i + 1) for i in range(1, devices - 1, 2)]
+    across += [(j, i) for i, j in across]
+
+    own, edge, sent = pack(coast_link, basin_state, basin_depth, devices // 2)
+    pair = lax.ppermute(own, "row", swap)
+    edge = lax.ppermute(edge, "row", across)
+    links = lax.all_to_all(sent, "row", 0, 0, axis_index_groups=parity, tiled=True)
+
+    basin_out = basin_run(own, pair, edge)
+    own, basin_out = lax.optimization_barrier((own, basin_out))
+    ghosts = make_strips(links, own, pair, coast_depth.shape[2])
+    ghosts = lax.all_to_all(ghosts, "row", 0, 0, axis_index_groups=parity, tiled=True)
     coast_out = coast_run(coast_link, ghosts, coast_depth[0], coast_flow[0])
     return (basin_out, coast_out[None])
 

time: 48.3 us -> 43.6 us (0.903)
  the two profiles are of different devices: /device:TPU:0 before, /device:TPU:1 now
where the time goes in v7:
time: 43.6 us; the launch traced here: 43.3 us
  Pallas kernels  17.2 us (39%)
  blocking collectives  10.9 us (25%)
  starting transfers between devices  9.23 us (21%)
  local copies, waits for them, and re-layouts  3.2 us (7%)
  waiting for transfers between devices  2.02 us (5%)
  between operations  0.66 us (2%)
    pallas_call x1, Pallas kernels, coast_run(): pl.pallas_call(coast_kernel, out_shape=jax.ShapeDtypeStruct((3, cells, ce...  11.9 us
    all_to_all x1, blocking collectives, local(): lax.all_to_all(ghosts, 'row', 0, 0, axis_index_groups=parity, tiled=True)  10.9 us
    all_to_all x1, starting transfers between devices, local(): lax.all_to_all(sent, 'row', 0, 0, axis_index_groups=parity, tiled=True)  4.61 us
    ppermute x1, starting transfers between devices, local(): edge = lax.ppermute(edge, 'row', across)  4.49 us
    pallas_call x1, Pallas kernels, basin_run(): pl.pallas_call(basin_kernel, out_shape=jax.ShapeDtypeStruct((3, rows, wid...  3.21 us
    unnamed x12, local copies, waits for them, and re-layouts  3.2 us
    ppermute x1, waiting for transfers between devices, local(): edge = lax.ppermute(edge, 'row', across)  1.49 us
    pallas_call x1, Pallas kernels, pack(): pl.pallas_call(pack_kernel, out_shape=(jax.ShapeDtypeStruct((4, rows, wid...  1.16 us
  transfers between devices with their start and end apart: 3, of which 2 were waited for; matrix products, arithmetic and copies ran while one was open for 0% of the time, Pallas kernels for 7%

profile of v7, /device:TPU:1, one launch (start us, length us, event | category | flops | bytes accessed | tf_op | source)
XLA Modules:
  0.0 43.3 jit_solution(2655754992803683890)
XLA Ops:
  0.6 0.0 copy-start.1
  0.6 1.0 %copy-done.1 = f32[3,16,2048]{2,1,0:T(8,128)S(1)} copy-done((f32[3,16,2048]{2,1,0:T(8,128)S(1)}, f32[3,16,2048]{2,1,0:T(8,128)}, u32[]{:S(2)}) %copy-start.1) | copy-done | bytes 393240
  1.6 0.0 copy-start.3
  1.6 0.9 %copy-done.3 = f32[16,2048]{1,0:T(8,128)S(1)} copy-done((f32[16,2048]{1,0:T(8,128)S(1)}, f32[16,2048]{1,0:T(8,128)}, u32[]{:S(2)}) %copy-start.3) | copy-done | bytes 131096
  2.5 0.0 copy-start.4
  2.5 0.7 %copy-done.4 = s32[1,3]{1,0:T(1,128)S(1)} copy-done((s32[1,3]{1,0:T(1,128)S(1)}, s32[1,3]{1,0:T(1,128)}, u32[]{:S(2)}) %copy-start.4) | copy-done | bytes 36
  3.2 1.2 %pack.1 = (f32[4,16,2048]{2,1,0:T(8,128)S(1)}, f32[4,8,2048]{2,1,0:T(8,128)S(1)}, s32[8,1,3]{2,1,0:T(1,128)}) custom-call(s32[1,3]{1,0:T(1,128)S(1)} %copy-done.4, f32[3,16,2048]{2,1,0:T(8,128)S(1)} %copy-done.1, f32[16,2048]{1,0:T(8,128)S(1)} %copy-done.3), custom_call_target="tpu_custom_call" | custom-call | tf_op jit(solution)/shard_map/pack/pallas_call | solution.py:324
  4.3 0.1 collective-permute-start
  4.5 4.5 %collective-permute-start.1 = (f32[4,8,2048]{2,1,0:T(8,128)S(1)}, f32[4,8,2048]{2,1,0:T(8,128)S(1)}, u32[]{:S(2)}, u32[]{:S(2)}) collective-permute-start(f32[4,8,2048]{2,1,0:T(8,128)S(1)} %get-tuple-element.8), channel_id=1, source_target_pairs={{1,2},{3,4},{5,6},{7,8},{9,10},{11,12},{13,14},{2,1},{4,3},{6,5},{... | collective-permute-start | bytes 786440 | tf_op jit(solution)/shard_map/ppermute | solution.py:398
  9.0 4.6 %all-to-all-start = ((s32[8,1,3]{2,1,0:T(1,128)}), s32[8,1,3]{2,1,0:T(1,128)S(1)}, u32[]{:S(2)}, u32[]{:S(2)}) async-start(s32[8,1,3]{2,1,0:T(1,128)} %get-tuple-element.10), calls=%async_computation | async-start | bytes 8192 | tf_op jit(solution)/shard_map/all_to_all | solution.py:399
  13.6 1.5 %collective-permute-done.1.edge = f32[4,8,2048]{2,1,0:T(8,128)S(1)} collective-permute-done((f32[4,8,2048]{2,1,0:T(8,128)S(1)}, f32[4,8,2048]{2,1,0:T(8,128)S(1)}, u32[]{:S(2)}, u32[]{:S(2)}) %collective-permute-start.1) | collective-permute-done | bytes 262176 | tf_op jit(solution)/shard_map/ppermute | solution.py:398
  15.1 0.0 collective-permute-done.pair
  15.1 3.2 %basin_steps.1 = f32[3,16,2048]{2,1,0:T(8,128)} custom-call(f32[4,16,2048]{2,1,0:T(8,128)S(1)} %get-tuple-element.11.own, f32[4,16,2048]{2,1,0:T(8,128)S(1)} %collective-permute-done.pair, f32[4,8,2048]{2,1,0:T(8,128)S(1)} %collective-permute-done.1.edge), custom_call_target="tpu_custom_call" | custom-call | flops 8388608 | bytes 1441792 | tf_op jit(solution)/shard_map/basin_steps/pallas_call | solution.py:288
  18.3 0.0 copy-start
  18.3 0.0 copy-start.2
  18.3 0.5 %all-to-all-done.links = s32[8,1,3]{2,1,0:T(1,128)S(1)} async-done(((s32[8,1,3]{2,1,0:T(1,128)}), s32[8,1,3]{2,1,0:T(1,128)S(1)}, u32[]{:S(2)}, u32[]{:S(2)}) %all-to-all-start) | async-done | bytes 128 | tf_op jit(solution)/shard_map/all_to_all | solution.py:399
  18.8 1.0 %strips.1 = f32[8,2,256]{2,1,0:T(2,128)S(1)} custom-call(s32[8,1,3]{2,1,0:T(1,128)S(1)} %all-to-all-done.links, f32[4,16,2048]{2,1,0:T(8,128)S(1)} %get-tuple-element.11.own, f32[4,16,2048]{2,1,0:T(8,128)S(1)} %collective-permute-done.pair), custom_call_target="tpu_custom_call" | custom-call | tf_op jit(solution)/shard_map/strips/pallas_call | solution.py:378
  19.8 10.9 %all_to_all.10.ghosts = f32[8,2,256]{2,1,0:T(2,128)S(1)} all-to-all(f32[8,2,256]{2,1,0:T(2,128)S(1)} %strips.1), channel_id=1, replica_groups={{0,2,4,6,8,10,12,14},{1,3,5,7,9,11,13,15},{16,18,20,22,24,26,28,30},{17..., dimensions={0} | all-to-all | bytes 32768 | tf_op jit(solution)/shard_map/all_to_all | solution.py:404
  30.8 0.0 copy-start.5
  30.8 0.0 copy-done
  30.8 0.0 copy-done.2
  30.8 0.6 %copy-done.5 = s32[1,3]{1,0:T(1,128)S(1)} copy-done((s32[1,3]{1,0:T(1,128)S(1)}, s32[1,3]{1,0:T(1,128)}, u32[]{:S(2)}) %copy-start.5) | copy-done | bytes 36
  31.4 11.9 %coast_steps.1 = f32[3,256,256]{2,1,0:T(8,128)} custom-call(s32[1,3]{1,0:T(1,128)S(1)} %copy-done.5, f32[8,2,256]{2,1,0:T(2,128)S(1)} %all_to_all.10.ghosts, f32[256,256]{1,0:T(8,128)S(1)} %bitcast.4, f32[2,256,256]{2,1,0:T(8,128)S(1)} %bitcast.3), custom_call_target="tpu_custom_call" | custom-call | flops 45875200 | bytes 1572864 | tf_op jit(solution)/shard_map/coast_steps/pallas_call | solution.py:219
Async XLA Ops:
  0.6 1.0 %copy-start.1 = (f32[3,16,2048]{2,1,0:T(8,128)S(1)}, f32[3,16,2048]{2,1,0:T(8,128)}, u32[]{:S(2)}) copy-start(f32[3,16,2048]{2,1,0:T(8,128)} %state.1) | copy-start | bytes 1179652
  1.6 0.9 %copy-start.3 = (f32[16,2048]{1,0:T(8,128)S(1)}, f32[16,2048]{1,0:T(8,128)}, u32[]{:S(2)}) copy-start(f32[16,2048]{1,0:T(8,128)} %depth.1) | copy-start | bytes 393220
  2.5 0.7 %copy-start.4 = (s32[1,3]{1,0:T(1,128)S(1)}, s32[1,3]{1,0:T(1,128)}, u32[]{:S(2)}) copy-start(s32[1,3]{1,0:T(1,128)} %link.3) | copy-start | bytes 40
  4.3 10.7 %collective-permute-start = (f32[4,16,2048]{2,1,0:T(8,128)S(1)}, f32[4,16,2048]{2,1,0:T(8,128)S(1)}, u32[]{:S(2)}, u32[]{:S(2)}) collective-permute-start(f32[4,16,2048]{2,1,0:T(8,128)S(1)} %get-tuple-element.11.own), channel_id=1, source_target_pairs={{0,1},{1,0},{2,3},{3,2},{4,5},{5,4},{6,7},{7,6},{8,9},{9,8},{10,11... | collective-permute-start | bytes 1572872 | tf_op jit(solution)/shard_map/ppermute | solution.py:397
  4.5 10.6 %collective-permute-start.1 = (f32[4,8,2048]{2,1,0:T(8,128)S(1)}, f32[4,8,2048]{2,1,0:T(8,128)S(1)}, u32[]{:S(2)}, u32[]{:S(2)}) collective-permute-start(f32[4,8,2048]{2,1,0:T(8,128)S(1)} %get-tuple-element.8), channel_id=1, source_target_pairs={{1,2},{3,4},{5,6},{7,8},{9,10},{11,12},{13,14},{2,1},{4,3},{6,5},{... | collective-permute-start | bytes 786440 | tf_op jit(solution)/shard_map/ppermute | solution.py:398
  9.0 9.8 %all-to-all-start = ((s32[8,1,3]{2,1,0:T(1,128)}), s32[8,1,3]{2,1,0:T(1,128)S(1)}, u32[]{:S(2)}, u32[]{:S(2)}) async-start(s32[8,1,3]{2,1,0:T(1,128)} %get-tuple-element.10), calls=%async_computation | async-start | bytes 8192 | tf_op jit(solution)/shard_map/all_to_all | solution.py:399
  18.3 12.5 %copy-start = (f32[1,2,256,256]{3,2,1,0:T(8,128)S(1)}, f32[1,2,256,256]{3,2,1,0:T(8,128)}, u32[]{:S(2)}) copy-start(f32[1,2,256,256]{3,2,1,0:T(8,128)} %param.8) | copy-start | bytes 1572868
  18.3 12.5 %copy-start.2 = (f32[1,256,256]{2,1,0:T(8,128)S(1)}, f32[1,256,256]{2,1,0:T(8,128)}, u32[]{:S(2)}) copy-start(f32[1,256,256]{2,1,0:T(8,128)} %param.7) | copy-start | bytes 786436
  30.8 0.7 %copy-start.5 = (s32[1,3]{1,0:T(1,128)S(1)}, s32[1,3]{1,0:T(1,128)}, u32[]{:S(2)}) copy-start(s32[1,3]{1,0:T(1,128)} %link.3) | copy-start | bytes 40

commit v8 on v7

--- a/solution.py
+++ b/solution.py
@@ -79,6 +79,7 @@
     first, last = lane == 0, lane == LANES - 1
     top, bottom = sub == 0, sub == SUB - 1
     zero = jnp.zeros((SUB, LANES), jnp.float32)
+    trips = rows // group
 
     def load(k):
         return [cell_terms([state[f, half, 1 + k] for f in range(3)]) for half in range(2)]
@@ -87,6 +88,9 @@
         for half in range(2):
             for f in range(3):
                 state[f, half, 1 + k] = both[half][f]
+
+    def added(xs, ys):
+        return [[x + y for x, y in zip(*pair)] for pair in zip(xs, ys)]
 
     def faces_of(cells):
         return [
@@ -100,38 +104,34 @@
             out[name] = [jnp.where(top, h, down(t)) for h, t in zip(head[name], tail[name])]
         return out
 
-    def step(_, carry):
-        tails, heads = load(rows - 1), load(0)
-        above = [wrapped(t, h) for t, h in zip(tails, ghost)]
-        start = [y_face(a, b) for a, b in zip(above, heads)]
-
-        def rows_from(begin, prev, acc):
-            for k in range(group):
-                cur = load(begin + k)
-                face = [y_face(a, b) for a, b in zip(prev, cur)]
-                store(begin + k - 1, [[x + g for x, g in zip(*pair)] for pair in zip(acc, face)])
-                acc = x_part(cur[0], cur[1], first, last)
-                acc = [[x - g for x, g in zip(*pair)] for pair in zip(acc, face)]
-                prev = faces_of(cur)
-            return prev, acc
-
-        prev, acc = lax.fori_loop(
-            0,
-            rows // group,
-            lambda i, c: rows_from(i * group, *c),
-            (above, [[zero] * 3 for _ in range(2)]),
-        )
+    def trip(j, carry):
+        prev, acc, over = carry
+        i = lax.rem(j, trips)
+        opening = jnp.broadcast_to(i, (SUB, LANES)) == 0
+        above = [wrapped(t, g) for t, g in zip(load(rows - 1), ghost)]
+        prev = jax.tree.map(lambda a, p: jnp.where(opening, a, p), above, prev)
+        for k in range(group):
+            cur = load(i * group + k)
+            face = [y_face(a, b) for a, b in zip(prev, cur)]
+            if k == 0:
+                over = [
+                    [jnp.where(opening, pltpu.roll(g, SUB - 1, 0), o) for g, o in zip(*pair)]
+                    for pair in zip(face, over)
+                ]
+            store(i * group + k - 1, added(acc, face))
+            acc = x_part(cur[0], cur[1], first, last)
+            acc = [[x - g for x, g in zip(*pair)] for pair in zip(acc, face)]
+            prev = faces_of(cur)
         end = [
-            [
-                jnp.where(bottom, -(f + f), pltpu.roll(g, SUB - 1, 0))
-                for f, g in zip(cell["fy"], gs)
-            ]
-            for cell, gs in zip(prev, start)
+            [jnp.where(bottom, -2.0 * f, o) for f, o in zip(cell["fy"], os)]
+            for cell, os in zip(prev, over)
         ]
-        store(rows - 1, [[x + g for x, g in zip(*pair)] for pair in zip(acc, end)])
-        return carry
-
-    lax.fori_loop(0, steps, step, 0)
+        store(jnp.where(i == trips - 1, rows - 1, -1), added(acc, end))
+        return prev, acc, over
+
+    blank = {"u": [zero] * 3, "fy": [zero] * 3, "sy": zero}
+    nothing = [[zero] * 3 for _ in range(2)]
+    lax.fori_loop(0, steps * trips, trip, ([blank, blank], nothing, nothing))
 
 
 GROUP = 16
@@ -162,18 +162,24 @@
     return pick(w, half + HALF * is_odd), pick(e, half + HALF * (1 - is_odd))
 
 
-def coast_kernel(link, ghosts, depth, flow, out, state, tmp):
+def coast_kernel(links, ghosts, depth, flow, out, state, tmp):
     rows = depth.shape[0] // SUB
     halves = (slice(0, LANES), slice(LANES, 2 * LANES))
     tall = 32
+    wet = links[0, 0, 2] > 0
 
     def copy_in(i, carry):
         at = pl.ds(pl.multiple_of(i * tall, tall), tall)
         for f in range(3):
             raw = depth[at] if f == 0 else flow[f - 1, at]
-            out[f, at] = raw
             for p in range(2):
                 tmp[f, p, at] = raw[:, halves[p]] * UNITS[f]
+        return carry
+
+    def copy_dry(i, carry):
+        at = pl.ds(pl.multiple_of(i * tall, tall), tall)
+        for f in range(3):
+            out[f, at] = depth[at] if f == 0 else flow[f - 1, at]
         return carry
 
     def fold(k, carry):
@@ -197,23 +203,26 @@
                 out[f, at, halves[p]] = tmp[f, p, at] * (1.0 / UNITS[f])
         return carry
 
-    lax.fori_loop(0, depth.shape[0] // tall, copy_in, 0)
-
-    @pl.when(link[0, 2] > 0)
+    @pl.when(jnp.logical_not(wet))
     def _():
-        lax.fori_loop(0, rows, fold, 0, unroll=4)
-        values = jnp.sum(ghosts[...], axis=0)
+        lax.fori_loop(0, depth.shape[0] // tall, copy_dry, 0)
+
+    @pl.when(wet)
+    def _():
+        lax.fori_loop(0, depth.shape[0] // tall, copy_in, 0)
+        lax.fori_loop(0, rows, fold, 0, unroll=16)
+        values = ghosts[0]
         level = (ghost_level + values[0:1]) * DEPTH_UNIT
         inflow = values[1:2] * FLOW_UNIT
         spread = [jnp.broadcast_to(v[:, half], (SUB, LANES)) for v in (level, inflow) for half in halves]
         h, mv = split_columns(*spread[:2]), split_columns(*spread[2:])
         ghost = [cell_terms([h[p], jnp.zeros_like(h[p]), mv[p]]) for p in range(2)]
         coast_steps(state, rows, GROUP, CSTEPS, ghost)
-        lax.fori_loop(0, rows, unfold, 0, unroll=4)
+        lax.fori_loop(0, rows, unfold, 0, unroll=16)
         lax.fori_loop(0, depth.shape[0] // tall, copy_out, 0)
 
 
-def coast_run(link, ghosts, depth, flow):
+def coast_run(links, ghosts, depth, flow):
     cells = depth.shape[0]
     vmem = pl.BlockSpec(memory_space=pltpu.VMEM)
     return pl.pallas_call(
@@ -230,11 +239,11 @@
             flops=CSTEPS * 70 * cells * cells, bytes_accessed=24 * cells * cells, transcendentals=0
         ),
         name="coast_steps",
-    )(link, ghosts, depth, flow)
-
-
-def basin_kernel(own, pair, edge, out, eta, hu, hv, dep):
-    rows, width = own.shape[1], own.shape[2]
+    )(links, ghosts, depth, flow)
+
+
+def basin_kernel(state, depth, pair_state, pair_depth, edge, out, eta, hu, hv, dep):
+    rows, width = depth.shape
     total = rows + 2 * HALO
     chunks = width // LANES
     position = lax.axis_index("row")
@@ -244,8 +253,9 @@
     pair_at = pl.multiple_of((1 - odd) * (HALO + rows), HALO)
     edge_at = pl.multiple_of(odd * (HALO + rows), HALO)
     for ref, field, unit in ((eta, 0, 1.0), (hu, 1, 0.5), (hv, 2, 0.5), (dep, 3, 0.25)):
-        ref[HALO : HALO + rows] = own[field] * unit
-        ref[pl.ds(pair_at, HALO)] = pair[field, pl.ds(pair_from, HALO)] * unit
+        own, pair = (depth, pair_depth) if field == 3 else (state.at[field], pair_state.at[field])
+        ref[HALO : HALO + rows] = own[...] * unit
+        ref[pl.ds(pair_at, HALO)] = pair[pl.ds(pair_from, HALO)] * unit
         ref[pl.ds(edge_at, HALO)] = edge[field] * unit
     lane = lax.broadcasted_iota(jnp.int32, (total, LANES), 1)
     first, last = lane == 0, lane == LANES - 1
@@ -281,14 +291,14 @@
     out[2] = hv[own] * 2.0
 
 
-def basin_run(own, pair, edge):
-    rows, width = own.shape[1:]
+def basin_run(state, depth, pair_state, pair_depth, edge):
+    rows, width = depth.shape
     total = rows + 2 * HALO
     vmem = pl.BlockSpec(memory_space=pltpu.VMEM)
     return pl.pallas_call(
         basin_kernel,
         out_shape=jax.ShapeDtypeStruct((3, rows, width), jnp.float32),
-        in_specs=[vmem, vmem, vmem],
+        in_specs=[vmem] * 5,
         out_specs=vmem,
         scratch_shapes=[pltpu.VMEM((total, width), jnp.float32)] * 4,
         compiler_params=pltpu.CompilerParams(vmem_limit_bytes=VMEM_LIMIT),
@@ -296,49 +306,12 @@
             flops=BSTEPS * 16 * total * width, bytes_accessed=4 * 11 * rows * width, transcendentals=0
         ),
         name="basin_steps",
-    )(own, pair, edge)
-
-
-def pack_kernel(link, state, depth, own, edge, sent, sems):
-    rows = depth.shape[0]
-    odd = lax.axis_index("row") % 2
-    edge_rows = pl.ds(pl.multiple_of(odd * (rows - HALO), HALO), HALO)
-    copies = [
-        pltpu.make_async_copy(state, own.at[:3], sems.at[0]),
-        pltpu.make_async_copy(depth, own.at[3], sems.at[1]),
-        pltpu.make_async_copy(state.at[:, edge_rows], edge.at[:3], sems.at[2]),
-        pltpu.make_async_copy(depth.at[edge_rows], edge.at[3], sems.at[3]),
-    ]
-    for copy in copies:
-        copy.start()
-    for b in range(sent.shape[0]):
-        sent[b] = link[...]
-    for copy in copies:
-        copy.wait()
-
-
-def pack(link, state, depth, peers):
-    vmem = pl.BlockSpec(memory_space=pltpu.VMEM)
-    hbm = pl.BlockSpec(memory_space=pltpu.HBM)
-    rows, width = depth.shape
-    return pl.pallas_call(
-        pack_kernel,
-        out_shape=(
-            jax.ShapeDtypeStruct((4, rows, width), jnp.float32),
-            jax.ShapeDtypeStruct((4, HALO, width), jnp.float32),
-            jax.ShapeDtypeStruct((peers,) + link.shape, link.dtype),
-        ),
-        in_specs=[vmem, hbm, hbm],
-        out_specs=(vmem, vmem, vmem),
-        scratch_shapes=[pltpu.SemaphoreType.DMA((4,))],
-        compiler_params=pltpu.CompilerParams(vmem_limit_bytes=VMEM_LIMIT),
-        name="pack",
-    )(link, state, depth)
-
-
-def strips_kernel(links, own, pair, ghosts, strips):
+    )(state, depth, pair_state, pair_depth, edge)
+
+
+def strips_kernel(links, own, pair, near, far, strips):
     rows, width = own.shape[1], own.shape[2]
-    count, cells = ghosts.shape[0], ghosts.shape[2]
+    count, cells = links.shape[0], near.shape[2]
     span = 2 * LANES
     position = lax.axis_index("row")
     tops = (position * rows, (position + 1 - 2 * (position % 2)) * rows)
@@ -367,8 +340,9 @@
     values = jnp.dot(
         strips[...], mix, precision=lax.Precision.HIGHEST, preferred_element_type=jnp.float32
     )
-    for b in range(count):
-        ghosts[b] = values[2 * b : 2 * b + 2]
+    for b in range(count // 2):
+        near[b] = values[2 * b : 2 * b + 2]
+        far[b] = values[count + 2 * b : count + 2 * b + 2]
 
 
 def make_strips(links, own, pair, cells):
@@ -377,32 +351,44 @@
     smem = pl.BlockSpec(memory_space=pltpu.SMEM)
     return pl.pallas_call(
         strips_kernel,
-        out_shape=jax.ShapeDtypeStruct((count, 2, cells), jnp.float32),
+        out_shape=(jax.ShapeDtypeStruct((count // 2, 2, cells), jnp.float32),) * 2,
         in_specs=[smem, vmem, vmem],
-        out_specs=vmem,
+        out_specs=(vmem, vmem),
         scratch_shapes=[pltpu.VMEM((2 * count, LANES), jnp.float32)],
         compiler_params=pltpu.CompilerParams(vmem_limit_bytes=VMEM_LIMIT),
         name="strips",
     )(links, own, pair)
 
 
+def swap(values, bit):
+    count = lax.axis_size("row")
+    return lax.ppermute(values, "row", [(i, i ^ bit) for i in range(count)])
+
+
 def local(basin_state, basin_depth, coast_depth, coast_flow, coast_link):
     devices = lax.axis_size("row")
-    parity = [list(range(p, devices, 2)) for p in range(2)]
-    swap = [(i, i ^ 1) for i in range(devices)]
+    odd = lax.axis_index("row") % 2
+    chips = devices // 2
+    assert chips & (chips - 1) == 0
+    bits = [1 << r for r in range(chips.bit_length() - 1)]
+
+    links = coast_link[None]
+    for bit in bits:
+        links = jnp.concatenate([links, swap(links, 2 * bit)], axis=0)
+
+    pair_state, pair_depth = swap(basin_state, 1), swap(basin_depth, 1)
+    rows = basin_depth.shape[0]
+    whole = jnp.concatenate([basin_state, basin_depth[None]], axis=0)
+    edge = jnp.where(odd == 1, whole[:, rows - HALO :], whole[:, :HALO])
     across = [(i, i + 1) for i in range(1, devices - 1, 2)]
-    across += [(j, i) for i, j in across]
-
-    own, edge, sent = pack(coast_link, basin_state, basin_depth, devices // 2)
-    pair = lax.ppermute(own, "row", swap)
-    edge = lax.ppermute(edge, "row", across)
-    links = lax.all_to_all(sent, "row", 0, 0, axis_index_groups=parity, tiled=True)
-
-    basin_out = basin_run(own, pair, edge)
-    own, basin_out = lax.optimization_barrier((own, basin_out))
-    ghosts = make_strips(links, own, pair, coast_depth.shape[2])
-    ghosts = lax.all_to_all(ghosts, "row", 0, 0, axis_index_groups=parity, tiled=True)
-    coast_out = coast_run(coast_link, ghosts, coast_depth[0], coast_flow[0])
+    edge = lax.ppermute(edge, "row", across + [(j, i) for i, j in across])
+
+    ghosts, far = make_strips(links, basin_state, pair_state, coast_depth.shape[2])
+    for bit in reversed(bits):
+        ghosts = ghosts + swap(far, 2 * bit)
+        ghosts, far = ghosts[: bit // 2], ghosts[bit // 2 :]
+    basin_out = basin_run(basin_state, basin_depth, pair_state, pair_depth, edge)
+    coast_out = coast_run(links, far, coast_depth[0], coast_flow[0])
     return (basin_out, coast_out[None])
 
 

time: 43.6 us -> 44.7 us (1.025)
  the two profiles are of different devices: /device:TPU:1 before, /device:TPU:0 now
where the time goes in v8:
time: 44.7 us; the launch traced here: 44.5 us
  Pallas kernels  17.8 us (40%)
  starting transfers between devices  12.8 us (29%)
  waiting for transfers between devices  11.3 us (25%)
  other arithmetic  1.17 us (3%)
  between operations  0.75 us (2%)
  local copies, waits for them, and re-layouts  0.68 us (2%)
    pallas_call x1, Pallas kernels, coast_run(): pl.pallas_call(coast_kernel, out_shape=jax.ShapeDtypeStruct((3, cells, ce...  13.6 us
    ppermute x8, starting transfers between devices, swap(): return lax.ppermute(values, 'row', [(i, i ^ bit) for i in range(count)])  12.1 us
    ppermute x8, waiting for transfers between devices, swap(): return lax.ppermute(values, 'row', [(i, i ^ bit) for i in range(count)])  11.3 us
    pallas_call x1, Pallas kernels, basin_run(): pl.pallas_call(basin_kernel, out_shape=jax.ShapeDtypeStruct((3, rows, wid...  3.22 us
    select_n x1, other arithmetic, local(): edge = jnp.where(odd == 1, whole[:, rows - HALO:], whole[:, :HALO])  1.14 us
    pallas_call x1, Pallas kernels, make_strips(): pl.pallas_call(strips_kernel, out_shape=(jax.ShapeDtypeStruct((count // 2...  0.98 us
  transfers between devices with their start and end apart: 9, of which 5 were waited for; matrix products, arithmetic and copies ran while one was open for 3% of the time, Pallas kernels for 9%

profile of v8, /device:TPU:0, one launch (start us, length us, event | category | flops | bytes accessed | tf_op | source)
XLA Modules:
  0.0 44.5 jit_solution(17437921905121259481)
XLA Ops:
  0.6 0.0 copy-start.4
  0.6 0.6 %copy-done.4 = s32[1,3]{1,0:T(1,128)S(1)} copy-done((s32[1,3]{1,0:T(1,128)S(1)}, s32[1,3]{1,0:T(1,128)}, u32[]{:S(2)}) %copy-start.4) | copy-done | bytes 36
  1.3 3.0 %collective-permute-start.3 = (s32[1,1,3]{2,1,0:T(1,128)S(1)}, s32[1,1,3]{2,1,0:T(1,128)S(1)}, u32[]{:S(2)}, u32[]{:S(2)}) collective-permute-start(s32[1,1,3]{2,1,0:T(1,128)S(1)} %bitcast.9), channel_id=1, source_target_pairs={{0,2},{1,3},{2,0},{3,1},{4,6},{5,7},{6,4},{7,5},{8,10},{9,11},{10,... | collective-permute-start | bytes 44 | tf_op jit(solution)/shard_map/ppermute | solution.py:365
  4.3 0.0 collective-permute-start
  4.3 0.0 copy-start
  4.3 1.1 %fusion.1 = f32[4,8,2048]{2,1,0:T(8,128)S(1)} fusion(f32[3,16,2048]{2,1,0:T(8,128)} %own.1, f32[1,16,2048]{2,1,0:T(8,128)} %bitcast.6, pred[]{:T(512)S(6)} %eq.5), kind=kLoop, calls=%fused_computation.3 | loop fusion | flops 196608 | bytes 786433 | tf_op jit(solution)/shard_map/jit(_where)/select_n | solution.py:382
  5.4 0.7 %collective-permute-start.2 = (f32[4,8,2048]{2,1,0:T(8,128)S(1)}, f32[4,8,2048]{2,1,0:T(8,128)S(1)}, u32[]{:S(2)}, u32[]{:S(2)}) collective-permute-start(f32[4,8,2048]{2,1,0:T(8,128)S(1)} %fusion.1), channel_id=1, source_target_pairs={{1,2},{3,4},{5,6},{7,8},{9,10},{11,12},{13,14},{2,1},{4,3},{6,5},{... | collective-permute-start | bytes 786440 | tf_op jit(solution)/shard_map/ppermute | solution.py:384
  6.1 0.0 collective-permute-done.3
  6.1 2.9 %collective-permute-start.4 = (s32[2,1,3]{2,1,0:T(1,128)S(1)}, s32[2,1,3]{2,1,0:T(1,128)S(1)}, u32[]{:S(2)}, u32[]{:S(2)}) collective-permute-start(s32[2,1,3]{2,1,0:T(1,128)S(1)} %pad_add_fusion.2), channel_id=1, source_target_pairs={{0,4},{1,5},{2,6},{3,7},{4,0},{5,1},{6,2},{7,3},{8,12},{9,13},{10,... | collective-permute-start | bytes 80 | tf_op jit(solution)/shard_map/ppermute | solution.py:365
  9.0 4.3 %collective-permute-done.4 = s32[2,1,3]{2,1,0:T(1,128)S(1)} collective-permute-done((s32[2,1,3]{2,1,0:T(1,128)S(1)}, s32[2,1,3]{2,1,0:T(1,128)S(1)}, u32[]{:S(2)}, u32[]{:S(2)}) %collective-permute-start.4) | collective-permute-done | bytes 56 | tf_op jit(solution)/shard_map/ppermute | solution.py:365
  13.3 3.1 %collective-permute-start.5 = (s32[4,1,3]{2,1,0:T(1,128)S(1)}, s32[4,1,3]{2,1,0:T(1,128)S(1)}, u32[]{:S(2)}, u32[]{:S(2)}) collective-permute-start(s32[4,1,3]{2,1,0:T(1,128)S(1)} %pad_add_fusion.1), channel_id=1, source_target_pairs={{0,8},{1,9},{2,10},{3,11},{4,12},{5,13},{6,14},{7,15},{8,0},{9,1},... | collective-permute-start | bytes 152 | tf_op jit(solution)/shard_map/ppermute | solution.py:365
  16.4 1.6 %collective-permute-done.5 = s32[4,1,3]{2,1,0:T(1,128)S(1)} collective-permute-done((s32[4,1,3]{2,1,0:T(1,128)S(1)}, s32[4,1,3]{2,1,0:T(1,128)S(1)}, u32[]{:S(2)}, u32[]{:S(2)}) %collective-permute-start.5) | collective-permute-done | bytes 80 | tf_op jit(solution)/shard_map/ppermute | solution.py:365
  18.0 0.0 copy-start.2
  18.0 0.0 collective-permute-done.pair_state.pair
  18.0 0.0 copy-done
  18.0 1.0 %strips.1 = (f32[4,2,256]{2,1,0:T(2,128)S(1)}, f32[4,2,256]{2,1,0:T(2,128)S(1)}) custom-call(s32[8,1,3]{2,1,0:T(1,128)S(1)} %pad_add_fusion.links, f32[3,16,2048]{2,1,0:T(8,128)S(1)} %copy-done, f32[3,16,2048]{2,1,0:T(8,128)S(1)} %collective-permute-done.pair_state.pair), custom_call_target="tpu_custom_call" | custom-call | tf_op jit(solution)/shard_map/strips/pallas_call | solution.py:352
  19.0 2.9 %collective-permute-start.6 = (f32[4,2,256]{2,1,0:T(2,128)S(1)}, f32[4,2,256]{2,1,0:T(2,128)S(1)}, u32[]{:S(2)}, u32[]{:S(2)}) collective-permute-start(f32[4,2,256]{2,1,0:T(2,128)S(1)} %get-tuple-element.5), channel_id=1, source_target_pairs={{0,8},{1,9},{2,10},{3,11},{4,12},{5,13},{6,14},{7,15},{8,0},{9,1},... | collective-permute-start | bytes 24584 | tf_op jit(solution)/shard_map/ppermute | solution.py:365
  21.9 1.6 %collective-permute-done.6 = f32[4,2,256]{2,1,0:T(2,128)S(1)} collective-permute-done((f32[4,2,256]{2,1,0:T(2,128)S(1)}, f32[4,2,256]{2,1,0:T(2,128)S(1)}, u32[]{:S(2)}, u32[]{:S(2)}) %collective-permute-start.6) | collective-permute-done | bytes 8224 | tf_op jit(solution)/shard_map/ppermute | solution.py:365
  23.5 0.1 collective-permute-start.7
  23.6 0.0 copy-done.2
  23.6 0.1 collective-permute-start.1
  23.7 3.5 %collective-permute-done.7 = f32[2,2,256]{2,1,0:T(2,128)S(1)} collective-permute-done((f32[2,2,256]{2,1,0:T(2,128)S(1)}, f32[2,2,256]{2,1,0:T(2,128)S(1)}, u32[]{:S(2)}, u32[]{:S(2)}) %collective-permute-start.7) | collective-permute-done | bytes 4128 | tf_op jit(solution)/shard_map/ppermute | solution.py:365
  27.2 0.0 copy-start.1
  27.2 0.0 copy-start.3
  27.2 0.1 collective-permute-start.8
  27.3 0.0 collective-permute-done.1.pair_depth
  27.3 0.0 collective-permute-done.2.edge
  27.3 3.2 %basin_steps.1 = f32[3,16,2048]{2,1,0:T(8,128)} custom-call(f32[3,16,2048]{2,1,0:T(8,128)S(1)} %copy-done, f32[16,2048]{1,0:T(8,128)S(1)} %copy-done.2, f32[3,16,2048]{2,1,0:T(8,128)S(1)} %collective-permute-done.pair_state.pair, f32[16,2048]{1,0:T(8,128)S(1)} %collective-permute-done.1.pair_depth, f32[4,8,2048]{2,1,0:T(8,128)S(1)} %collective-permute-done.2.edge), custom_call_target="tpu_custom_call" | custom-call | flops 8388608 | bytes 1441792 | tf_op jit(solution)/shard_map/basin_steps/pallas_call | solution.py:298
  30.6 0.3 collective-permute-done.8
  30.9 0.0 copy-done.1
  30.9 0.0 copy-done.3
  30.9 13.6 %coast_steps.1 = f32[3,256,256]{2,1,0:T(8,128)} custom-call(s32[8,1,3]{2,1,0:T(1,128)S(1)} %pad_add_fusion.links, f32[1,2,256]{2,1,0:T(2,128)S(1)} %slice_add_fusion.1.ghosts, f32[256,256]{1,0:T(8,128)S(1)} %bitcast.7, f32[2,256,256]{2,1,0:T(8,128)S(1)} %bitcast.5), custom_call_target="tpu_custom_call" | custom-call | flops 45875200 | bytes 1572864 | tf_op jit(solution)/shard_map/coast_steps/pallas_call | solution.py:228
  (8 shorter events, 0.0 us)
Async XLA Ops:
  0.6 0.7 %copy-start.4 = (s32[1,3]{1,0:T(1,128)S(1)}, s32[1,3]{1,0:T(1,128)}, u32[]{:S(2)}) copy-start(s32[1,3]{1,0:T(1,128)} %param.9) | copy-start | bytes 40
  1.3 4.8 %collective-permute-start.3 = (s32[1,1,3]{2,1,0:T(1,128)S(1)}, s32[1,1,3]{2,1,0:T(1,128)S(1)}, u32[]{:S(2)}, u32[]{:S(2)}) collective-permute-start(s32[1,1,3]{2,1,0:T(1,128)S(1)} %bitcast.9), channel_id=1, source_target_pairs={{0,2},{1,3},{2,0},{3,1},{4,6},{5,7},{6,4},{7,5},{8,10},{9,11},{10,... | collective-permute-start | bytes 44 | tf_op jit(solution)/shard_map/ppermute | solution.py:365
  4.3 13.7 %collective-permute-start = (f32[3,16,2048]{2,1,0:T(8,128)}, f32[3,16,2048]{2,1,0:T(8,128)S(1)}, u32[]{:S(2)}, u32[]{:S(2)}) collective-permute-start(f32[3,16,2048]{2,1,0:T(8,128)} %own.1), channel_id=1, source_target_pairs={{0,1},{1,0},{2,3},{3,2},{4,5},{5,4},{6,7},{7,6},{8,9},{9,8},{10,11... | collective-permute-start | bytes 1179656 | tf_op jit(solution)/shard_map/ppermute | solution.py:365
  4.3 13.7 %copy-start = (f32[3,16,2048]{2,1,0:T(8,128)S(1)}, f32[3,16,2048]{2,1,0:T(8,128)}, u32[]{:S(2)}) copy-start(f32[3,16,2048]{2,1,0:T(8,128)} %own.1) | copy-start | bytes 1179652
  5.4 21.9 %collective-permute-start.2 = (f32[4,8,2048]{2,1,0:T(8,128)S(1)}, f32[4,8,2048]{2,1,0:T(8,128)S(1)}, u32[]{:S(2)}, u32[]{:S(2)}) collective-permute-start(f32[4,8,2048]{2,1,0:T(8,128)S(1)} %fusion.1), channel_id=1, source_target_pairs={{1,2},{3,4},{5,6},{7,8},{9,10},{11,12},{13,14},{2,1},{4,3},{6,5},{... | collective-permute-start | bytes 786440 | tf_op jit(solution)/shard_map/ppermute | solution.py:384
  6.1 7.2 %collective-permute-start.4 = (s32[2,1,3]{2,1,0:T(1,128)S(1)}, s32[2,1,3]{2,1,0:T(1,128)S(1)}, u32[]{:S(2)}, u32[]{:S(2)}) collective-permute-start(s32[2,1,3]{2,1,0:T(1,128)S(1)} %pad_add_fusion.2), channel_id=1, source_target_pairs={{0,4},{1,5},{2,6},{3,7},{4,0},{5,1},{6,2},{7,3},{8,12},{9,13},{10,... | collective-permute-start | bytes 80 | tf_op jit(solution)/shard_map/ppermute | solution.py:365
  13.3 4.7 %collective-permute-start.5 = (s32[4,1,3]{2,1,0:T(1,128)S(1)}, s32[4,1,3]{2,1,0:T(1,128)S(1)}, u32[]{:S(2)}, u32[]{:S(2)}) collective-permute-start(s32[4,1,3]{2,1,0:T(1,128)S(1)} %pad_add_fusion.1), channel_id=1, source_target_pairs={{0,8},{1,9},{2,10},{3,11},{4,12},{5,13},{6,14},{7,15},{8,0},{9,1},... | collective-permute-start | bytes 152 | tf_op jit(solution)/shard_map/ppermute | solution.py:365
  18.0 5.7 %copy-start.2 = (f32[16,2048]{1,0:T(8,128)S(1)}, f32[16,2048]{1,0:T(8,128)}, u32[]{:S(2)}) copy-start(f32[16,2048]{1,0:T(8,128)} %depth.1) | copy-start | bytes 393220
  19.0 4.6 %collective-permute-start.6 = (f32[4,2,256]{2,1,0:T(2,128)S(1)}, f32[4,2,256]{2,1,0:T(2,128)S(1)}, u32[]{:S(2)}, u32[]{:S(2)}) collective-permute-start(f32[4,2,256]{2,1,0:T(2,128)S(1)} %get-tuple-element.5), channel_id=1, source_target_pairs={{0,8},{1,9},{2,10},{3,11},{4,12},{5,13},{6,14},{7,15},{8,0},{9,1},... | collective-permute-start | bytes 24584 | tf_op jit(solution)/shard_map/ppermute | solution.py:365
  23.5 3.7 %collective-permute-start.7 = (f32[2,2,256]{2,1,0:T(2,128)S(1)}, f32[2,2,256]{2,1,0:T(2,128)S(1)}, u32[]{:S(2)}, u32[]{:S(2)}) collective-permute-start(f32[2,2,256]{2,1,0:T(2,128)S(1)} %slice.27), channel_id=1, source_target_pairs={{0,4},{1,5},{2,6},{3,7},{4,0},{5,1},{6,2},{7,3},{8,12},{9,13},{10,... | collective-permute-start | bytes 12296 | tf_op jit(solution)/shard_map/ppermute | solution.py:365
  23.6 3.7 %collective-permute-start.1 = (f32[16,2048]{1,0:T(8,128)S(1)}, f32[16,2048]{1,0:T(8,128)S(1)}, u32[]{:S(2)}, u32[]{:S(2)}) collective-permute-start(f32[16,2048]{1,0:T(8,128)S(1)} %copy-done.2), channel_id=1, source_target_pairs={{0,1},{1,0},{2,3},{3,2},{4,5},{5,4},{6,7},{7,6},{8,9},{9,8},{10,11... | collective-permute-start | bytes 393224 | tf_op jit(solution)/shard_map/ppermute | solution.py:365
  27.2 3.7 %copy-start.1 = (f32[1,2,256,256]{3,2,1,0:T(8,128)S(1)}, f32[1,2,256,256]{3,2,1,0:T(8,128)}, u32[]{:S(2)}) copy-start(f32[1,2,256,256]{3,2,1,0:T(8,128)} %param.8) | copy-start | bytes 1572868
  27.2 3.7 %copy-start.3 = (f32[1,256,256]{2,1,0:T(8,128)S(1)}, f32[1,256,256]{2,1,0:T(8,128)}, u32[]{:S(2)}) copy-start(f32[1,256,256]{2,1,0:T(8,128)} %param.7) | copy-start | bytes 786436
  27.2 3.7 %collective-permute-start.8 = (f32[1,2,256]{2,1,0:T(2,128)S(1)}, f32[1,2,256]{2,1,0:T(2,128)S(1)}, u32[]{:S(2)}, u32[]{:S(2)}) collective-permute-start(f32[1,2,256]{2,1,0:T(2,128)S(1)} %slice.29), channel_id=1, source_target_pairs={{0,2},{1,3},{2,0},{3,1},{4,6},{5,7},{6,4},{7,5},{8,10},{9,11},{10,... | collective-permute-start | bytes 6152 | tf_op jit(solution)/shard_map/ppermute | solution.py:365
